TPU v7x, 128 devices: a whole 4x4x4 slice. The times are simulated.
128 devices in a mesh: nodes: 32 (over x, z, core), hid: 4 (over y).
Axes of the slice: x: 4, y: 4, z: 4, core: 2. Of those that a mesh axis runs over, the one named last changes fastest.
Arguments:
- features: bfloat16 [8192, 512], P('nodes', 'hid'), may hold values from -6 to 6
- neighbors: int32 [8192, 80], P('nodes'), may hold values from 0 to 767, as said below
- degree: int32 [8192], P('nodes'), may hold values from 1 to 80
- send_rows: int32 [32, 32, 16], P('nodes'), may hold values from 0 to 255, as said below
- node_count: int32 [32], P('nodes'), may hold values from 128 to 256, as said below
- w_first: bfloat16 [2, 512, 2048], P(None, None, 'hid'), may hold values from -0.1875 to 0.1875
- w_second: bfloat16 [2, 2048, 2048], P(None, 'hid'), may hold values from -0.09375 to 0.09375
- cotangent: bfloat16 [8192, 2048], P('nodes', 'hid'), may hold values from -6 to 6
Outputs:
- grad_w_first: float32 [512, 2, 2048], P('nodes', None, 'hid')
- grad_w_second: float32 [2048, 2, 2048], P('nodes', None, 'hid')
- grad_features: float32 [8192, 512], P('nodes', 'hid')
Inputs may be any that keep to these rules, and one draw needn't show every extreme that they name: `neighbors`: for node i of partition q, each used entry is either a row below node_count[q] of q's own block or 256 + p * 16 + s naming slot s of what partition p != q sends to q; unused entries are 0. send_rows[p, q, s] is a row of partition p below node_count[p]. `node_count`: some partition is full in every draw.
All inputs are finite; a program needn't handle non-finite values.
Results may differ from a plain program's by a relative error of at most 0.024.
Values may be sent and summed in bfloat16 or wider, within the bound.
No kernel may reach another device: no remote copies, remote signals or barrier semaphores. Data moves between devices by JAX's collectives and lax.ppermute only.
A program may use at most 128 MiB of HBM per device.

v0:
```python
import jax
import jax.numpy as jnp
from jax import lax
from jax.sharding import PartitionSpec as P


def silu_slope(value):
    sig = jax.nn.sigmoid(value)
    return sig * (1.0 + value * (1.0 - sig))


def contract_last(left_op, right_op):
    return lax.dot_general(
        left_op, right_op, (((1,), (1,)), ((), ())), preferred_element_type=jnp.float32
    )


def contract_first(left_op, right_op):
    return lax.dot_general(
        left_op, right_op, (((0,), (0,)), ((), ())), preferred_element_type=jnp.float32
    )


def build_adjacency(neighbors, slot_used, extent):
    width = 128
    marked = jnp.where(slot_used, neighbors, -1)

    def one_block(block_start):
        columns = block_start + lax.broadcasted_iota(jnp.int32, (1, 1, width), 2)
        hits = (marked[:, :, None] == columns).astype(jnp.float32)
        return jnp.sum(hits, axis=1).astype(jnp.bfloat16)

    starts = jnp.arange(extent // width, dtype=jnp.int32) * width
    blocks = lax.map(one_block, starts)
    return jnp.transpose(blocks, (1, 0, 2)).reshape(neighbors.shape[0], extent)


def on_device(features, neighbors, degree, send_rows, node_count, w_first, w_second, cotangent):
    row_count = features.shape[0]
    routes = send_rows[0]
    peer_count = routes.shape[0]
    slot_count = routes.shape[1]
    extent = row_count + peer_count * slot_count
    flat_routes = routes.reshape(-1)
    slot_used = lax.broadcasted_iota(jnp.int32, neighbors.shape, 1) < degree[:, None]
    adjacency = build_adjacency(neighbors, slot_used, extent)
    selector_bool = flat_routes[:, None] == lax.broadcasted_iota(jnp.int32, (1, row_count), 1)
    selector = selector_bool.astype(jnp.bfloat16)
    selector_wide = selector_bool.astype(jnp.float32)
    divisor = degree.astype(jnp.float32)[:, None]
    live_rows = lax.broadcasted_iota(jnp.int32, (row_count, 1), 0) < node_count[0]
    grad_scale = float(row_count * lax.axis_size("nodes")) ** (-0.5)

    def gather_rows(values):
        picked = jnp.dot(selector, values, preferred_element_type=jnp.float32).astype(values.dtype)
        return picked.reshape(peer_count, slot_count, values.shape[1])

    def aggregate(own_rows, halo_rows):
        extended = jnp.concatenate([own_rows, halo_rows.reshape(-1, own_rows.shape[1])], axis=0)
        return (jnp.dot(adjacency, extended, preferred_element_type=jnp.float32) / divisor).astype(
            jnp.bfloat16
        )

    def spread(scaled):
        extended_grad = contract_first(adjacency, scaled)
        return (
            extended_grad[:row_count],
            extended_grad[row_count:].reshape(peer_count, slot_count, scaled.shape[1]),
        )

    def settle(own_rows, returned):
        added = lax.dot_general(
            selector_wide,
            returned.reshape(-1, own_rows.shape[1]),
            (((0,), (0,)), ((), ())),
            precision=lax.Precision.HIGHEST,
            preferred_element_type=jnp.float32,
        )
        return own_rows + added

    full_feat = lax.all_gather(features, "hid", axis=1, tiled=True)
    far_feat = lax.all_to_all(
        gather_rows(full_feat), "nodes", split_axis=0, concat_axis=0, tiled=True
    )
    agg_features = aggregate(full_feat, far_feat)
    pre_first = jnp.dot(full_feat, w_first[0], preferred_element_type=jnp.float32) + jnp.dot(
        agg_features, w_first[1], preferred_element_type=jnp.float32
    )
    hidden_one = jax.nn.silu(pre_first).astype(jnp.bfloat16)
    far_hidden = lax.all_to_all(
        gather_rows(hidden_one), "nodes", split_axis=0, concat_axis=0, tiled=True
    )
    agg_hidden = aggregate(hidden_one, far_hidden)
    partial_value = jnp.dot(hidden_one, w_second[0], preferred_element_type=jnp.float32) + jnp.dot(
        agg_hidden, w_second[1], preferred_element_type=jnp.float32
    )
    pre_second = lax.psum(partial_value.astype(jnp.bfloat16), "hid").astype(jnp.float32)
    cot_full = lax.all_gather(cotangent, "hid", axis=1, tiled=True)
    slope_two = cot_full.astype(jnp.float32) * silu_slope(pre_second)
    grad_second = jnp.where(live_rows, slope_two, jnp.zeros_like(slope_two)).astype(jnp.bfloat16)
    stacked_second = jnp.concatenate([hidden_one, agg_hidden], axis=1)
    unit_count = hidden_one.shape[1]
    grad_w_second = lax.psum_scatter(
        (contract_first(grad_second, stacked_second) * grad_scale)
        .reshape(
            grad_second.shape[1] // lax.axis_size("nodes") * lax.axis_size("nodes"), 2, unit_count
        )
        .astype(jnp.bfloat16),
        "nodes",
        scatter_dimension=0,
        tiled=True,
    ).astype(jnp.float32)
    grad_agg_hidden = (contract_last(grad_second, w_second[1]) / divisor).astype(jnp.bfloat16)
    own_back, halo_back = spread(grad_agg_hidden)
    returned_hidden = lax.all_to_all(
        halo_back.astype(jnp.bfloat16), "nodes", split_axis=0, concat_axis=0, tiled=True
    ).astype(halo_back.dtype)
    grad_hidden = settle(contract_last(grad_second, w_second[0]) + own_back, returned_hidden)
    grad_first = (grad_hidden * silu_slope(pre_first)).astype(jnp.bfloat16)
    grad_w_first = lax.psum_scatter(
        (
            jnp.stack(
                [contract_first(full_feat, grad_first), contract_first(agg_features, grad_first)],
                axis=1,
            )
            * grad_scale
        ).astype(jnp.bfloat16),
        "nodes",
        scatter_dimension=0,
        tiled=True,
    ).astype(jnp.float32)
    self_part = contract_last(grad_first, w_first[0])
    mean_part = contract_last(grad_first, w_first[1])
    self_share, mean_share = (
        lax.psum_scatter(
            self_part.astype(jnp.bfloat16), "hid", scatter_dimension=1, tiled=True
        ).astype(jnp.float32),
        lax.psum_scatter(
            mean_part.astype(jnp.bfloat16), "hid", scatter_dimension=1, tiled=True
        ).astype(jnp.float32),
    )
    scaled_input = (mean_share / divisor).astype(jnp.bfloat16)
    own_input, halo_input = spread(scaled_input)
    returned_input = lax.all_to_all(
        halo_input.astype(jnp.bfloat16), "nodes", split_axis=0, concat_axis=0, tiled=True
    ).astype(halo_input.dtype)
    grad_features = settle(self_share + own_input, returned_input)
    return (grad_w_first, grad_w_second, grad_features)


def solution(mesh):
    placed = (
        P("nodes", "hid"),
        P("nodes", None),
        P("nodes"),
        P("nodes", None, None),
        P("nodes"),
        P(None, None, "hid"),
        P(None, "hid", None),
        P("nodes", "hid"),
    )
    return jax.shard_map(
        on_device,
        mesh=mesh,
        in_specs=placed,
        out_specs=(P("nodes", None, "hid"), P("nodes", None, "hid"), P("nodes", "hid")),
        check_vma=False,
    )
```

profile of v0, /device:TPU:1, one launch (start us, length us, event | category | flops | bytes accessed | tf_op | source)
XLA Modules:
  0.0 331.1 jit_solution(6379530511833177197)
XLA Ops:
  7.2 11.8 %all_gather.7 = bf16[256,512]{1,0:T(8,128)(2,1)S(1)} all-gather(bf16[256,128]{1,0:T(8,128)(2,1)} %param.10), channel_id=1, replica_groups=mesh['nodes'=32,'hid'=4] {'hid'}, dimensions={1}, use_global_device_ids=true | all-gather | bytes 327680 | tf_op jit(solution)/shard_map/all_gather | solution.py:81
  19.8 1.2 convolution_convert_fusion.1
  21.0 10.2 %all-to-all-start = ((bf16[32,16,512]{2,1,0:T(8,128)(2,1)}), bf16[32,16,512]{2,1,0:T(8,128)(2,1)S(1)}, u32[]{:S(2)}, u32[]{:S(2)}) async-start(bf16[32,16,512]{2,1,0:T(8,128)(2,1)} %bitcast.6), calls=%async_computation | async-start | bytes 1048576 | tf_op jit(solution)/shard_map/all_to_all | solution.py:82
  32.2 32.4 %while.10 = (s32[]{:T(128)}, bf16[6,256,128]{1,2,0:T(8,128)(2,1)S(1)}, s32[256,80]{1,0:T(8,128)S(1)}, s32[6]{0:T(128)S(1)}, s32[]{:T(128)}) while((s32[]{:T(128)}, bf16[6,256,128]{1,2,0:T(8,128)(2,1)S(1)}, s32[256,80]{1,0:T(8,128)S(1)}, s32[6]{0:T(128)S(1)}, s32[]{:T(128)}) %tuple.25), condition=%wide.region_2.3_spmd, body=%wide.region_0.2_spmd.sunk | while | flops 7831682 | bytes 410705 | solution.py:34
  33.5 4.0 %convert_reduce_fusion.2 = bf16[256,128]{1,0:T(8,128)(2,1)S(1)} fusion(s32[128]{0:T(128)S(1)} %iota_add_fusion.2, s32[256,80]{1,0:T(8,128)S(1)} %get-tuple-element.81), kind=kLoop, calls=%fused_computation.clone.1 | loop fusion | flops 7831552 | bytes 147968 | tf_op jit(solution)/shard_map/while/body/eval_jaxpr/reduce_sum | solution.py:31
  38.9 4.0 %convert_reduce_fusion.2 = bf16[256,128]{1,0:T(8,128)(2,1)S(1)} fusion(s32[128]{0:T(128)S(1)} %iota_add_fusion.2, s32[256,80]{1,0:T(8,128)S(1)} %get-tuple-element.81), kind=kLoop, calls=%fused_computation.clone.1 | loop fusion | flops 7831552 | bytes 147968 | tf_op jit(solution)/shard_map/while/body/eval_jaxpr/reduce_sum | solution.py:31
  44.3 4.0 %convert_reduce_fusion.2 = bf16[256,128]{1,0:T(8,128)(2,1)S(1)} fusion(s32[128]{0:T(128)S(1)} %iota_add_fusion.2, s32[256,80]{1,0:T(8,128)S(1)} %get-tuple-element.81), kind=kLoop, calls=%fused_computation.clone.1 | loop fusion | flops 7831552 | bytes 147968 | tf_op jit(solution)/shard_map/while/body/eval_jaxpr/reduce_sum | solution.py:31
  49.7 4.0 %convert_reduce_fusion.2 = bf16[256,128]{1,0:T(8,128)(2,1)S(1)} fusion(s32[128]{0:T(128)S(1)} %iota_add_fusion.2, s32[256,80]{1,0:T(8,128)S(1)} %get-tuple-element.81), kind=kLoop, calls=%fused_computation.clone.1 | loop fusion | flops 7831552 | bytes 147968 | tf_op jit(solution)/shard_map/while/body/eval_jaxpr/reduce_sum | solution.py:31
  55.1 4.0 %convert_reduce_fusion.2 = bf16[256,128]{1,0:T(8,128)(2,1)S(1)} fusion(s32[128]{0:T(128)S(1)} %iota_add_fusion.2, s32[256,80]{1,0:T(8,128)S(1)} %get-tuple-element.81), kind=kLoop, calls=%fused_computation.clone.1 | loop fusion | flops 7831552 | bytes 147968 | tf_op jit(solution)/shard_map/while/body/eval_jaxpr/reduce_sum | solution.py:31
  60.5 4.0 %convert_reduce_fusion.2 = bf16[256,128]{1,0:T(8,128)(2,1)S(1)} fusion(s32[128]{0:T(128)S(1)} %iota_add_fusion.2, s32[256,80]{1,0:T(8,128)S(1)} %get-tuple-element.81), kind=kLoop, calls=%fused_computation.clone.1 | loop fusion | flops 7831552 | bytes 147968 | tf_op jit(solution)/shard_map/while/body/eval_jaxpr/reduce_sum | solution.py:31
  66.2 1.1 multiply_convert_fusion.1
  67.3 1.1 convolution_convert_fusion
  68.4 7.4 %all-to-all-start.1 = ((bf16[32,16,512]{2,1,0:T(8,128)(2,1)}), bf16[32,16,512]{2,1,0:T(8,128)(2,1)S(1)}, u32[]{:S(2)}, u32[]{:S(2)}) async-start(bf16[32,16,512]{2,1,0:T(8,128)(2,1)} %bitcast.11), calls=%async_computation.1 | async-start | bytes 1048576 | tf_op jit(solution)/shard_map/all_to_all | solution.py:90
  75.9 2.3 fusion.15
  78.2 9.2 %all-to-all-done.1 = bf16[32,16,512]{2,1,0:T(8,128)(2,1)S(1)} async-done(((bf16[32,16,512]{2,1,0:T(8,128)(2,1)}), bf16[32,16,512]{2,1,0:T(8,128)(2,1)S(1)}, u32[]{:S(2)}, u32[]{:S(2)}) %all-to-all-start.1) | async-done | bytes 524320 | tf_op jit(solution)/shard_map/all_to_all | solution.py:90
  87.4 1.4 fusion.31
  89.5 3.4 %fusion = bf16[256,2048]{1,0:T(8,128)(2,1)} fusion(f32[256,2048]{1,0:T(8,128)S(1)} %fusion.15, bf16[256,512]{1,0:T(8,128)(2,1)S(1)} %fusion.31, bf16[2,512,2048]{2,1,0:T(8,128)(2,1)} %param.16), kind=kOutput, calls=%fused_computation.8 | convolution fusion | flops 537919488 | bytes 5505024 | tf_op jit(solution)/shard_map/dot_general | solution.py:94
  93.7 40.7 %all-reduce.6.cloned.1.call-done = bf16[256,2048]{1,0:T(8,128)(2,1)} async-done(((bf16[256,2048]{1,0:T(8,128)(2,1)}), bf16[256,2048]{1,0:T(8,128)(2,1)}) %all-reduce.6.cloned.1.call-update) | async-done | bytes 1048592 | tf_op jit(solution)/shard_map/psum | solution.py:97
  134.3 3.8 %fusion.42 = f32[768,512]{1,0:T(8,128)S(1)} fusion(bf16[256,768]{0,1:T(8,128)(2,1)} %bitcast.100, bf16[2,512,2048]{2,1,0:T(8,128)(2,1)} %param.16, f32[256]{0:T(256)S(1)} %convert_element_type.96, bf16[256,2048]{1,0:T(8,128)(2,1)} %all-reduce.6.cloned.1.call-done, bf16[256,2048]{1,0:T(8,128)(2,1)} %all-gather.2.cloned.1.call-done, ...), kind=kOutput, calls=%fused_computation.47 | convolution fusion | flops 744751104 | bytes 6161664 | tf_op jit(solution)/shard_map/dot_general | solution.py:19
  138.2 20.8 %all_to_all.20 = bf16[32,16,512]{2,1,0:T(8,128)(2,1)S(1)} all-to-all(bf16[32,16,512]{2,1,0:T(8,128)(2,1)S(1)} %bitcast.90), channel_id=1, replica_groups=mesh['nodes'=32,'hid'=4] {'nodes'}, dimensions={0} | all-to-all | bytes 1048576 | tf_op jit(solution)/shard_map/all_to_all | solution.py:115
  159.5 3.0 fusion.32
  165.0 5.3 %multiply_convert_fusion = bf16[2048,1024]{0,1:T(8,128)(2,1)} fusion(bf16[256,512]{1,0:T(8,128)(2,1)S(1)} %copy-done.4, bf16[256,512]{1,0:T(8,128)(2,1)S(1)} %get-tuple-element.42, bf16[256,2048]{1,0:T(8,128)(2,1)} %all-reduce.6.cloned.1.call-done, bf16[256,2048]{1,0:T(8,128)(2,1)} %all-gather.2.cloned.1.call-done, pred[256]{0:T(512)(128)(4,1)S(1)} %iota_compare_fusion.6), kind=kOutput, calls=%fused_computation.4 | convolution fusion | flops 1085276160 | bytes 6816000 | tf_op jit(solution)/shard_map/dot_general | solution.py:19
  170.3 11.2 %copy.32 = bf16[2048,2,512]{2,1,0:T(2,128)(2,1)} copy(bf16[2048,2,512]{0,2,1:T(8,128)(2,1)} %bitcast.88) | data formatting | bytes 8388608 | tf_op jit(solution)/shard_map/convert_element_type | solution.py:108
  182.4 2.1 copy.31
  184.6 1.0 copy.37
  186.6 4.2 %all-to-all-start.3 = ((bf16[32,16,128]{2,1,0:T(8,128)(2,1)}), bf16[32,16,128]{2,1,0:T(8,128)(2,1)S(1)}, u32[]{:S(2)}, u32[]{:S(2)}) async-start(bf16[32,16,128]{2,1,0:T(8,128)(2,1)} %bitcast.20), calls=%async_computation.3 | async-start | bytes 262144 | tf_op jit(solution)/shard_map/all_to_all | solution.py:144
  192.8 9.2 %reduce-scatter.7.cloned.1.call-done = bf16[128,256]{1,0:T(8,128)(2,1)} async-done(((bf16[512,256]{1,0:T(8,128)(2,1)}), bf16[128,256]{1,0:T(8,128)(2,1)}) %reduce-scatter.7.cloned.1.call-update) | async-done | bytes 65552
  202.0 0.9 copy.35
  202.9 1.1 convolution_add_fusion.2
  204.0 117.4 %all-reduce.8.cloned.1.call-done = (bf16[512,2,512]{2,1,0:T(2,128)(2,1)}, bf16[2048,2,512]{2,1,0:T(2,128)(2,1)}) async-done(((bf16[512,2,512]{2,1,0:T(2,128)(2,1)}, bf16[2048,2,512]{2,1,0:T(2,128)(2,1)}), (bf16[512,2,512]{2,1,0:T(2,128)(2,1)}, bf16[2048,2,512]{2,1,0:T(2,128)(2,1)})) %all-reduce.8.cloned.1.call-update) | async-done | bytes 5242896
  321.4 1.7 dynamic-slice_convert_fusion
  323.1 1.4 dynamic-slice_convert_fusion.1
  (88 shorter events, 17.8 us)
Async XLA Ops:
  7.2 24.8 %copy-start.6 = (s32[256,80]{0,1:T(8,128)S(1)}, s32[256,80]{0,1:T(8,128)}, u32[]{:S(2)}) copy-start(s32[256,80]{0,1:T(8,128)} %param.11) | copy-start | bytes 245764
  7.2 24.9 %copy-start.7 = (s32[256]{0:T(256)S(1)}, s32[256]{0:T(256)}, u32[]{:S(2)}) copy-start(s32[256]{0:T(256)} %param.12) | copy-start | bytes 3076
  21.0 43.6 %copy-start = (bf16[2,512,512]{2,1,0:T(8,128)(2,1)S(1)}, bf16[2,512,512]{2,1,0:T(8,128)(2,1)}, u32[]{:S(2)}) copy-start(bf16[2,512,512]{2,1,0:T(8,128)(2,1)} %param.15) | copy-start | bytes 3145732
  21.0 44.0 %all-to-all-start = ((bf16[32,16,512]{2,1,0:T(8,128)(2,1)}), bf16[32,16,512]{2,1,0:T(8,128)(2,1)S(1)}, u32[]{:S(2)}, u32[]{:S(2)}) async-start(bf16[32,16,512]{2,1,0:T(8,128)(2,1)} %bitcast.6), calls=%async_computation | async-start | bytes 1048576 | tf_op jit(solution)/shard_map/all_to_all | solution.py:82
  31.2 62.4 %all-gather.2.cloned.1.call-start = ((), (), s32[]{:S(2)}) async-start(), calls=%async_computation.6 | async-start | bytes 1310720 | tf_op jit(solution)/shard_map/all_gather | solution.py:98
  64.6 0.8 copy-start.10
  65.0 1.2 copy-start.1
  68.4 19.0 %all-to-all-start.1 = ((bf16[32,16,512]{2,1,0:T(8,128)(2,1)}), bf16[32,16,512]{2,1,0:T(8,128)(2,1)S(1)}, u32[]{:S(2)}, u32[]{:S(2)}) async-start(bf16[32,16,512]{2,1,0:T(8,128)(2,1)} %bitcast.11), calls=%async_computation.1 | async-start | bytes 1048576 | tf_op jit(solution)/shard_map/all_to_all | solution.py:90
  75.8 58.5 %all-reduce.6.cloned.1.call-start = ((), (), s32[]{:S(2)}) async-start(), calls=%async_computation.7 | async-start | bytes 2097152 | tf_op jit(solution)/shard_map/psum | solution.py:97
  88.8 0.7 copy-start.3
  92.9 91.7 %reduce-scatter.9.cloned.1.call-start = ((), (), s32[]{:S(2)}) async-start(), calls=%async_computation.9 | async-start | bytes 327680
  138.1 21.3 %copy-start.5 = (f32[768,512]{1,0:T(8,128)}, f32[768,512]{1,0:T(8,128)S(1)}, u32[]{:S(2)}) copy-start(f32[768,512]{1,0:T(8,128)S(1)} %fusion.42) | copy-start | bytes 4718596
  138.1 21.3 %copy-start.8 = (bf16[256,2048]{1,0:T(8,128)(2,1)S(1)}, bf16[256,2048]{1,0:T(8,128)(2,1)}, u32[]{:S(2)}) copy-start(bf16[256,2048]{1,0:T(8,128)(2,1)} %all-gather.2.cloned.1.call-done) | copy-start | bytes 3145732
  138.1 21.3 %copy-start.9 = (bf16[256,2048]{1,0:T(8,128)(2,1)S(1)}, bf16[256,2048]{1,0:T(8,128)(2,1)}, u32[]{:S(2)}) copy-start(bf16[256,2048]{1,0:T(8,128)(2,1)} %all-reduce.6.cloned.1.call-done) | copy-start | bytes 3145732
  138.1 21.3 %copy-start.13 = (f32[256,512]{1,0:T(8,128)S(1)}, f32[256,512]{1,0:T(8,128)}, u32[]{:S(2)}) copy-start(f32[256,512]{1,0:T(8,128)} %get-tuple-element.43) | copy-start | bytes 1572868
  159.5 3.0 copy-start.2
  162.4 2.5 copy-start.4
  163.7 38.3 %reduce-scatter.7.cloned.1.call-start = ((), (), s32[]{:S(2)}) async-start(), calls=%async_computation.8 | async-start | bytes 327680
  164.9 156.5 %all-reduce.8.cloned.1.call-start = ((), (), s32[]{:S(2)}) async-start(), calls=%async_computation.10 | async-start | bytes 10485760
  184.5 1.1 copy-start.11
  184.5 6.3 %copy-start.12 = (u32[128]{0:T(128)S(1)}, u32[128]{0:T(128)}, u32[]{:S(2)}) copy-start(u32[128]{0:T(128)} %constant.31) | copy-start | bytes 1540
  186.6 16.3 %all-to-all-start.3 = ((bf16[32,16,128]{2,1,0:T(8,128)(2,1)}), bf16[32,16,128]{2,1,0:T(8,128)(2,1)S(1)}, u32[]{:S(2)}, u32[]{:S(2)}) async-start(bf16[32,16,128]{2,1,0:T(8,128)(2,1)} %bitcast.20), calls=%async_computation.3 | async-start | bytes 262144 | tf_op jit(solution)/shard_map/all_to_all | solution.py:144
Sparse Core Ops, SparseCore 0:
  33.7 22.9 all-gather.1
  93.0 41.2 all-reduce.5
  163.8 15.1 reduce-scatter.8
  181.2 20.6 reduce-scatter.6
  205.7 115.6 all-reduce.7
where the time goes:
time: 332 us; the launch traced here: 331 us
  waiting for transfers between devices  177 us (53%)
  blocking collectives  32.6 us (10%)
  other arithmetic  31.4 us (9%)
  matrix products  26.4 us (8%)
  local copies, waits for them, and re-layouts  25 us (8%)
  starting transfers between devices  22.1 us (7%)
  between operations  16.1 us (5%)
    unnamed x8, waiting for transfers between devices  127 us
    psum x1, waiting for transfers between devices, on_device(): lax.psum(partial_value.astype(jnp.bfloat16), 'hid').astype(jnp.float32)  40.7 us
    reduce_sum x6, other arithmetic, one_block(): return jnp.sum(hits, axis=1).astype(jnp.bfloat16)  24 us
    all_to_all x1, blocking collectives, on_device(): lax.all_to_all(halo_back.astype(jnp.bfloat16), 'nodes', split_axis=0, con...  20.8 us
    all_gather x1, blocking collectives, on_device(): full_feat = lax.all_gather(features, 'hid', axis=1, tiled=True)  11.8 us
    convert_element_type x1, local copies, waits for them, and re-layouts, on_device(): grad_w_second = lax.psum_scatter((contract_first(grad_second, stacked_sec...  11.2 us
    all_to_all x1, starting transfers between devices, on_device(): lax.all_to_all(gather_rows(full_feat), 'nodes', split_axis=0, concat_axis...  10.2 us
    dot_general x5, matrix products, contract_first(): lax.dot_general(left_op, right_op, (((0,), (0,)), ((), ())), preferred_el...  10.1 us
  transfers between devices with their start and end apart: 8, of which 4 were waited for; matrix products, arithmetic and copies ran while one was open for 20% of the time, Pallas kernels for 0%

commit v1 on v0

v1 whole, which is shorter than its diff:
```python
import jax
import jax.numpy as jnp
from jax import lax
from jax.experimental import pallas as pl
from jax.experimental.pallas import tpu as pltpu
from jax.sharding import PartitionSpec as P

BF16 = jnp.bfloat16
F32 = jnp.float32
ROWS = 256
PEERS = 32
SLOTS = 16
FAR = PEERS * SLOTS
HID = 4
LANES = 128
UNITS = 512
KEPT = 80


def mm(left_op, right_op):
    return jnp.dot(left_op, right_op, preferred_element_type=F32)


def mm_last(left_op, right_op):
    return lax.dot_general(left_op, right_op, (((1,), (1,)), ((), ())), preferred_element_type=F32)


def mm_first(left_op, right_op):
    return lax.dot_general(left_op, right_op, (((0,), (0,)), ((), ())), preferred_element_type=F32)


def wide(column, width):
    return jnp.concatenate([column] * (width // LANES), axis=1)


def pick_kernel(routes_ref, feat_ref, sel_ref, selt_ref, send_ref):
    row = lax.broadcasted_iota(jnp.int32, (ROWS, FAR), 0)
    chosen = jnp.where(row == routes_ref[...], 1.0, 0.0)
    selt_ref[...] = chosen.astype(BF16)
    sel = chosen.T.astype(BF16)
    sel_ref[...] = sel
    picked = mm(sel, feat_ref[...]).astype(BF16).reshape(PEERS, SLOTS, LANES)
    for part in range(HID):
        send_ref[:, part] = picked


def count_kernel(neigh_ref, degree_ref, adj_ref, adjt_ref, inv_ref, deg_ref):
    deg_ref[...] = jnp.broadcast_to(degree_ref[...].astype(F32), (LANES, ROWS)).T
    inv_ref[...] = 1.0 / deg_ref[...]
    group = 32

    def step(index, carry):
        rows = pl.ds(pl.multiple_of(index * group, group), group)
        entry = neigh_ref[rows, :]
        place = lax.broadcasted_iota(jnp.int32, (group, KEPT), 1).astype(F32)
        used = place < deg_ref[rows, :][:, :KEPT]
        block = entry >> 7
        upper = block >= 3
        key = (entry & 127) + jnp.where(upper, LANES, 0)
        weight = jnp.where(used, jnp.left_shift(1, 10 * jnp.where(upper, block - 3, block)), 0)
        lane = lax.broadcasted_iota(jnp.int32, (group, LANES), 1)
        low = jnp.zeros((group, LANES), jnp.int32)
        high = jnp.zeros((group, LANES), jnp.int32)
        for j in range(KEPT):
            key_j = jnp.broadcast_to(key[:, j : j + 1], (group, LANES))
            weight_j = jnp.broadcast_to(weight[:, j : j + 1], (group, LANES))
            low = low + jnp.where(key_j == lane, weight_j, 0)
            high = high + jnp.where(key_j == lane + LANES, weight_j, 0)
        for t in range(3):
            for base, packed in ((0, low), (3, high)):
                count = jnp.right_shift(packed, 10 * t) & 1023
                adj_ref[rows, (base + t) * LANES : (base + t + 1) * LANES] = count.astype(F32).astype(BF16)
        return carry

    lax.fori_loop(0, ROWS // group, step, 0)
    for t in range((ROWS + FAR) // LANES):
        cols = slice(t * LANES, (t + 1) * LANES)
        adjt_ref[cols, :] = adj_ref[:, cols].astype(F32).T.astype(BF16)


def first_kernel(
    place_ref, f0, f1, f2, f3, far_ref, adj_ref, inv_ref, w_ref, sel_ref,
    both_ref, hidden_ref, slope_ref, send_ref, ext_ref,
):
    me = place_ref[0]
    for d, piece in enumerate((f0, f1, f2, f3)):
        origin = lax.rem(me + HID - d, HID)
        cols = pl.ds(pl.multiple_of(origin * LANES, LANES), LANES)
        ext_ref[:ROWS, cols] = piece[...]
    for origin in range(HID):
        ext_ref[ROWS:, origin * LANES : (origin + 1) * LANES] = far_ref[:, origin].reshape(FAR, LANES)
    both_ref[:, :UNITS] = ext_ref[:ROWS, :]
    agg = mm(adj_ref[...], ext_ref[...]) * wide(inv_ref[...], UNITS)
    both_ref[:, UNITS:] = agg.astype(BF16)
    pre = mm(both_ref[...], w_ref[...])
    sig = 1.0 / (1.0 + jnp.exp(-pre))
    hidden = (pre * sig).astype(BF16)
    hidden_ref[...] = hidden
    slope_ref[...] = sig * (1.0 + pre * (1.0 - sig))
    send_ref[...] = mm(sel_ref[...], hidden).astype(BF16).reshape(PEERS, SLOTS, UNITS)


def second_kernel(
    place_ref, hidden_ref, far_ref, adj_ref, inv_ref, w_ref, stacked_ref, own_ref, s1, s2, s3
):
    me = place_ref[0]
    hidden = hidden_ref[...]
    total = mm(adj_ref[:, :ROWS], hidden) + mm(adj_ref[:, ROWS:], far_ref[...].reshape(FAR, UNITS))
    stacked_ref[:, :UNITS] = hidden
    stacked_ref[:, UNITS:] = (total * wide(inv_ref[...], UNITS)).astype(BF16)
    for d, out in ((2, s2), (1, s1), (3, s3), (0, own_ref)):
        target = lax.rem(me + d, HID)
        cols = pl.ds(pl.multiple_of(target * UNITS, UNITS), UNITS)
        out[...] = mm(stacked_ref[...], w_ref[:, cols]).astype(out.dtype)


def slope_kernel(place_ref, own_ref, r1, r2, r3, cot_ref, grad_ref):
    pre = own_ref[...] + r1[...].astype(F32) + r2[...].astype(F32) + r3[...].astype(F32)
    sig = 1.0 / (1.0 + jnp.exp(-pre))
    slope = cot_ref[...].astype(F32) * (sig * (1.0 + pre * (1.0 - sig)))
    live = lax.broadcasted_iota(jnp.int32, (ROWS, UNITS), 0) < place_ref[2]
    grad_ref[...] = jnp.where(live, slope, 0.0).astype(BF16)


def spread_kernel(place_ref, g0, g1, g2, g3, w_ref, inv_ref, adjt_ref, mean_ref, halo_ref):
    me = place_ref[0]
    total = jnp.zeros((ROWS, UNITS), F32)
    for d, grad in enumerate((g0, g1, g2, g3)):
        origin = lax.rem(me + HID - d, HID)
        cols = pl.ds(pl.multiple_of(origin * UNITS, UNITS), UNITS)
        total = total + mm_last(grad[...], w_ref[UNITS:, cols])
    mean = (total * wide(inv_ref[...], UNITS)).astype(BF16)
    mean_ref[...] = mean
    halo_ref[...] = mm(adjt_ref[ROWS:, :], mean).astype(BF16).reshape(PEERS, SLOTS, UNITS)


def own_kernel(place_ref, g0, g1, g2, g3, w_ref, mean_ref, adjt_ref, own_ref):
    me = place_ref[0]
    total = mm(adjt_ref[:ROWS, :], mean_ref[...])
    for d, grad in enumerate((g0, g1, g2, g3)):
        origin = lax.rem(me + HID - d, HID)
        cols = pl.ds(pl.multiple_of(origin * UNITS, UNITS), UNITS)
        total = total + mm_last(grad[...], w_ref[:UNITS, cols])
    own_ref[...] = total


def outer_second_kernel(scale, place_ref, g0, g1, g2, g3, stacked_ref, keep_ref, give_ref):
    me = place_ref[0]
    core = place_ref[1]
    for d, grad in enumerate((g0, g1, g2, g3)):
        origin = lax.rem(me + HID - d, HID)
        blocks = pl.ds(origin * HID, HID)
        product = (mm_first(grad[...], stacked_ref[...]) * scale).astype(BF16)
        product = product.reshape(HID, 2, 64, 2 * UNITS)

        @pl.when(core == 0)
        def _():
            keep_ref[blocks] = product[:, 0]
            give_ref[blocks] = product[:, 1]

        @pl.when(core == 1)
        def _():
            keep_ref[blocks] = product[:, 1]
            give_ref[blocks] = product[:, 0]


def add_kernel(left_ref, right_ref, out_ref):
    out_ref[...] = (left_ref[...].astype(F32) + right_ref[...].astype(F32)).astype(BF16)


def settle_kernel(
    back_ref, own_ref, slope_ref, selt_ref, w_ref, inv_ref, adjt_ref, grad_ref, mean_ref, halo_ref
):
    grad = own_ref[...] + mm(selt_ref[...], back_ref[...].reshape(FAR, UNITS))
    grad = (grad * slope_ref[...]).astype(BF16)
    grad_ref[...] = grad
    mean = (mm_last(grad, w_ref[UNITS:, :]) * wide(inv_ref[...], UNITS)).astype(BF16)
    mean_ref[...] = mean
    halo = mm(adjt_ref[ROWS:, :], mean).astype(BF16)
    for part in range(HID):
        halo_ref[:, part] = halo[:, part * LANES : (part + 1) * LANES].reshape(PEERS, SLOTS, LANES)


def share_kernel(place_ref, grad_ref, mean_ref, w_ref, adjt_ref, own_ref, s1, s2, s3, total_ref):
    me = place_ref[0]
    total_ref[...] = mm_last(grad_ref[...], w_ref[:UNITS, :]) + mm(adjt_ref[:ROWS, :], mean_ref[...])
    for d, out in ((2, s2), (1, s1), (3, s3), (0, own_ref)):
        target = lax.rem(me + d, HID)
        cols = pl.ds(pl.multiple_of(target * LANES, LANES), LANES)
        out[...] = total_ref[:, cols].astype(out.dtype)


def outer_first_kernel(scale, both_ref, grad_ref, out_ref):
    product = (mm_first(both_ref[...], grad_ref[...]) * scale).astype(BF16)
    product = product.reshape(2, PEERS, SLOTS, UNITS)
    out_ref[:, :SLOTS] = product[0]
    out_ref[:, SLOTS:] = product[1]


def final_kernel(own_ref, r1, r2, r3, selt_ref, back_ref, out_ref):
    total = own_ref[...] + r1[...].astype(F32) + r2[...].astype(F32) + r3[...].astype(F32)
    for origin in range(HID):
        total = total + mm(selt_ref[...], back_ref[:, origin].reshape(FAR, LANES))
    out_ref[...] = total


def sum_kernel(parts_ref, out_ref):
    total = parts_ref[0].astype(F32)
    for index in range(1, parts_ref.shape[0]):
        total = total + parts_ref[index].astype(F32)
    out_ref[...] = total


def call(kernel, name, operands, outs, scratch=(), flops=0, scalars=0):
    shapes = [jax.ShapeDtypeStruct(shape, dtype) for shape, dtype in outs]
    in_specs = [
        pl.BlockSpec(memory_space=pltpu.SMEM if index < scalars else pltpu.VMEM)
        for index in range(len(operands))
    ]
    moved = sum(o.size * o.dtype.itemsize for o in list(operands) + shapes)
    results = pl.pallas_call(
        kernel,
        out_shape=shapes,
        in_specs=in_specs,
        out_specs=[pl.BlockSpec(memory_space=pltpu.VMEM) for _ in shapes],
        scratch_shapes=list(scratch),
        compiler_params=pltpu.CompilerParams(vmem_limit_bytes=32 * 1024 * 1024),
        cost_estimate=pl.CostEstimate(flops=flops, bytes_accessed=moved, transcendentals=0),
        name=name,
    )(*operands)
    return results[0] if len(outs) == 1 else results


def around(values):
    return [lax.ppermute(v, "hid", [(i, (i + d) % HID) for i in range(HID)]) for d, v in values]


def on_device(features, neighbors, degree, send_rows, node_count, w_first, w_second, cotangent):
    hid = lax.axis_index("hid").astype(jnp.int32)
    node = lax.axis_index("nodes").astype(jnp.int32)
    place = jnp.stack([hid, node % 2, node_count[0]])
    scale = float(ROWS * PEERS) ** (-0.5)
    routes = send_rows.reshape(1, FAR)
    w1 = w_first.reshape(2 * UNITS, UNITS)
    w2 = w_second.reshape(2 * UNITS, HID * UNITS)
    big = 2 * ROWS * UNITS * UNITS

    sel, selt, send_feat = call(
        pick_kernel, "pick", (routes, features),
        [((FAR, ROWS), BF16), ((ROWS, FAR), BF16), ((PEERS, HID, SLOTS, LANES), BF16)],
        flops=2 * FAR * ROWS * LANES,
    )
    far_feat = lax.all_to_all(
        send_feat.reshape(PEERS * HID, SLOTS, LANES), ("nodes", "hid"), 0, 0, tiled=True
    ).reshape(PEERS, HID, SLOTS, LANES)
    f1, f2, f3 = around([(1, features), (2, features), (3, features)])
    adj, adjt, inv = call(
        count_kernel, "count", (neighbors, degree.reshape(1, ROWS)),
        [((ROWS, ROWS + FAR), BF16), ((ROWS + FAR, ROWS), BF16), ((ROWS, LANES), F32)],
        scratch=[pltpu.VMEM((ROWS, LANES), F32)],
        flops=4 * big,
    )
    both, hidden, slope, send_hidden = call(
        first_kernel, "first",
        (place, features, f1, f2, f3, far_feat, adj, inv, w1, sel),
        [
            ((ROWS, 2 * UNITS), BF16), ((ROWS, UNITS), BF16), ((ROWS, UNITS), F32),
            ((PEERS, SLOTS, UNITS), BF16),
        ],
        scratch=[pltpu.VMEM((ROWS + FAR, UNITS), BF16)],
        flops=8 * big, scalars=1,
    )
    far_hidden = lax.all_to_all(send_hidden, "nodes", 0, 0, tiled=True)
    stacked, own_pre, s1, s2, s3 = call(
        second_kernel, "second",
        (place, hidden, far_hidden, adj, inv, w2),
        [((ROWS, 2 * UNITS), BF16), ((ROWS, UNITS), F32)] + [((ROWS, UNITS), BF16)] * 3,
        flops=10 * big, scalars=1,
    )
    r2, r1, r3 = around([(2, s2), (1, s1), (3, s3)])
    g0 = call(
        slope_kernel, "slope", (place, own_pre, r1, r2, r3, cotangent),
        [((ROWS, UNITS), BF16)], scalars=1,
    )
    g2, g1, g3 = around([(2, g0), (1, g0), (3, g0)])
    mean_hidden, halo_hidden = call(
        spread_kernel, "spread", (place, g0, g1, g2, g3, w2, inv, adjt),
        [((ROWS, UNITS), BF16), ((PEERS, SLOTS, UNITS), BF16)],
        flops=5 * big, scalars=1,
    )
    back_hidden = lax.all_to_all(halo_hidden, "nodes", 0, 0, tiled=True)
    own_hidden = call(
        own_kernel, "own", (place, g0, g1, g2, g3, w2, mean_hidden, adjt),
        [((ROWS, UNITS), F32)], flops=5 * big, scalars=1,
    )
    keep, give = call(
        lambda *refs: outer_second_kernel(scale, *refs), "outer_second",
        (place, g0, g1, g2, g3, stacked),
        [((16, 64, 2 * UNITS), BF16)] * 2,
        flops=8 * big, scalars=1,
    )
    got = lax.ppermute(give, "nodes", [(i, i ^ 1) for i in range(PEERS)])
    pair = call(add_kernel, "pair", (keep, got), [((16, 64, 2 * UNITS), BF16)])
    grad, mean_first, halo_first = call(
        settle_kernel, "settle",
        (back_hidden, own_hidden, slope, selt, w1, inv, adjt),
        [((ROWS, UNITS), BF16), ((ROWS, UNITS), BF16), ((PEERS, HID, SLOTS, LANES), BF16)],
        flops=4 * big,
    )
    back_first = lax.all_to_all(
        halo_first.reshape(PEERS * HID, SLOTS, LANES), ("nodes", "hid"), 0, 0, tiled=True
    ).reshape(PEERS, HID, SLOTS, LANES)
    outer_first = call(
        lambda *refs: outer_first_kernel(scale, *refs), "outer_first", (both, grad),
        [((PEERS, 2 * SLOTS, UNITS), BF16)], flops=2 * big,
    )
    parts_first = lax.all_to_all(outer_first, "nodes", 0, 0, tiled=True)
    own_share, t1, t2, t3 = call(
        share_kernel, "share", (place, grad, mean_first, w1, adjt),
        [((ROWS, LANES), F32)] + [((ROWS, LANES), BF16)] * 3,
        scratch=[pltpu.VMEM((ROWS, UNITS), F32)],
        flops=2 * big, scalars=1,
    )
    u2, u1, u3 = around([(2, t2), (1, t1), (3, t3)])
    same_core = [[2 * chip + core for chip in range(16)] for core in range(2)]
    parts_second = lax.all_to_all(pair, "nodes", 0, 0, tiled=True, axis_index_groups=same_core)
    grad_w_second = call(sum_kernel, "sum_second", (parts_second,), [((64, 2 * UNITS), F32)])
    grad_features = call(
        final_kernel, "final", (own_share, u1, u2, u3, selt, back_first),
        [((ROWS, LANES), F32)], flops=big,
    )
    grad_w_first = call(sum_kernel, "sum_first", (parts_first,), [((2 * SLOTS, UNITS), F32)])
    return (
        jnp.swapaxes(grad_w_first.reshape(2, SLOTS, UNITS), 0, 1),
        grad_w_second.reshape(64, 2, UNITS),
        grad_features,
    )


def solution(mesh):
    placed = (
        P("nodes", "hid"),
        P("nodes", None),
        P("nodes"),
        P("nodes", None, None),
        P("nodes"),
        P(None, None, "hid"),
        P(None, "hid", None),
        P("nodes", "hid"),
    )
    return jax.shard_map(
        on_device,
        mesh=mesh,
        in_specs=placed,
        out_specs=(P("nodes", None, "hid"), P("nodes", None, "hid"), P("nodes", "hid")),
        check_vma=False,
    )
```

time: 332 us -> 193 us (0.58)
  waiting for transfers between devices: 177 us -> 77.2 us
  other arithmetic: 31.4 us -> 0.08 us
  Pallas kernels: 0 us -> 31 us
  matrix products: 26.4 us -> 0 us
  starting transfers between devices: 22.1 us -> 41.4 us
  between operations: 16.1 us -> 1.54 us
  blocking collectives: 32.6 us -> 19.8 us
  local copies, waits for them, and re-layouts: 25 us -> 20.6 us
    unnamed x8 -> x0, waiting for transfers between devices: 127 us -> none
    psum x1 -> x0, waiting for transfers between devices: 40.7 us -> none  [on_device(): lax.psum(partial_value.astype(jnp.bfloat16), 'hid').astype(jnp.float32)]
    all_to_all x3 -> x5, waiting for transfers between devices: 9.23 us -> 47.7 us  [the longest x1 17.9 us: on_device(): lax.all_to_all(pair, 'nodes', 0, 0, tiled=True, axis_index_groups=same_core)]
    pallas_call x0 -> x15, Pallas kernels: none -> 31 us  [call(): pl.pallas_call(kernel, out_shape=shapes, in_specs=in_specs, out_specs=[pl...]
    ppermute x0 -> x13, waiting for transfers between devices: none -> 29.5 us  [the longest x12 29.5 us: around(): lax.ppermute(v, 'hid', [(i, (i + d) % HID) for i in range(HID)])]
    dot_general x18 -> x0, matrix products: 26.4 us -> none  [the longest x5 10.1 us: contract_first(): lax.dot_general(left_op, right_op, (((0,), (0,)), ((), ())), preferred_el...]
    reduce_sum x6 -> x0, other arithmetic: 24 us -> none  [one_block(): return jnp.sum(hits, axis=1).astype(jnp.bfloat16)]
    ppermute x0 -> x13, starting transfers between devices: none -> 14.8 us  [the longest x12 14.3 us: around(): lax.ppermute(v, 'hid', [(i, (i + d) % HID) for i in range(HID)])]
  transfers between devices with their start and end apart: 8 -> 18, of which waited for: 4 -> 13; matrix products, arithmetic and copies ran while one was open for 20% -> 1% of each run, Pallas kernels for 0% -> 10%
where the time goes in v1:
time: 193 us; the launch traced here: 192 us
  waiting for transfers between devices  77.2 us (40%)
  starting transfers between devices  41.4 us (21%)
  Pallas kernels  31 us (16%)
  local copies, waits for them, and re-layouts  20.6 us (11%)
  blocking collectives  19.8 us (10%)
    pallas_call x15, Pallas kernels, call(): pl.pallas_call(kernel, out_shape=shapes, in_specs=in_specs, out_specs=[pl...  31 us
    ppermute x12, waiting for transfers between devices, around(): lax.ppermute(v, 'hid', [(i, (i + d) % HID) for i in range(HID)])  29.5 us
    all_to_all x1, blocking collectives, on_device(): far_hidden = lax.all_to_all(send_hidden, 'nodes', 0, 0, tiled=True)  19.8 us
    unnamed x56, local copies, waits for them, and re-layouts  18.9 us
    all_to_all x1, waiting for transfers between devices, on_device(): lax.all_to_all(pair, 'nodes', 0, 0, tiled=True, axis_index_groups=same_core)  17.9 us
    ppermute x12, starting transfers between devices, around(): lax.ppermute(v, 'hid', [(i, (i + d) % HID) for i in range(HID)])  14.3 us
    all_to_all x1, waiting for transfers between devices, on_device(): parts_first = lax.all_to_all(outer_first, 'nodes', 0, 0, tiled=True)  11.9 us
    all_to_all x1, waiting for transfers between devices, on_device(): lax.all_to_all(halo_first.reshape(PEERS * HID, SLOTS, LANES), ('nodes', '...  11.6 us
  transfers between devices with their start and end apart: 18, of which 13 were waited for; matrix products, arithmetic and copies ran while one was open for 1% of the time, Pallas kernels for 10%

profile of v1, /device:TPU:1, one launch (start us, length us, event | category | flops | bytes accessed | tf_op | source)
XLA Modules:
  0.0 191.6 jit_solution(17008770410182399143)
XLA Ops:
  1.6 1.9 %pick.1 = (bf16[512,256]{1,0:T(8,128)(2,1)S(1)}, bf16[256,512]{1,0:T(8,128)(2,1)S(1)}, bf16[32,4,16,128]{3,2,1,0:T(8,128)(2,1)}) custom-call(s32[1,512]{1,0:T(1,128)S(1)} %reshape.36.routes_ref, bf16[256,128]{1,0:T(8,128)(2,1)} %f0.1), custom_call_target="tpu_custom_call" | custom-call | flops 33554432 | bytes 1116160 | tf_op jit(solution)/shard_map/pick/pallas_call | solution.py:221
  4.2 11.5 %all-to-all-start = ((bf16[128,16,128]{2,1,0:T(8,128)(2,1)}), bf16[128,16,128]{2,1,0:T(8,128)(2,1)S(1)}, u32[]{:S(2)}, u32[]{:S(2)}) async-start(bf16[128,16,128]{2,1,0:T(8,128)(2,1)} %bitcast.2), calls=%async_computation | async-start | bytes 1048576 | tf_op jit(solution)/shard_map/all_to_all | solution.py:253
  15.7 2.7 %collective-permute-start.2 = (bf16[256,128]{1,0:T(8,128)(2,1)}, bf16[256,128]{1,0:T(8,128)(2,1)S(1)}, u32[]{:S(2)}, u32[]{:S(2)}) collective-permute-start(bf16[256,128]{1,0:T(8,128)(2,1)} %f0.1), channel_id=1, source_target_pairs={{0,3},{1,0},{2,1},{3,2},{4,7},{5,4},{6,5},{7,6},{8,11},{9,8},{10,9... | collective-permute-start | bytes 196616 | tf_op jit(solution)/shard_map/ppermute | solution.py:235
  22.0 7.7 %count.1 = (bf16[256,768]{1,0:T(8,128)(2,1)S(1)}, bf16[768,256]{1,0:T(8,128)(2,1)S(1)}, f32[256,128]{1,0:T(8,128)S(1)}) custom-call(s32[256,80]{1,0:T(8,128)S(1)} %copy.15.neigh_ref, s32[1,256]{1,0:T(1,128)S(1)} %bitcast.23), custom_call_target="tpu_custom_call" | custom-call | flops 536870912 | bytes 1000448 | tf_op jit(solution)/shard_map/count/pallas_call | solution.py:221
  29.9 2.1 %first.1 = (bf16[256,1024]{1,0:T(8,128)(2,1)S(1)}, bf16[256,512]{1,0:T(8,128)(2,1)S(1)}, f32[256,512]{1,0:T(8,128)S(1)}, bf16[32,16,512]{2,1,0:T(8,128)(2,1)S(1)}) custom-call(s32[3]{0:T(128)S(1)} %pad_add_fusion.place_ref.refs_0_, bf16[256,128]{1,0:T(8,128)(2,1)} %f0.1, bf16[256,128]{1,0:T(8,128)(2,1)S(1)} %collective-permute-done.f1, ...), custom_call_target="tpu_custom_call" | custom-call | flops 1073741824 | bytes 4456460 | tf_op jit(solution)/shard_map/first/pallas_call | solution.py:221
  32.8 19.8 %all_to_all.30.far_ref = bf16[32,16,512]{2,1,0:T(8,128)(2,1)S(1)} all-to-all(bf16[32,16,512]{2,1,0:T(8,128)(2,1)S(1)} %get-tuple-element.35), channel_id=1, replica_groups=mesh['nodes'=32,'hid'=4] {'nodes'}, dimensions={0} | all-to-all | bytes 1048576 | tf_op jit(solution)/shard_map/all_to_all | solution.py:273
  52.6 2.0 %second.1 = (bf16[256,1024]{1,0:T(8,128)(2,1)S(1)}, f32[256,512]{1,0:T(8,128)S(1)}, bf16[256,512]{1,0:T(8,128)(2,1)S(1)}, bf16[256,512]{1,0:T(8,128)(2,1)S(1)}, bf16[256,512]{1,0:T(8,128)(2,1)S(1)}) custom-call(s32[3]{0:T(128)S(1)} %pad_add_fusion.place_ref.refs_0_, bf16[256,512]{1,0:T(8,128)(2,1)S(1)} %get-tuple-element.34.hidden_ref, ...), custom_call_target="tpu_custom_call" | custom-call | flops 1342177280 | bytes 7340044 | tf_op jit(solution)/shard_map/second/pallas_call | solution.py:221
  54.6 1.6 collective-permute-start.3
  56.3 1.7 collective-permute-start.4
  58.8 5.2 %collective-permute-done.3.r1 = bf16[256,512]{1,0:T(8,128)(2,1)S(1)} collective-permute-done((bf16[256,512]{1,0:T(8,128)(2,1)S(1)}, bf16[256,512]{1,0:T(8,128)(2,1)S(1)}, u32[]{:S(2)}, u32[]{:S(2)}) %collective-permute-start.3) | collective-permute-done | bytes 262176 | tf_op jit(solution)/shard_map/ppermute | solution.py:235
  64.0 6.2 %collective-permute-done.4.r2 = bf16[256,512]{1,0:T(8,128)(2,1)S(1)} collective-permute-done((bf16[256,512]{1,0:T(8,128)(2,1)S(1)}, bf16[256,512]{1,0:T(8,128)(2,1)S(1)}, u32[]{:S(2)}, u32[]{:S(2)}) %collective-permute-start.4) | collective-permute-done | bytes 262176 | tf_op jit(solution)/shard_map/ppermute | solution.py:235
  71.0 2.7 %collective-permute-start.8 = (bf16[256,512]{1,0:T(8,128)(2,1)S(1)}, bf16[256,512]{1,0:T(8,128)(2,1)S(1)}, u32[]{:S(2)}, u32[]{:S(2)}) collective-permute-start(bf16[256,512]{1,0:T(8,128)(2,1)S(1)} %slope.1.g0.refs_1_), channel_id=1, source_target_pairs={{0,3},{1,0},{2,1},{3,2},{4,7},{5,4},{6,5},{7,6},{8,11},{9,8},{10,9... | collective-permute-start | bytes 786440 | tf_op jit(solution)/shard_map/ppermute | solution.py:235
  74.5 5.4 %collective-permute-done.8.g3.refs_4_ = bf16[256,512]{1,0:T(8,128)(2,1)S(1)} collective-permute-done((bf16[256,512]{1,0:T(8,128)(2,1)S(1)}, bf16[256,512]{1,0:T(8,128)(2,1)S(1)}, u32[]{:S(2)}, u32[]{:S(2)}) %collective-permute-start.8) | collective-permute-done | bytes 262176 | tf_op jit(solution)/shard_map/ppermute | solution.py:235
  79.9 2.5 %collective-permute-done.7.g2.refs_3_ = bf16[256,512]{1,0:T(8,128)(2,1)S(1)} collective-permute-done((bf16[256,512]{1,0:T(8,128)(2,1)S(1)}, bf16[256,512]{1,0:T(8,128)(2,1)S(1)}, u32[]{:S(2)}, u32[]{:S(2)}) %collective-permute-start.7) | collective-permute-done | bytes 262176 | tf_op jit(solution)/shard_map/ppermute | solution.py:235
  82.4 6.7 %collective-permute-done.6.g1.refs_2_ = bf16[256,512]{1,0:T(8,128)(2,1)S(1)} collective-permute-done((bf16[256,512]{1,0:T(8,128)(2,1)S(1)}, bf16[256,512]{1,0:T(8,128)(2,1)S(1)}, u32[]{:S(2)}, u32[]{:S(2)}) %collective-permute-start.6) | collective-permute-done | bytes 262176 | tf_op jit(solution)/shard_map/ppermute | solution.py:235
  89.1 4.4 %outer_second.1 = (bf16[16,64,1024]{2,1,0:T(8,128)(2,1)S(1)}, bf16[16,64,1024]{2,1,0:T(8,128)(2,1)}) custom-call(s32[3]{0:T(128)S(1)} %pad_add_fusion.place_ref.refs_0_, bf16[256,512]{1,0:T(8,128)(2,1)S(1)} %slope.1.g0.refs_1_, bf16[256,512]{1,0:T(8,128)(2,1)S(1)} %collective-permute-done.6.g1.refs_2_, ...), custom_call_target="tpu_custom_call" | custom-call | flops 1073741824 | bytes 5767180 | tf_op jit(solution)/shard_map/outer_second/pallas_call | solution.py:221
  94.0 2.4 %spread.1 = (bf16[256,512]{1,0:T(8,128)(2,1)S(1)}, bf16[32,16,512]{2,1,0:T(8,128)(2,1)}) custom-call(s32[3]{0:T(128)S(1)} %pad_add_fusion.place_ref.refs_0_, bf16[256,512]{1,0:T(8,128)(2,1)S(1)} %slope.1.g0.refs_1_, bf16[256,512]{1,0:T(8,128)(2,1)S(1)} %collective-permute-done.6.g1.refs_2_, bf16[256,512]{1,0:T(8,128)(2,1)S(1)} %collective-permute-done.7.g2.refs_3_, ...), custom_call_target="tpu_custom_call" | custom-call | flops 671088640 | bytes 6553612 | tf_op jit(solution)/shard_map/spread/pallas_call | solution.py:221
  97.1 3.9 %all-to-all-start.2 = ((bf16[32,16,512]{2,1,0:T(8,128)(2,1)}), bf16[32,16,512]{2,1,0:T(8,128)(2,1)S(1)}, u32[]{:S(2)}, u32[]{:S(2)}) async-start(bf16[32,16,512]{2,1,0:T(8,128)(2,1)} %get-tuple-element.41), calls=%async_computation.2 | async-start | bytes 1048576 | tf_op jit(solution)/shard_map/all_to_all | solution.py:291
  101.0 2.2 %copy-done.1 = bf16[2,512,2048]{2,1,0:T(8,128)(2,1)S(1)} copy-done((bf16[2,512,2048]{2,1,0:T(8,128)(2,1)S(1)}, bf16[2,512,2048]{2,1,0:T(8,128)(2,1)}, u32[]{:S(2)}) %copy-start.1) | copy-done | bytes 4194328
  105.1 1.4 own.1.own_ref
  106.5 6.2 %all-to-all-done.2.back_ref = bf16[32,16,512]{2,1,0:T(8,128)(2,1)S(1)} async-done(((bf16[32,16,512]{2,1,0:T(8,128)(2,1)}), bf16[32,16,512]{2,1,0:T(8,128)(2,1)S(1)}, u32[]{:S(2)}, u32[]{:S(2)}) %all-to-all-start.2) | async-done | bytes 524320 | tf_op jit(solution)/shard_map/all_to_all | solution.py:291
  117.0 3.5 %all-to-all-start.5 = ((bf16[128,16,128]{2,1,0:T(8,128)(2,1)}), bf16[128,16,128]{2,1,0:T(8,128)(2,1)S(1)}, u32[]{:S(2)}, u32[]{:S(2)}) async-start(bf16[128,16,128]{2,1,0:T(8,128)(2,1)} %bitcast.21), calls=%async_computation.5 | async-start | bytes 1048576 | tf_op jit(solution)/shard_map/all_to_all | solution.py:310
  121.6 1.4 outer_first.1
  123.0 11.6 %all-to-all-done.5 = bf16[128,16,128]{2,1,0:T(8,128)(2,1)S(1)} async-done(((bf16[128,16,128]{2,1,0:T(8,128)(2,1)}), bf16[128,16,128]{2,1,0:T(8,128)(2,1)S(1)}, u32[]{:S(2)}, u32[]{:S(2)}) %all-to-all-start.5) | async-done | bytes 524320 | tf_op jit(solution)/shard_map/all_to_all | solution.py:310
  135.4 4.0 %all-to-all-start.3 = ((bf16[32,32,512]{2,1,0:T(8,128)(2,1)}), bf16[32,32,512]{2,1,0:T(8,128)(2,1)S(1)}, u32[]{:S(2)}, u32[]{:S(2)}) async-start(bf16[32,32,512]{2,1,0:T(8,128)(2,1)} %outer_first.1), calls=%async_computation.3 | async-start | bytes 2097152 | tf_op jit(solution)/shard_map/all_to_all | solution.py:317
  139.5 1.6 copy-done.6
  141.1 3.4 %pair.1 = bf16[16,64,1024]{2,1,0:T(8,128)(2,1)} custom-call(bf16[16,64,1024]{2,1,0:T(8,128)(2,1)S(1)} %copy-done.6, bf16[16,64,1024]{2,1,0:T(8,128)(2,1)} %collective-permute-done.9.right_ref), custom_call_target="tpu_custom_call" | custom-call | bytes 6291456 | tf_op jit(solution)/shard_map/pair/pallas_call | solution.py:221
  144.5 11.9 %all-to-all-done.3.parts_ref = bf16[32,32,512]{2,1,0:T(8,128)(2,1)S(1)} async-done(((bf16[32,32,512]{2,1,0:T(8,128)(2,1)}), bf16[32,32,512]{2,1,0:T(8,128)(2,1)S(1)}, u32[]{:S(2)}, u32[]{:S(2)}) %all-to-all-start.3) | async-done | bytes 1048608 | tf_op jit(solution)/shard_map/all_to_all | solution.py:317
  157.4 3.7 %all-to-all-start.4 = ((bf16[16,64,1024]{2,1,0:T(8,128)(2,1)}), bf16[16,64,1024]{2,1,0:T(8,128)(2,1)S(1)}, u32[]{:S(2)}, u32[]{:S(2)}) async-start(bf16[16,64,1024]{2,1,0:T(8,128)(2,1)} %pair.1), calls=%async_computation.4 | async-start | bytes 4194304 | tf_op jit(solution)/shard_map/all_to_all | solution.py:326
  164.6 2.0 %collective-permute-start.11 = (bf16[256,128]{1,0:T(8,128)(2,1)S(1)}, bf16[256,128]{1,0:T(8,128)(2,1)S(1)}, u32[]{:S(2)}, u32[]{:S(2)}) collective-permute-start(bf16[256,128]{1,0:T(8,128)(2,1)S(1)} %get-tuple-element.52), channel_id=1, source_target_pairs={{0,2},{1,3},{2,0},{3,1},{4,6},{5,7},{6,4},{7,5},{8,10},{9,11},{10,... | collective-permute-start | bytes 196616 | tf_op jit(solution)/shard_map/ppermute | solution.py:235
  167.1 2.0 %collective-permute-done.10.r1 = bf16[256,128]{1,0:T(8,128)(2,1)S(1)} collective-permute-done((bf16[256,128]{1,0:T(8,128)(2,1)S(1)}, bf16[256,128]{1,0:T(8,128)(2,1)S(1)}, u32[]{:S(2)}, u32[]{:S(2)}) %collective-permute-start.10) | collective-permute-done | bytes 65568 | tf_op jit(solution)/shard_map/ppermute | solution.py:235
  172.6 17.9 %all-to-all-done.4.parts_ref = bf16[16,64,1024]{2,1,0:T(8,128)(2,1)S(1)} async-done(((bf16[16,64,1024]{2,1,0:T(8,128)(2,1)}), bf16[16,64,1024]{2,1,0:T(8,128)(2,1)S(1)}, u32[]{:S(2)}, u32[]{:S(2)}) %all-to-all-start.4) | async-done | bytes 2097184 | tf_op jit(solution)/shard_map/all_to_all | solution.py:326
  (80 shorter events, 26.9 us)
Async XLA Ops:
  0.6 29.3 %copy-start.2 = (bf16[2,512,512]{2,1,0:T(8,128)(2,1)S(1)}, bf16[2,512,512]{2,1,0:T(8,128)(2,1)}, u32[]{:S(2)}) copy-start(bf16[2,512,512]{2,1,0:T(8,128)(2,1)} %param.13) | copy-start | bytes 3145732
  4.2 25.6 %all-to-all-start = ((bf16[128,16,128]{2,1,0:T(8,128)(2,1)}), bf16[128,16,128]{2,1,0:T(8,128)(2,1)S(1)}, u32[]{:S(2)}, u32[]{:S(2)}) async-start(bf16[128,16,128]{2,1,0:T(8,128)(2,1)} %bitcast.2), calls=%async_computation | async-start | bytes 1048576 | tf_op jit(solution)/shard_map/all_to_all | solution.py:253
  15.7 13.9 %collective-permute-start.2 = (bf16[256,128]{1,0:T(8,128)(2,1)}, bf16[256,128]{1,0:T(8,128)(2,1)S(1)}, u32[]{:S(2)}, u32[]{:S(2)}) collective-permute-start(bf16[256,128]{1,0:T(8,128)(2,1)} %f0.1), channel_id=1, source_target_pairs={{0,3},{1,0},{2,1},{3,2},{4,7},{5,4},{6,5},{7,6},{8,11},{9,8},{10,9... | collective-permute-start | bytes 196616 | tf_op jit(solution)/shard_map/ppermute | solution.py:235
  18.5 11.2 %collective-permute-start.1 = (bf16[256,128]{1,0:T(8,128)(2,1)}, bf16[256,128]{1,0:T(8,128)(2,1)S(1)}, u32[]{:S(2)}, u32[]{:S(2)}) collective-permute-start(bf16[256,128]{1,0:T(8,128)(2,1)} %f0.1), channel_id=1, source_target_pairs={{0,2},{1,3},{2,0},{3,1},{4,6},{5,7},{6,4},{7,5},{8,10},{9,11},{10,... | collective-permute-start | bytes 196616 | tf_op jit(solution)/shard_map/ppermute | solution.py:235
  19.0 10.7 %collective-permute-start = (bf16[256,128]{1,0:T(8,128)(2,1)}, bf16[256,128]{1,0:T(8,128)(2,1)S(1)}, u32[]{:S(2)}, u32[]{:S(2)}) collective-permute-start(bf16[256,128]{1,0:T(8,128)(2,1)} %f0.1), channel_id=1, source_target_pairs={{0,1},{1,2},{2,3},{3,0},{4,5},{5,6},{6,7},{7,4},{8,9},{9,10},{10,1... | collective-permute-start | bytes 196616 | tf_op jit(solution)/shard_map/ppermute | solution.py:235
  29.9 22.7 %copy-start = (bf16[2,512,2048]{2,1,0:T(8,128)(2,1)S(1)}, bf16[2,512,2048]{2,1,0:T(8,128)(2,1)}, u32[]{:S(2)}) copy-start(bf16[2,512,2048]{2,1,0:T(8,128)(2,1)} %param.14) | copy-start | bytes 12582916
  32.8 21.8 %copy-start.16 = (bf16[256,1024]{1,0:T(8,128)(2,1)}, bf16[256,1024]{1,0:T(8,128)(2,1)S(1)}, u32[]{:S(2)}) copy-start(bf16[256,1024]{1,0:T(8,128)(2,1)S(1)} %get-tuple-element.33.refs_0_) | copy-start | bytes 1572868
  52.6 17.5 %copy-start.25 = (bf16[256,512]{1,0:T(8,128)(2,1)S(1)}, bf16[256,512]{1,0:T(8,128)(2,1)}, u32[]{:S(2)}) copy-start(bf16[256,512]{1,0:T(8,128)(2,1)} %cot_ref.1) | copy-start | bytes 786436
  54.6 9.3 %collective-permute-start.3 = (bf16[256,512]{1,0:T(8,128)(2,1)S(1)}, bf16[256,512]{1,0:T(8,128)(2,1)S(1)}, u32[]{:S(2)}, u32[]{:S(2)}) collective-permute-start(bf16[256,512]{1,0:T(8,128)(2,1)S(1)} %get-tuple-element.37), channel_id=1, source_target_pairs={{0,1},{1,2},{2,3},{3,0},{4,5},{5,6},{6,7},{7,4},{8,9},{9,10},{10,1... | collective-permute-start | bytes 786440 | tf_op jit(solution)/shard_map/ppermute | solution.py:235
  56.3 13.9 %collective-permute-start.4 = (bf16[256,512]{1,0:T(8,128)(2,1)S(1)}, bf16[256,512]{1,0:T(8,128)(2,1)S(1)}, u32[]{:S(2)}, u32[]{:S(2)}) collective-permute-start(bf16[256,512]{1,0:T(8,128)(2,1)S(1)} %get-tuple-element.38), channel_id=1, source_target_pairs={{0,2},{1,3},{2,0},{3,1},{4,6},{5,7},{6,4},{7,5},{8,10},{9,11},{10,... | collective-permute-start | bytes 786440 | tf_op jit(solution)/shard_map/ppermute | solution.py:235
  58.0 12.2 %collective-permute-start.5 = (bf16[256,512]{1,0:T(8,128)(2,1)S(1)}, bf16[256,512]{1,0:T(8,128)(2,1)S(1)}, u32[]{:S(2)}, u32[]{:S(2)}) collective-permute-start(bf16[256,512]{1,0:T(8,128)(2,1)S(1)} %get-tuple-element.39), channel_id=1, source_target_pairs={{0,3},{1,0},{2,1},{3,2},{4,7},{5,4},{6,5},{7,6},{8,11},{9,8},{10,9... | collective-permute-start | bytes 786440 | tf_op jit(solution)/shard_map/ppermute | solution.py:235
  71.0 8.9 %collective-permute-start.8 = (bf16[256,512]{1,0:T(8,128)(2,1)S(1)}, bf16[256,512]{1,0:T(8,128)(2,1)S(1)}, u32[]{:S(2)}, u32[]{:S(2)}) collective-permute-start(bf16[256,512]{1,0:T(8,128)(2,1)S(1)} %slope.1.g0.refs_1_), channel_id=1, source_target_pairs={{0,3},{1,0},{2,1},{3,2},{4,7},{5,4},{6,5},{7,6},{8,11},{9,8},{10,9... | collective-permute-start | bytes 786440 | tf_op jit(solution)/shard_map/ppermute | solution.py:235
  73.8 8.7 %collective-permute-start.7 = (bf16[256,512]{1,0:T(8,128)(2,1)S(1)}, bf16[256,512]{1,0:T(8,128)(2,1)S(1)}, u32[]{:S(2)}, u32[]{:S(2)}) collective-permute-start(bf16[256,512]{1,0:T(8,128)(2,1)S(1)} %slope.1.g0.refs_1_), channel_id=1, source_target_pairs={{0,2},{1,3},{2,0},{3,1},{4,6},{5,7},{6,4},{7,5},{8,10},{9,11},{10,... | collective-permute-start | bytes 786440 | tf_op jit(solution)/shard_map/ppermute | solution.py:235
  74.5 14.6 %collective-permute-start.6 = (bf16[256,512]{1,0:T(8,128)(2,1)S(1)}, bf16[256,512]{1,0:T(8,128)(2,1)S(1)}, u32[]{:S(2)}, u32[]{:S(2)}) collective-permute-start(bf16[256,512]{1,0:T(8,128)(2,1)S(1)} %slope.1.g0.refs_1_), channel_id=1, source_target_pairs={{0,1},{1,2},{2,3},{3,0},{4,5},{5,6},{6,7},{7,4},{8,9},{9,10},{10,1... | collective-permute-start | bytes 786440 | tf_op jit(solution)/shard_map/ppermute | solution.py:235
  89.1 7.3 %copy-start.11 = (bf16[256,512]{1,0:T(8,128)(2,1)}, bf16[256,512]{1,0:T(8,128)(2,1)S(1)}, u32[]{:S(2)}) copy-start(bf16[256,512]{1,0:T(8,128)(2,1)S(1)} %collective-permute-done.6.g1.refs_2_) | copy-start | bytes 786436
  93.5 2.9 %copy-start.5 = (bf16[16,64,1024]{2,1,0:T(8,128)(2,1)}, bf16[16,64,1024]{2,1,0:T(8,128)(2,1)S(1)}, u32[]{:S(2)}) copy-start(bf16[16,64,1024]{2,1,0:T(8,128)(2,1)S(1)} %get-tuple-element.47.left_ref) | copy-start | bytes 6291460
  93.5 46.0 %collective-permute-start.9 = (bf16[16,64,1024]{2,1,0:T(8,128)(2,1)}, bf16[16,64,1024]{2,1,0:T(8,128)(2,1)}, u32[]{:S(2)}, u32[]{:S(2)}) collective-permute-start(bf16[16,64,1024]{2,1,0:T(8,128)(2,1)} %get-tuple-element.48), channel_id=1, source_target_pairs={{0,4},{4,0},{8,12},{12,8},{16,20},{20,16},{24,28},{28,24},{32,36},... | collective-permute-start | bytes 6291464 | tf_op jit(solution)/shard_map/ppermute | solution.py:302
  97.1 15.5 %all-to-all-start.2 = ((bf16[32,16,512]{2,1,0:T(8,128)(2,1)}), bf16[32,16,512]{2,1,0:T(8,128)(2,1)S(1)}, u32[]{:S(2)}, u32[]{:S(2)}) async-start(bf16[32,16,512]{2,1,0:T(8,128)(2,1)} %get-tuple-element.41), calls=%async_computation.2 | async-start | bytes 1048576 | tf_op jit(solution)/shard_map/all_to_all | solution.py:291
  101.0 2.2 %copy-start.1 = (bf16[2,512,2048]{2,1,0:T(8,128)(2,1)S(1)}, bf16[2,512,2048]{2,1,0:T(8,128)(2,1)}, u32[]{:S(2)}) copy-start(bf16[2,512,2048]{2,1,0:T(8,128)(2,1)} %param.14) | copy-start | bytes 12582916
  117.0 18.5 %copy-start.9 = (bf16[256,512]{1,0:T(8,128)(2,1)}, bf16[256,512]{1,0:T(8,128)(2,1)S(1)}, u32[]{:S(2)}) copy-start(bf16[256,512]{1,0:T(8,128)(2,1)S(1)} %get-tuple-element.45.refs_1_.grad_ref) | copy-start | bytes 786436
  117.0 17.6 %all-to-all-start.5 = ((bf16[128,16,128]{2,1,0:T(8,128)(2,1)}), bf16[128,16,128]{2,1,0:T(8,128)(2,1)S(1)}, u32[]{:S(2)}, u32[]{:S(2)}) async-start(bf16[128,16,128]{2,1,0:T(8,128)(2,1)} %bitcast.21), calls=%async_computation.5 | async-start | bytes 1048576 | tf_op jit(solution)/shard_map/all_to_all | solution.py:310
  120.5 1.0 copy-start.17
  135.4 21.0 %all-to-all-start.3 = ((bf16[32,32,512]{2,1,0:T(8,128)(2,1)}), bf16[32,32,512]{2,1,0:T(8,128)(2,1)S(1)}, u32[]{:S(2)}, u32[]{:S(2)}) async-start(bf16[32,32,512]{2,1,0:T(8,128)(2,1)} %outer_first.1), calls=%async_computation.3 | async-start | bytes 2097152 | tf_op jit(solution)/shard_map/all_to_all | solution.py:317
  139.5 1.6 copy-start.6
  157.4 33.0 %all-to-all-start.4 = ((bf16[16,64,1024]{2,1,0:T(8,128)(2,1)}), bf16[16,64,1024]{2,1,0:T(8,128)(2,1)S(1)}, u32[]{:S(2)}, u32[]{:S(2)}) async-start(bf16[16,64,1024]{2,1,0:T(8,128)(2,1)} %pair.1), calls=%async_computation.4 | async-start | bytes 4194304 | tf_op jit(solution)/shard_map/all_to_all | solution.py:326
  161.1 9.5 %copy-start.8 = (bf16[128,16,128]{2,1,0:T(8,128)(2,1)S(1)}, bf16[128,16,128]{2,1,0:T(8,128)(2,1)}, u32[]{:S(2)}) copy-start(bf16[128,16,128]{2,1,0:T(8,128)(2,1)} %copy-done.7) | copy-start | bytes 1572868
  161.2 10.6 %copy-start.4 = (bf16[32,32,512]{2,1,0:T(8,128)(2,1)S(1)}, bf16[32,32,512]{2,1,0:T(8,128)(2,1)}, u32[]{:S(2)}) copy-start(bf16[32,32,512]{2,1,0:T(8,128)(2,1)} %copy-done.3) | copy-start | bytes 3145732
  161.2 1.1 copy-start.10
  163.2 7.5 %copy-start.15 = (bf16[256,512]{1,0:T(8,128)(2,1)S(1)}, bf16[256,512]{1,0:T(8,128)(2,1)}, u32[]{:S(2)}) copy-start(bf16[256,512]{1,0:T(8,128)(2,1)} %copy-done.13) | copy-start | bytes 786436
  164.2 4.9 %collective-permute-start.10 = (bf16[256,128]{1,0:T(8,128)(2,1)S(1)}, bf16[256,128]{1,0:T(8,128)(2,1)S(1)}, u32[]{:S(2)}, u32[]{:S(2)}) collective-permute-start(bf16[256,128]{1,0:T(8,128)(2,1)S(1)} %get-tuple-element.51), channel_id=1, source_target_pairs={{0,1},{1,2},{2,3},{3,0},{4,5},{5,6},{6,7},{7,4},{8,9},{9,10},{10,1... | collective-permute-start | bytes 196616 | tf_op jit(solution)/shard_map/ppermute | solution.py:235
  164.6 5.5 %collective-permute-start.11 = (bf16[256,128]{1,0:T(8,128)(2,1)S(1)}, bf16[256,128]{1,0:T(8,128)(2,1)S(1)}, u32[]{:S(2)}, u32[]{:S(2)}) collective-permute-start(bf16[256,128]{1,0:T(8,128)(2,1)S(1)} %get-tuple-element.52), channel_id=1, source_target_pairs={{0,2},{1,3},{2,0},{3,1},{4,6},{5,7},{6,4},{7,5},{8,10},{9,11},{10,... | collective-permute-start | bytes 196616 | tf_op jit(solution)/shard_map/ppermute | solution.py:235
  166.6 4.1 %collective-permute-start.12 = (bf16[256,128]{1,0:T(8,128)(2,1)S(1)}, bf16[256,128]{1,0:T(8,128)(2,1)S(1)}, u32[]{:S(2)}, u32[]{:S(2)}) collective-permute-start(bf16[256,128]{1,0:T(8,128)(2,1)S(1)} %get-tuple-element.53), channel_id=1, source_target_pairs={{0,3},{1,0},{2,1},{3,2},{4,7},{5,4},{6,5},{7,6},{8,11},{9,8},{10,9... | collective-permute-start | bytes 196616 | tf_op jit(solution)/shard_map/ppermute | solution.py:235
  (13 other events, 11.2 us)

commit v2 on v0

v2 whole, which is shorter than its diff:
```python
import math

import jax
import jax.numpy as jnp
from jax import lax
from jax.experimental import pallas as pl
from jax.experimental.pallas import tpu as pltpu
from jax.sharding import PartitionSpec as P

BF16 = jnp.bfloat16
F32 = jnp.float32
ROWS = 256
PEERS = 32
SLOTS = 16
FAR = PEERS * SLOTS
HID = 4
LANES = 128
UNITS = 512
KEPT = 80
BIG = 2 * ROWS * UNITS * UNITS


def mm(left_op, right_op):
    return jnp.dot(left_op, right_op, preferred_element_type=F32)


def mm_last(left_op, right_op):
    return lax.dot_general(left_op, right_op, (((1,), (1,)), ((), ())), preferred_element_type=F32)


def mm_first(left_op, right_op):
    return lax.dot_general(left_op, right_op, (((0,), (0,)), ((), ())), preferred_element_type=F32)


def wide(column, width):
    return jnp.concatenate([column] * (width // LANES), axis=1)


def route_rows(routes_ref):
    peer = lax.broadcasted_iota(jnp.int32, (PEERS, FAR), 0)
    lane_peer = lax.broadcasted_iota(jnp.int32, (PEERS, FAR), 1) >> 4
    spread_out = jnp.where(peer == lane_peer, 1.0, 0.0).astype(BF16)
    by_slot = mm(routes_ref[...].astype(F32).astype(BF16), spread_out)
    slot = lax.broadcasted_iota(jnp.int32, (SLOTS, FAR), 0)
    lane_slot = lax.broadcasted_iota(jnp.int32, (SLOTS, FAR), 1) & (SLOTS - 1)
    routes = jnp.sum(jnp.where(slot == lane_slot, by_slot, 0.0), axis=0, keepdims=True)
    row = lax.broadcasted_iota(jnp.int32, (ROWS, FAR), 0).astype(F32)
    return jnp.where(row == routes, 1.0, 0.0)


def pick_kernel(place, f0, f1, f2, f3, sel_ref, full_ref, send_ref):
    for d, piece in enumerate((f0, f1, f2, f3)):
        origin = lax.rem(place.hid + HID - d, HID)
        full_ref[:, pl.ds(pl.multiple_of(origin * LANES, LANES), LANES)] = piece[...]
    send_ref[...] = mm(sel_ref[...], full_ref[...]).astype(BF16).reshape(PEERS, SLOTS, UNITS)


def count_kernel(
    neigh_ref, degree_ref, routes_ref, adj_ref, adjt_ref, inv_ref, sel_ref, selt_ref, key_ref, low_ref, high_ref
):
    chosen = route_rows(routes_ref)
    selt_ref[...] = chosen.astype(BF16)
    sel_ref[...] = chosen.T.astype(BF16)
    inv_ref[...] = 1.0 / jnp.broadcast_to(degree_ref[...].astype(F32), (LANES, ROWS)).T
    entry = neigh_ref[...]
    used = lax.broadcasted_iota(jnp.int32, (KEPT, ROWS), 0) < degree_ref[...]
    block = entry >> 7
    upper = block >= 3
    weight = jnp.where(used, jnp.left_shift(1, 10 * jnp.where(upper, block - 3, block)), 0)
    key_ref[...] = entry & (LANES - 1)
    low_ref[...] = jnp.where(upper, 0, weight)
    high_ref[...] = jnp.where(upper, weight, 0)
    tall = 64
    for half in range(LANES // tall):
        value = lax.broadcasted_iota(jnp.int32, (tall, LANES), 0) + half * tall
        for side in range(ROWS // LANES):
            cols = slice(side * LANES, (side + 1) * LANES)

            def step(index, carry):
                low, high = carry
                at = pl.ds(pl.multiple_of(index * 8, 8), 8)
                keys, lows, highs = key_ref[at, cols], low_ref[at, cols], high_ref[at, cols]
                for j in range(8):
                    same = keys[j : j + 1] == value
                    low = low + jnp.where(same, lows[j : j + 1], 0)
                    high = high + jnp.where(same, highs[j : j + 1], 0)
                return low, high

            empty = jnp.zeros((tall, LANES), jnp.int32)
            low, high = lax.fori_loop(0, KEPT // 8, step, (empty, empty))
            for t in range(3):
                for base, packed in ((0, low), (3, high)):
                    count = jnp.right_shift(packed, 10 * t) & 1023
                    start = (base + t) * LANES + half * tall
                    adjt_ref[start : start + tall, cols] = count.astype(F32).astype(BF16)
    for t in range((ROWS + FAR) // LANES):
        rows = slice(t * LANES, (t + 1) * LANES)
        adj_ref[:, rows] = adjt_ref[rows, :].astype(F32).T.astype(BF16)


def first_kernel(full_ref, far_ref, adj_ref, inv_ref, w_ref, sel_ref, both_ref, hidden_ref, send_ref):
    full = full_ref[...]
    agg = mm(adj_ref[:, :ROWS], full) + mm(adj_ref[:, ROWS:], far_ref[...].reshape(FAR, UNITS))
    both_ref[:, :UNITS] = full
    both_ref[:, UNITS:] = (agg * wide(inv_ref[...], UNITS)).astype(BF16)
    pre = mm(both_ref[...], w_ref[...])
    sig = 1.0 / (1.0 + jnp.exp(-pre))
    hidden = (pre * sig).astype(BF16)
    hidden_ref[...] = hidden
    send_ref[...] = mm(sel_ref[...], hidden).astype(BF16).reshape(PEERS, SLOTS, UNITS)


def gate_kernel(both_ref, stacked_ref, w1_ref, slope_ref, saved_ref):
    saved_ref[...] = stacked_ref[...]
    pre = mm(both_ref[...], w1_ref[...])
    sig = 1.0 / (1.0 + jnp.exp(-pre))
    slope_ref[...] = sig * (1.0 + pre * (1.0 - sig))


def second_kernel(
    place, hidden_ref, far_ref, adj_ref, inv_ref, w_ref, stacked_ref, own_ref, s1, s2, s3
):
    hidden = hidden_ref[...]
    total = mm(adj_ref[:, :ROWS], hidden) + mm(adj_ref[:, ROWS:], far_ref[...].reshape(FAR, UNITS))
    stacked_ref[:, :UNITS] = hidden
    stacked_ref[:, UNITS:] = (total * wide(inv_ref[...], UNITS)).astype(BF16)
    for d, out in ((2, s2), (1, s1), (3, s3), (0, own_ref)):
        target = lax.rem(place.hid + d, HID)
        cols = pl.ds(pl.multiple_of(target * UNITS, UNITS), UNITS)
        out[...] = mm(stacked_ref[...], w_ref[:, cols]).astype(out.dtype)


def slope_kernel(count_ref, own_ref, r1, r2, r3, cot_ref, grad_ref):
    pre = own_ref[...] + r1[...].astype(F32) + r2[...].astype(F32) + r3[...].astype(F32)
    sig = 1.0 / (1.0 + jnp.exp(-pre))
    slope = cot_ref[...].astype(F32) * (sig * (1.0 + pre * (1.0 - sig)))
    live = lax.broadcasted_iota(jnp.int32, (ROWS, UNITS), 0) < count_ref[0]
    grad_ref[...] = jnp.where(live, slope, 0.0).astype(BF16)


def spread_kernel(place, g0, g1, g2, g3, w_ref, inv_ref, adjt_ref, halo_ref, own_ref, others_ref):
    order = ((0, g0), (3, g3), (1, g1), (2, g2))
    for index, grad in enumerate((g1, g2, g3)):
        others_ref[index] = grad[...]

    def back(base):
        total = None
        for d, grad in order:
            origin = lax.rem(place.hid + HID - d, HID)
            cols = pl.ds(pl.multiple_of(origin * UNITS, UNITS), UNITS)
            term = mm_last(grad[...], w_ref[base : base + UNITS, cols])
            total = term if total is None else total + term
        return total

    mean = (back(UNITS) * wide(inv_ref[...], UNITS)).astype(BF16)
    halo_ref[...] = mm(adjt_ref[ROWS:, :], mean).astype(BF16).reshape(PEERS, SLOTS, UNITS)
    own_ref[...] = back(0) + mm(adjt_ref[:ROWS, :], mean)


def outer_second_kernel(scale, slots, place, grads_ref, mates_ref, stacked_ref, stacked_mate_ref, *refs):
    a_outs, b_outs, (block_ref, sems) = refs[-10:-6], refs[-6:-2], refs[-2:]
    row = lax.broadcasted_iota(jnp.int32, (UNITS, UNITS // 2), 0)
    col = lax.broadcasted_iota(jnp.int32, (UNITS, UNITS // 2), 1)
    wanted = (col >> 6) * 128 + place.core * 64 + (col & 63)
    keep = jnp.where(row == wanted, 1.0, 0.0).astype(BF16)
    copies = []
    for index, slot in enumerate(slots):
        mine = mm(grads_ref[index], keep).astype(BF16)
        other = mm(mates_ref[index], keep).astype(BF16)
        total = mm_first(mine, stacked_ref[...]) + mm_first(other, stacked_mate_ref[...])
        total = (total * scale).astype(BF16)
        block_ref[index, 0] = total[:, :UNITS].reshape(HID, 64, UNITS)
        block_ref[index, 1] = total[:, UNITS:].reshape(HID, 64, UNITS)
        for d, out in enumerate(a_outs):
            copies.append(pltpu.make_async_copy(
                block_ref.at[index, 0, lax.rem(place.z + d, HID)], out.at[slot], sems.at[index, d]
            ))
            copies[-1].start()
        step = lax.rem(place.hid + 2 * HID - place.x - slot, HID)
        for d, out in enumerate(b_outs):

            @pl.when(step == d)
            def _():
                pltpu.make_async_copy(block_ref.at[index, 1], out, sems.at[index, HID]).start()

    for index, slot in enumerate(slots):
        pltpu.make_async_copy(block_ref.at[index, 1], b_outs[0], sems.at[index, HID]).wait()
    for copy in copies:
        copy.wait()


def middle_kernel(place, a0, a1, a2, a3, b0, b1, b2, b3, c0, c1, c2, c3, d0, d1, d2, d3, total_ref):
    total_ref[0] = a0[...].astype(F32) + a1[...].astype(F32) + a2[...].astype(F32) + a3[...].astype(F32)
    total_ref[1] = b0[...].astype(F32) + b1[...].astype(F32) + b2[...].astype(F32) + b3[...].astype(F32)
    for d, out in enumerate((c0, c1, c2, c3)):
        out[...] = total_ref[0, lax.rem(place.hid + 2 * HID - place.x - d, HID)].astype(out.dtype)
    for d, out in enumerate((d0, d1, d2, d3)):
        out[...] = total_ref[1, lax.rem(place.z + d, HID)].astype(out.dtype)


def last_second_kernel(c0, c1, c2, c3, d0, d1, d2, d3, out_ref):
    for half, parts in enumerate(((c0, c1, c2, c3), (d0, d1, d2, d3))):
        total = parts[0][...]
        for part in parts[1:]:
            total = total + part[...].astype(F32)
        out_ref[:, half, :] = total


def settle_kernel(
    place, back_ref, own_ref, slope_ref, selt_ref, w_ref, grad_ref, mine_ref, s1, s2, s3, full_ref
):
    me = place.hid
    grad = own_ref[...] + mm(selt_ref[...], back_ref[...].reshape(FAR, UNITS))
    grad = (grad * slope_ref[...]).astype(BF16)
    grad_ref[...] = grad
    full_ref[...] = mm_last(grad, w_ref[...])
    for d, out in ((2, s2), (1, s1), (3, s3), (0, mine_ref)):
        target = lax.rem(me + d, HID)
        for half, base in ((1, 0), (0, UNITS)):
            cols = pl.ds(pl.multiple_of(base + target * LANES, LANES), LANES)
            out[:, half * LANES : (half + 1) * LANES] = full_ref[:, cols].astype(out.dtype)


def outer_first_kernel(scale, both_ref, grad_ref, out_ref):
    product = (mm_first(both_ref[...], grad_ref[...]) * scale).astype(BF16)
    product = product.reshape(2, PEERS, SLOTS, UNITS)
    for part in range(HID):
        for kind in range(2):
            start = (part * 2 + kind) * SLOTS
            out_ref[:, start : start + SLOTS] = product[kind, :, :, part * LANES : (part + 1) * LANES]


def return_kernel(mine_ref, r1, r2, r3, inv_ref, adjt_ref, merged_ref, base_ref, out_ref, halo_ref, sem):
    total = mine_ref[...] + r1[...].astype(F32) + r2[...].astype(F32) + r3[...].astype(F32)
    mean = (total[:, :LANES] * inv_ref[...]).astype(BF16)
    halo_ref[...] = mm(adjt_ref[ROWS:, :], mean).astype(BF16).reshape(PEERS, SLOTS, LANES)
    copy = pltpu.make_async_copy(halo_ref, out_ref.at[:, pl.ds(LANES, SLOTS), :], sem)
    copy.start()
    base_ref[...] = total[:, LANES:] + mm(adjt_ref[:ROWS, :], mean)
    copy.wait()


def final_kernel(base_ref, selt_ref, parts_ref, feat_ref, weight_ref):
    back = parts_ref[:, LANES:].reshape(FAR, LANES)
    feat_ref[...] = base_ref[...] + mm(selt_ref[...], back)
    total = parts_ref[0, :LANES].astype(F32)
    for index in range(1, PEERS):
        total = total + parts_ref[index, :LANES].astype(F32)
    for part in range(HID):
        for kind in range(2):
            start = (part * 2 + kind) * SLOTS
            weight_ref[:, kind, part * LANES : (part + 1) * LANES] = total[start : start + SLOTS]


class Place:
    def __init__(self):
        node = lax.axis_index("nodes")
        self.hid = lax.axis_index("hid")
        self.core = node & 1
        self.x = node >> 3
        self.z = (node >> 1) & 3


class Late:
    def __init__(self, source, ref, sem):
        self.ref = ref
        self.source = source
        self.copy = pltpu.make_async_copy(source, ref, sem)
        self.copy.start()
        self.waited = False

    def __getitem__(self, index):
        if not self.waited:
            self.copy.wait()
            self.waited = True
        return self.ref[index]


def in_hbm(value):
    return pltpu.with_memory_space_constraint(value, pltpu.HBM)


def call(
    kernel, name, operands, outs, scratch=(), placed=False, scalars=0, after=(), late=(), held=(), stored=(),
    loose=(), aliases=None, work=1,
):
    shapes = [
        pltpu.HBM(shape, dtype) if index in (*stored, *loose) else jax.ShapeDtypeStruct(shape, dtype)
        for index, (shape, dtype) in enumerate(outs)
    ]
    operands = [in_hbm(o) if index in (*late, *held) else o for index, o in enumerate(operands)]
    count = len(operands)
    in_specs = [
        pl.BlockSpec(memory_space=pltpu.SMEM if index < scalars else pltpu.VMEM) for index in range(count)
    ] + [pl.BlockSpec(memory_space=pl.ANY)] * len(after)
    for index in (*late, *held, *(aliases or {})):
        in_specs[index] = pl.BlockSpec(memory_space=pltpu.HBM)
    out_specs = [
        pl.BlockSpec(memory_space=pltpu.HBM if index in (*stored, *loose) else pltpu.VMEM)
        for index in range(len(shapes))
    ]
    first_out = count + len(after)
    fixed = first_out + len(shapes) + len(scratch)
    buffers = [pltpu.VMEM(operands[index].shape, operands[index].dtype) for index in late]
    buffers += [pltpu.VMEM(*outs[index]) for index in stored]
    sems = [pltpu.SemaphoreType.DMA for _ in buffers]

    def body(*refs):
        inputs = list(refs[:count])
        outputs = list(refs[first_out : first_out + len(shapes)])
        spare, flags = refs[fixed : fixed + len(buffers)], refs[fixed + len(buffers) :]
        for slot, index in enumerate(late):
            inputs[index] = Late(inputs[index], spare[slot], flags[slot])
        copies = []
        for slot, index in enumerate(stored, len(late)):
            copies.append(pltpu.make_async_copy(spare[slot], outputs[index], flags[slot]))
            outputs[index] = spare[slot]
        kernel(*([Place()] if placed else []), *inputs, *outputs, *refs[first_out + len(shapes) : fixed])
        for copy in copies:
            copy.start()
        for copy in copies:
            copy.wait()

    moved = sum(o.size * o.dtype.itemsize for o in operands) + sum(
        math.prod(shape) * jnp.dtype(dtype).itemsize for shape, dtype in outs
    )
    results = pl.pallas_call(
        body,
        out_shape=shapes,
        in_specs=in_specs,
        out_specs=out_specs,
        scratch_shapes=list(scratch) + buffers + sems,
        input_output_aliases=aliases or {},
        compiler_params=pltpu.CompilerParams(vmem_limit_bytes=16 * 1024 * 1024),
        cost_estimate=pl.CostEstimate(flops=work * BIG, bytes_accessed=moved, transcendentals=0),
        name=name,
    )(*operands, *after)
    return results[0] if len(outs) == 1 else results


def around(values):
    return [lax.ppermute(v, "hid", [(i, (i + d) % HID) for i in range(HID)]) for d, v in values]


def node_at(x, z, core):
    return ((x % 4) * 4 + z % 4) * 2 + core


def swap(value):
    return lax.ppermute(value, "nodes", [(i, i ^ 1) for i in range(PEERS)])


def along_z(values):
    return [
        lax.ppermute(v, "nodes", [
            (node_at(x, z, c), node_at(x, z + d, c)) for x in range(4) for z in range(4) for c in range(2)
        ])
        for d, v in values
    ]


def along_x(values):
    return [
        lax.ppermute(v, "nodes", [
            (node_at(x, z, c), node_at(x + d, z, c)) for x in range(4) for z in range(4) for c in range(2)
        ])
        for d, v in values
    ]


def on_device(features, neighbors, degree, send_rows, node_count, w_first, w_second, cotangent):
    scale = float(ROWS * PEERS) ** (-0.5)
    routes = jnp.swapaxes(send_rows, 1, 2).reshape(SLOTS, PEERS)
    w1 = w_first.reshape(2 * UNITS, UNITS)
    w2 = w_second.reshape(2 * UNITS, HID * UNITS)
    chunk = ((ROWS, UNITS), BF16)

    wide_chunk = ((ROWS, UNITS), F32)
    halo = ((PEERS, SLOTS, UNITS), BF16)
    f2, f1, f3 = around([(2, features), (1, features), (3, features)])
    adj, adjt, inv, sel, selt = call(
        count_kernel, "count", (jnp.swapaxes(neighbors, 0, 1), degree.reshape(1, ROWS), routes),
        [
            ((ROWS, ROWS + FAR), BF16), ((ROWS + FAR, ROWS), BF16), ((ROWS, LANES), F32),
            ((FAR, ROWS), BF16), ((ROWS, FAR), BF16),
        ],
        scratch=[pltpu.VMEM((KEPT, ROWS), jnp.int32)] * 3, late=(2, 1, 0), stored=(4,), work=8,
    )
    full, send_feat = call(
        pick_kernel, "pick", (features, f1, f2, f3, sel), [chunk, halo], placed=True,
    )
    far_feat = lax.all_to_all(send_feat, "nodes", 0, 0, tiled=True)
    both, hidden, send_hidden = call(
        first_kernel, "first", (full, far_feat, adj, inv, w1, sel),
        [((ROWS, 2 * UNITS), BF16), chunk, halo], work=6,
    )
    far_hidden = lax.all_to_all(send_hidden, "nodes", 0, 0, tiled=True)
    stacked, own_pre, s1, s2, s3 = call(
        second_kernel, "second", (hidden, far_hidden, adj, inv, w2),
        [((ROWS, 2 * UNITS), BF16), wide_chunk] + [chunk] * 3, placed=True, work=10,
    )
    r2, r1, r3 = around([(2, s2), (1, s1), (3, s3)])
    slope, saved = call(
        gate_kernel, "gate", (both, stacked, w1), [wide_chunk, ((ROWS, 2 * UNITS), BF16)],
        after=(s1,), late=(2,), stored=(0, 1), work=2,
    )
    saved_mate = swap(saved)
    g0 = call(
        slope_kernel, "slope", (node_count, own_pre, r1, r2, r3, cotangent), [chunk], scalars=1,
        after=(in_hbm(slope),),
    )
    g2, g1, g3 = around([(2, g0), (1, g0), (3, g0)])

    def outer(slots, grads, held):
        return tuple(call(
            lambda *refs: outer_second_kernel(scale, slots, *refs), "outer_second",
            (grads, swap(grads), saved, saved_mate, *held),
            [((HID, 64, UNITS), BF16)] * 8,
            scratch=[
                pltpu.VMEM((len(slots), 2, HID, 64, UNITS), BF16),
                pltpu.SemaphoreType.DMA((len(slots), HID + 1)),
            ],
            placed=True, loose=tuple(range(8)), late=(2, 0, 3, 1),
            aliases={4 + index: index for index in range(8)} if held else None, work=3 * len(slots),
        ))

    z = outer((0,), g0.reshape(1, ROWS, UNITS), ())
    halo_hidden, own_hidden, others = call(
        spread_kernel, "spread", (g0, g1, g2, g3, w2, inv, adjt),
        [halo, wide_chunk, ((3, ROWS, UNITS), BF16)], placed=True, after=(in_hbm(z[0]),), work=10, stored=(2,),
    )
    back_hidden = lax.all_to_all(halo_hidden, "nodes", 0, 0, tiled=True)
    z = outer((1, 2, 3), others, z)
    a0, a1, a2, a3, b0, b1, b2, b3 = z
    a2, b2, a1, b1, a3, b3 = (
        along_z([(2, a2)]) + along_x([(2, b2)]) + along_z([(1, a1)]) + along_x([(1, b1)])
        + along_z([(3, a3)]) + along_x([(3, b3)])
    )
    c0, c1, c2, c3, d0, d1, d2, d3 = call(
        middle_kernel, "middle", (a0, a1, a2, a3, b0, b1, b2, b3),
        ([((64, UNITS), F32)] + [((64, UNITS), BF16)] * 3) * 2,
        scratch=[pltpu.VMEM((2, HID, 64, UNITS), F32)], placed=True, late=tuple(range(8)),
    )
    grad, mine, s1, s2, s3 = call(
        settle_kernel, "settle",
        (back_hidden, own_hidden, slope, selt, w1),
        [chunk, ((ROWS, 2 * LANES), F32)] + [((ROWS, 2 * LANES), BF16)] * 3,
        scratch=[pltpu.VMEM((ROWS, 2 * UNITS), F32)], placed=True, late=(3, 2, 4), work=6,
    )
    r2, r1, r3 = around([(2, s2), (1, s1), (3, s3)])
    merged = call(
        lambda *refs: outer_first_kernel(scale, *refs), "outer_first", (both, grad),
        [((PEERS, LANES + SLOTS, LANES), BF16)], after=(s1,), stored=(0,), work=2,
    )
    base, merged = call(
        return_kernel, "return", (mine, r1, r2, r3, inv, adjt, merged),
        [((ROWS, LANES), F32), ((PEERS, LANES + SLOTS, LANES), BF16)],
        scratch=[pltpu.VMEM((PEERS, SLOTS, LANES), BF16), pltpu.SemaphoreType.DMA],
        loose=(1,), aliases={6: 1}, after=(c0,),
    )
    parts = lax.all_to_all(merged, "nodes", 0, 0, tiled=True)
    c2, d2, c1, d1, c3, d3 = (
        along_x([(2, c2)]) + along_z([(2, d2)]) + along_x([(1, c1)]) + along_z([(1, d1)])
        + along_x([(3, c3)]) + along_z([(3, d3)])
    )
    grad_features, grad_w_first = call(
        final_kernel, "final", (base, selt, parts),
        [((ROWS, LANES), F32), ((SLOTS, 2, UNITS), F32)],
    )
    grad_w_second = call(last_second_kernel, "last_second", (c0, c1, c2, c3, d0, d1, d2, d3), [((64, 2, UNITS), F32)])
    return grad_w_first, grad_w_second, grad_features


def solution(mesh):
    placed = (
        P("nodes", "hid"),
        P("nodes", None),
        P("nodes"),
        P("nodes", None, None),
        P("nodes"),
        P(None, None, "hid"),
        P(None, "hid", None),
        P("nodes", "hid"),
    )
    return jax.shard_map(
        on_device,
        mesh=mesh,
        in_specs=placed,
        out_specs=(P("nodes", None, "hid"), P("nodes", None, "hid"), P("nodes", "hid")),
        check_vma=False,
    )
```

time: 332 us -> 153 us (0.46)
  waiting for transfers between devices: 177 us -> 39.2 us
  other arithmetic: 31.4 us -> 0 us
  Pallas kernels: 0 us -> 28.6 us
  matrix products: 26.4 us -> 0 us
  local copies, waits for them, and re-layouts: 25 us -> 3.35 us
  starting transfers between devices: 22.1 us -> 43.2 us
  between operations: 16.1 us -> 1.59 us
  blocking collectives: 32.6 us -> 36.2 us
    unnamed x8 -> x0, waiting for transfers between devices: 127 us -> none
    psum x1 -> x0, waiting for transfers between devices: 40.7 us -> none  [on_device(): lax.psum(partial_value.astype(jnp.bfloat16), 'hid').astype(jnp.float32)]
    ppermute x0 -> x27, waiting for transfers between devices: none -> 39.2 us  [the longest x12 23.5 us: around(): lax.ppermute(v, 'hid', [(i, (i + d) % HID) for i in range(HID)])]
    ppermute x0 -> x27, starting transfers between devices: none -> 34.5 us  [the longest x12 12.2 us: around(): lax.ppermute(v, 'hid', [(i, (i + d) % HID) for i in range(HID)])]
    pallas_call x0 -> x15, Pallas kernels: none -> 28.6 us  [call(): pl.pallas_call(body, out_shape=shapes, in_specs=in_specs, out_specs=out_s...]
    dot_general x18 -> x0, matrix products: 26.4 us -> none  [the longest x5 10.1 us: contract_first(): lax.dot_general(left_op, right_op, (((0,), (0,)), ((), ())), preferred_el...]
    reduce_sum x6 -> x0, other arithmetic: 24 us -> none  [one_block(): return jnp.sum(hits, axis=1).astype(jnp.bfloat16)]
    all_to_all x1 -> x2, blocking collectives: 20.8 us -> 36.2 us  [the longest x1 21.1 us: on_device(): far_feat = lax.all_to_all(send_feat, 'nodes', 0, 0, tiled=True)]
  transfers between devices with their start and end apart: 8 -> 29, of which waited for: 4 -> 13; matrix products, arithmetic and copies ran while one was open for 20% -> 0% of each run, Pallas kernels for 0% -> 14%
where the time goes in v2:
time: 153 us; the launch traced here: 152 us
  starting transfers between devices  43.2 us (28%)
  waiting for transfers between devices  39.2 us (26%)
  blocking collectives  36.2 us (24%)
  Pallas kernels  28.6 us (19%)
  local copies, waits for them, and re-layouts  3.35 us (2%)
  between operations  1.59 us (1%)
    pallas_call x15, Pallas kernels, call(): pl.pallas_call(body, out_shape=shapes, in_specs=in_specs, out_specs=out_s...  28.6 us
    ppermute x12, waiting for transfers between devices, around(): lax.ppermute(v, 'hid', [(i, (i + d) % HID) for i in range(HID)])  23.5 us
    all_to_all x1, blocking collectives, on_device(): far_feat = lax.all_to_all(send_feat, 'nodes', 0, 0, tiled=True)  21.1 us
    all_to_all x1, blocking collectives, on_device(): far_hidden = lax.all_to_all(send_hidden, 'nodes', 0, 0, tiled=True)  15.1 us
    ppermute x12, starting transfers between devices, around(): lax.ppermute(v, 'hid', [(i, (i + d) % HID) for i in range(HID)])  12.2 us
    ppermute x6, starting transfers between devices, along_z(): lax.ppermute(v, 'nodes', [(node_at(x, z, c), node_at(x, z + d, c)) for x...  10.9 us
    ppermute x6, starting transfers between devices, along_x(): lax.ppermute(v, 'nodes', [(node_at(x, z, c), node_at(x + d, z, c)) for x...  9.57 us
    ppermute x6, waiting for transfers between devices, along_x(): lax.ppermute(v, 'nodes', [(node_at(x, z, c), node_at(x + d, z, c)) for x...  8.92 us
  transfers between devices with their start and end apart: 29, of which 13 were waited for; matrix products, arithmetic and copies ran while one was open for 0% of the time, Pallas kernels for 14%

profile of v2, /device:TPU:1, one launch (start us, length us, event | category | flops | bytes accessed | tf_op | source)
XLA Modules:
  0.0 152.2 jit_solution(4162209735890026039)
XLA Ops:
  0.6 3.8 %collective-permute-start.1 = (bf16[256,128]{1,0:T(8,128)(2,1)}, bf16[256,128]{1,0:T(8,128)(2,1)S(1)}, u32[]{:S(2)}, u32[]{:S(2)}) collective-permute-start(bf16[256,128]{1,0:T(8,128)(2,1)} %refs_0_.2), channel_id=1, source_target_pairs={{0,2},{1,3},{2,0},{3,1},{4,6},{5,7},{6,4},{7,5},{8,10},{9,11},{10,... | collective-permute-start | bytes 196616 | tf_op jit(solution)/shard_map/ppermute | solution.py:342
  4.9 2.3 %collective-permute-start.2 = (bf16[256,128]{1,0:T(8,128)(2,1)}, bf16[256,128]{1,0:T(8,128)(2,1)S(1)}, u32[]{:S(2)}, u32[]{:S(2)}) collective-permute-start(bf16[256,128]{1,0:T(8,128)(2,1)} %refs_0_.2), channel_id=1, source_target_pairs={{0,3},{1,0},{2,1},{3,2},{4,7},{5,4},{6,5},{7,6},{8,11},{9,8},{10,9... | collective-permute-start | bytes 196616 | tf_op jit(solution)/shard_map/ppermute | solution.py:342
  7.1 4.0 %count.1 = (bf16[256,768]{1,0:T(8,128)(2,1)S(1)}, bf16[768,256]{1,0:T(8,128)(2,1)S(1)}, f32[256,128]{1,0:T(8,128)S(1)}, bf16[512,256]{1,0:T(8,128)(2,1)S(1)}, bf16[256,512]{1,0:T(8,128)(2,1)}) custom-call(s32[80,256]{1,0:T(8,128)} %bitcast.15, s32[1,256]{1,0:T(1,128)} %bitcast.17, s32[16,32]{1,0:T(8,128)} %bitcast.16), custom_call_target="tpu_custom_call" | custom-call | flops 1073741824 | bytes 1526784 | tf_op jit(solution)/shard_map/count/pallas_call | solution.py:327
  11.5 21.1 %all_to_all.20.refs_1_ = bf16[32,16,512]{2,1,0:T(8,128)(2,1)S(1)} all-to-all(bf16[32,16,512]{2,1,0:T(8,128)(2,1)S(1)} %get-tuple-element.58), channel_id=1, replica_groups=mesh['nodes'=32,'hid'=4] {'nodes'}, dimensions={0} | all-to-all | bytes 1048576 | tf_op jit(solution)/shard_map/all_to_all | solution.py:392
  33.7 15.1 %all_to_all.21.refs_1_ = bf16[32,16,512]{2,1,0:T(8,128)(2,1)S(1)} all-to-all(bf16[32,16,512]{2,1,0:T(8,128)(2,1)S(1)} %get-tuple-element.62), channel_id=1, replica_groups=mesh['nodes'=32,'hid'=4] {'nodes'}, dimensions={0} | all-to-all | bytes 1048576 | tf_op jit(solution)/shard_map/all_to_all | solution.py:397
  48.7 1.5 second.1
  50.3 1.6 %collective-permute-start.5 = (bf16[256,512]{1,0:T(8,128)(2,1)S(1)}, bf16[256,512]{1,0:T(8,128)(2,1)S(1)}, u32[]{:S(2)}, u32[]{:S(2)}) collective-permute-start(bf16[256,512]{1,0:T(8,128)(2,1)S(1)} %get-tuple-element.66), channel_id=1, source_target_pairs={{0,3},{1,0},{2,1},{3,2},{4,7},{5,4},{6,5},{7,6},{8,11},{9,8},{10,9... | collective-permute-start | bytes 786440 | tf_op jit(solution)/shard_map/ppermute | solution.py:342
  52.2 2.6 %gate.1 = (f32[256,512]{1,0:T(8,128)}, bf16[256,1024]{1,0:T(8,128)(2,1)}) custom-call(bf16[256,1024]{1,0:T(8,128)(2,1)S(1)} %get-tuple-element.67.refs_0_, bf16[256,1024]{1,0:T(8,128)(2,1)S(1)} %get-tuple-element.68.refs_1_, bf16[1024,512]{1,0:T(8,128)(2,1)} %bitcast.12, bf16[256,512]{1,0:T(8,128)(2,1)S(1)} %get-tuple-element.64.refs_3_), custom_call_target="tpu_custom_call" | custom-call | flops 268435456 | bytes 3145728 | tf_op jit(solution)/shard_map/gate/pallas_call | solution.py:327
  56.0 3.9 %collective-permute-done.4.refs_3_ = bf16[256,512]{1,0:T(8,128)(2,1)S(1)} collective-permute-done((bf16[256,512]{1,0:T(8,128)(2,1)S(1)}, bf16[256,512]{1,0:T(8,128)(2,1)S(1)}, u32[]{:S(2)}, u32[]{:S(2)}) %collective-permute-start.4) | collective-permute-done | bytes 262176 | tf_op jit(solution)/shard_map/ppermute | solution.py:342
  59.9 4.6 %collective-permute-done.5.refs_4_ = bf16[256,512]{1,0:T(8,128)(2,1)S(1)} collective-permute-done((bf16[256,512]{1,0:T(8,128)(2,1)S(1)}, bf16[256,512]{1,0:T(8,128)(2,1)S(1)}, u32[]{:S(2)}, u32[]{:S(2)}) %collective-permute-start.5) | collective-permute-done | bytes 262176 | tf_op jit(solution)/shard_map/ppermute | solution.py:342
  66.5 1.3 collective-permute-start.8
  69.9 3.1 %outer_second.2 = (bf16[4,64,512]{2,1,0:T(8,128)(2,1)}, bf16[4,64,512]{2,1,0:T(8,128)(2,1)}, bf16[4,64,512]{2,1,0:T(8,128)(2,1)}, bf16[4,64,512]{2,1,0:T(8,128)(...) custom-call(bf16[1,256,512]{2,1,0:T(8,128)(2,1)} %bitcast.11, ...), custom_call_target="tpu_custom_call" | custom-call | flops 402653184 | bytes 3670016 | tf_op jit(solution)/shard_map/outer_second/pallas_call | solution.py:327
  73.0 1.4 collective-permute-done.8.refs_3_
  74.4 2.5 %collective-permute-done.7.refs_2_ = bf16[256,512]{1,0:T(8,128)(2,1)S(1)} collective-permute-done((bf16[256,512]{1,0:T(8,128)(2,1)S(1)}, bf16[256,512]{1,0:T(8,128)(2,1)S(1)}, u32[]{:S(2)}, u32[]{:S(2)}) %collective-permute-start.7) | collective-permute-done | bytes 262176 | tf_op jit(solution)/shard_map/ppermute | solution.py:342
  76.9 5.7 %collective-permute-done.6.refs_1_ = bf16[256,512]{1,0:T(8,128)(2,1)S(1)} collective-permute-done((bf16[256,512]{1,0:T(8,128)(2,1)S(1)}, bf16[256,512]{1,0:T(8,128)(2,1)S(1)}, u32[]{:S(2)}, u32[]{:S(2)}) %collective-permute-start.6) | collective-permute-done | bytes 262176 | tf_op jit(solution)/shard_map/ppermute | solution.py:342
  83.6 3.2 %spread.1 = (bf16[32,16,512]{2,1,0:T(8,128)(2,1)}, f32[256,512]{1,0:T(8,128)S(1)}, bf16[3,256,512]{2,1,0:T(8,128)(2,1)}) custom-call(bf16[256,512]{1,0:T(8,128)(2,1)S(1)} %copy-done.2, bf16[256,512]{1,0:T(8,128)(2,1)S(1)} %collective-permute-done.6.refs_1_, bf16[256,512]{1,0:T(8,128)(2,1)S(1)} %collective-permute-done.7.refs_2_, ...), custom_call_target="tpu_custom_call" | custom-call | flops 1342177280 | bytes 7602176 | tf_op jit(solution)/shard_map/spread/pallas_call | solution.py:327
  87.7 3.9 %all-to-all-start.2 = ((bf16[32,16,512]{2,1,0:T(8,128)(2,1)}), bf16[32,16,512]{2,1,0:T(8,128)(2,1)S(1)}, u32[]{:S(2)}, u32[]{:S(2)}) async-start(bf16[32,16,512]{2,1,0:T(8,128)(2,1)} %get-tuple-element.73), calls=%async_computation.2 | async-start | bytes 1048576 | tf_op jit(solution)/shard_map/all_to_all | solution.py:432
  92.4 4.5 %outer_second.3 = (bf16[4,64,512]{2,1,0:T(8,128)(2,1)}, bf16[4,64,512]{2,1,0:T(8,128)(2,1)}, bf16[4,64,512]{2,1,0:T(8,128)(2,1)}, bf16[4,64,512]{2,1,0:T(8,128)(...) custom-call(bf16[3,256,512]{2,1,0:T(8,128)(2,1)} %get-tuple-element., ...), custom_call_target="tpu_custom_call", output_to_operand_aliasing={{0}: (4, {}), {1}: (5, {}), {2}: (6, {}), {3}: (7, {}), {4}... | custom-call | flops 1207959552 | bytes 6815744 | tf_op jit(solution)/shard_map/outer_second/pallas_call | solution.py:327
  98.1 2.4 %collective-permute-start.16 = (bf16[4,64,512]{2,1,0:T(8,128)(2,1)}, bf16[4,64,512]{2,1,0:T(8,128)(2,1)S(1)}, u32[]{:S(2)}, u32[]{:S(2)}) collective-permute-start(bf16[4,64,512]{2,1,0:T(8,128)(2,1)} %get-tuple-element.91), channel_id=1, source_target_pairs={{0,16},{4,20},{8,24},{12,28},{16,0},{20,4},{24,8},{28,12},{32,48},... | collective-permute-start | bytes 786440 | tf_op jit(solution)/shard_map/ppermute | solution.py:355
  102.9 2.5 %collective-permute-start.19 = (bf16[4,64,512]{2,1,0:T(8,128)(2,1)}, bf16[4,64,512]{2,1,0:T(8,128)(2,1)}, u32[]{:S(2)}, u32[]{:S(2)}) collective-permute-start(bf16[4,64,512]{2,1,0:T(8,128)(2,1)} %get-tuple-element.95), channel_id=1, source_target_pairs={{0,64},{4,68},{8,72},{12,76},{16,80},{20,84},{24,88},{28,92},{32,9... | collective-permute-start | bytes 786440 | tf_op jit(solution)/shard_map/ppermute | solution.py:364
  105.4 2.5 %collective-permute-done.15.refs_1_ = bf16[4,64,512]{2,1,0:T(8,128)(2,1)S(1)} collective-permute-done((bf16[4,64,512]{2,1,0:T(8,128)(2,1)}, bf16[4,64,512]{2,1,0:T(8,128)(2,1)S(1)}, u32[]{:S(2)}, u32[]{:S(2)}) %collective-permute-start.15) | collective-permute-done | bytes 262176 | tf_op jit(solution)/shard_map/ppermute | solution.py:355
  108.7 2.1 %settle.1 = (bf16[256,512]{1,0:T(8,128)(2,1)S(1)}, f32[256,256]{1,0:T(8,128)S(1)}, bf16[256,256]{1,0:T(8,128)(2,1)S(1)}, bf16[256,256]{1,0:T(8,128)(2,1)S(1)}, bf16[256,256]{1,0:T(8,128)(2,1)S(1)}) custom-call(bf16[32,16,512]{2,1,0:T(8,128)(2,1)S(1)} %all-to-all-done.2.refs_0_, f32[256,512]{1,0:T(8,128)S(1)} %get-tuple-element.74.refs_1_, ...), custom_call_target="tpu_custom_call" | custom-call | flops 805306368 | bytes 3801088 | tf_op jit(solution)/shard_map/settle/pallas_call | solution.py:327
  110.8 2.9 %collective-permute-done.16.refs_2_ = bf16[4,64,512]{2,1,0:T(8,128)(2,1)S(1)} collective-permute-done((bf16[4,64,512]{2,1,0:T(8,128)(2,1)}, bf16[4,64,512]{2,1,0:T(8,128)(2,1)S(1)}, u32[]{:S(2)}, u32[]{:S(2)}) %collective-permute-start.16) | collective-permute-done | bytes 262176 | tf_op jit(solution)/shard_map/ppermute | solution.py:355
  115.5 1.6 %outer_first.1.refs_6_ = bf16[32,144,128]{2,1,0:T(8,128)(2,1)} custom-call(bf16[256,1024]{1,0:T(8,128)(2,1)S(1)} %get-tuple-element.67.refs_0_, bf16[256,512]{1,0:T(8,128)(2,1)S(1)} %get-tuple-element.80.refs_1_, bf16[256,256]{1,0:T(8,128)(2,1)S(1)} %get-tuple-element.77.refs_2_), custom_call_target="tpu_custom_call" | custom-call | flops 268435456 | bytes 1966080 | tf_op jit(solution)/shard_map/outer_first/pallas_call | solution.py:327
  117.2 1.7 %middle.1 = (f32[64,512]{1,0:T(8,128)S(1)}, bf16[64,512]{1,0:T(8,128)(2,1)S(1)}, bf16[64,512]{1,0:T(8,128)(2,1)S(1)}, bf16[64,512]{1,0:T(8,128)(2,1)S(1)}, f32[6...) custom-call(bf16[4,64,512]{2,1,0:T(8,128)(2,1)} %get-tuple-element.89, ...), custom_call_target="tpu_custom_call" | custom-call | flops 134217728 | bytes 2752512 | tf_op jit(solution)/shard_map/middle/pallas_call | solution.py:327
  120.7 2.4 %collective-permute-done.11.refs_1_ = bf16[256,256]{1,0:T(8,128)(2,1)S(1)} collective-permute-done((bf16[256,256]{1,0:T(8,128)(2,1)S(1)}, bf16[256,256]{1,0:T(8,128)(2,1)S(1)}, u32[]{:S(2)}, u32[]{:S(2)}) %collective-permute-start.11) | collective-permute-done | bytes 131104 | tf_op jit(solution)/shard_map/ppermute | solution.py:342
  124.1 4.9 %all-to-all-start.3 = ((bf16[32,144,128]{2,1,0:T(8,128)(2,1)}), bf16[32,144,128]{2,1,0:T(8,128)(2,1)S(1)}, u32[]{:S(2)}, u32[]{:S(2)}) async-start(bf16[32,144,128]{2,1,0:T(8,128)(2,1)} %get-tuple-element.99), calls=%async_computation.3 | async-start | bytes 2359296 | tf_op jit(solution)/shard_map/all_to_all | solution.py:461
  129.0 1.5 collective-permute-start.21
  130.4 2.4 %collective-permute-start.22 = (bf16[64,512]{1,0:T(8,128)(2,1)S(1)}, bf16[64,512]{1,0:T(8,128)(2,1)S(1)}, u32[]{:S(2)}, u32[]{:S(2)}) collective-permute-start(bf16[64,512]{1,0:T(8,128)(2,1)S(1)} %get-tuple-element.102), channel_id=1, source_target_pairs={{0,64},{4,68},{8,72},{12,76},{16,80},{20,84},{24,88},{28,92},{32,9... | collective-permute-start | bytes 196616 | tf_op jit(solution)/shard_map/ppermute | solution.py:364
  135.2 2.4 %collective-permute-start.25 = (bf16[64,512]{1,0:T(8,128)(2,1)S(1)}, bf16[64,512]{1,0:T(8,128)(2,1)S(1)}, u32[]{:S(2)}, u32[]{:S(2)}) collective-permute-start(bf16[64,512]{1,0:T(8,128)(2,1)S(1)} %get-tuple-element.106), channel_id=1, source_target_pairs={{0,16},{4,20},{8,24},{12,28},{16,0},{20,4},{24,8},{28,12},{32,48},... | collective-permute-start | bytes 196616 | tf_op jit(solution)/shard_map/ppermute | solution.py:355
  137.6 8.9 %collective-permute-done.21.refs_1_ = bf16[64,512]{1,0:T(8,128)(2,1)S(1)} collective-permute-done((bf16[64,512]{1,0:T(8,128)(2,1)S(1)}, bf16[64,512]{1,0:T(8,128)(2,1)S(1)}, u32[]{:S(2)}, u32[]{:S(2)}) %collective-permute-start.21) | collective-permute-done | bytes 65568 | tf_op jit(solution)/shard_map/ppermute | solution.py:364
  146.5 2.6 %collective-permute-start.26 = (bf16[64,512]{1,0:T(8,128)(2,1)S(1)}, bf16[64,512]{1,0:T(8,128)(2,1)S(1)}, u32[]{:S(2)}, u32[]{:S(2)}) collective-permute-start(bf16[64,512]{1,0:T(8,128)(2,1)S(1)} %get-tuple-element.107), channel_id=1, source_target_pairs={{0,24},{4,28},{8,0},{12,4},{16,8},{20,12},{24,16},{28,20},{32,56},... | collective-permute-start | bytes 196616 | tf_op jit(solution)/shard_map/ppermute | solution.py:355
  (71 shorter events, 23.8 us)
Async XLA Ops:
  0.6 10.5 %collective-permute-start.1 = (bf16[256,128]{1,0:T(8,128)(2,1)}, bf16[256,128]{1,0:T(8,128)(2,1)S(1)}, u32[]{:S(2)}, u32[]{:S(2)}) collective-permute-start(bf16[256,128]{1,0:T(8,128)(2,1)} %refs_0_.2), channel_id=1, source_target_pairs={{0,2},{1,3},{2,0},{3,1},{4,6},{5,7},{6,4},{7,5},{8,10},{9,11},{10,... | collective-permute-start | bytes 196616 | tf_op jit(solution)/shard_map/ppermute | solution.py:342
  4.5 6.7 %collective-permute-start = (bf16[256,128]{1,0:T(8,128)(2,1)}, bf16[256,128]{1,0:T(8,128)(2,1)S(1)}, u32[]{:S(2)}, u32[]{:S(2)}) collective-permute-start(bf16[256,128]{1,0:T(8,128)(2,1)} %refs_0_.2), channel_id=1, source_target_pairs={{0,1},{1,2},{2,3},{3,0},{4,5},{5,6},{6,7},{7,4},{8,9},{9,10},{10,1... | collective-permute-start | bytes 196616 | tf_op jit(solution)/shard_map/ppermute | solution.py:342
  4.9 6.3 %collective-permute-start.2 = (bf16[256,128]{1,0:T(8,128)(2,1)}, bf16[256,128]{1,0:T(8,128)(2,1)S(1)}, u32[]{:S(2)}, u32[]{:S(2)}) collective-permute-start(bf16[256,128]{1,0:T(8,128)(2,1)} %refs_0_.2), channel_id=1, source_target_pairs={{0,3},{1,0},{2,1},{3,2},{4,7},{5,4},{6,5},{7,6},{8,11},{9,8},{10,9... | collective-permute-start | bytes 196616 | tf_op jit(solution)/shard_map/ppermute | solution.py:342
  11.1 21.6 %copy-start.3 = (bf16[2,512,512]{2,1,0:T(8,128)(2,1)S(1)}, bf16[2,512,512]{2,1,0:T(8,128)(2,1)}, u32[]{:S(2)}) copy-start(bf16[2,512,512]{2,1,0:T(8,128)(2,1)} %param.13) | copy-start | bytes 3145732
  11.5 37.2 %copy-start = (bf16[2,512,2048]{2,1,0:T(8,128)(2,1)S(1)}, bf16[2,512,2048]{2,1,0:T(8,128)(2,1)}, u32[]{:S(2)}) copy-start(bf16[2,512,2048]{2,1,0:T(8,128)(2,1)} %param.14) | copy-start | bytes 12582916
  50.2 9.7 %collective-permute-start.4 = (bf16[256,512]{1,0:T(8,128)(2,1)S(1)}, bf16[256,512]{1,0:T(8,128)(2,1)S(1)}, u32[]{:S(2)}, u32[]{:S(2)}) collective-permute-start(bf16[256,512]{1,0:T(8,128)(2,1)S(1)} %get-tuple-element.65), channel_id=1, source_target_pairs={{0,2},{1,3},{2,0},{3,1},{4,6},{5,7},{6,4},{7,5},{8,10},{9,11},{10,... | collective-permute-start | bytes 786440 | tf_op jit(solution)/shard_map/ppermute | solution.py:342
  50.3 14.2 %collective-permute-start.5 = (bf16[256,512]{1,0:T(8,128)(2,1)S(1)}, bf16[256,512]{1,0:T(8,128)(2,1)S(1)}, u32[]{:S(2)}, u32[]{:S(2)}) collective-permute-start(bf16[256,512]{1,0:T(8,128)(2,1)S(1)} %get-tuple-element.66), channel_id=1, source_target_pairs={{0,3},{1,0},{2,1},{3,2},{4,7},{5,4},{6,5},{7,6},{8,11},{9,8},{10,9... | collective-permute-start | bytes 786440 | tf_op jit(solution)/shard_map/ppermute | solution.py:342
  51.9 13.8 %collective-permute-start.3 = (bf16[256,512]{1,0:T(8,128)(2,1)S(1)}, bf16[256,512]{1,0:T(8,128)(2,1)S(1)}, u32[]{:S(2)}, u32[]{:S(2)}) collective-permute-start(bf16[256,512]{1,0:T(8,128)(2,1)S(1)} %get-tuple-element.64.refs_3_), channel_id=1, source_target_pairs={{0,1},{1,2},{2,3},{3,0},{4,5},{5,6},{6,7},{7,4},{8,9},{9,10},{10,1... | collective-permute-start | bytes 786440 | tf_op jit(solution)/shard_map/ppermute | solution.py:342
  54.9 13.5 %collective-permute-start.10 = (bf16[256,1024]{1,0:T(8,128)(2,1)}, bf16[256,1024]{1,0:T(8,128)(2,1)S(1)}, u32[]{:S(2)}, u32[]{:S(2)}) collective-permute-start(bf16[256,1024]{1,0:T(8,128)(2,1)} %get-tuple-element.71.refs_2_), channel_id=1, source_target_pairs={{0,4},{4,0},{8,12},{12,8},{16,20},{20,16},{24,28},{28,24},{32,36},... | collective-permute-start | bytes 1572872 | tf_op jit(solution)/shard_map/ppermute | solution.py:350
  66.0 2.4 %collective-permute-start.9 = (bf16[1,256,512]{2,1,0:T(8,128)(2,1)S(1)}, bf16[1,256,512]{2,1,0:T(8,128)(2,1)S(1)}, u32[]{:S(2)}, u32[]{:S(2)}) collective-permute-start(bf16[1,256,512]{2,1,0:T(8,128)(2,1)S(1)} %bitcast.10), channel_id=1, source_target_pairs={{0,4},{4,0},{8,12},{12,8},{16,20},{20,16},{24,28},{28,24},{32,36},... | collective-permute-start | bytes 786440 | tf_op jit(solution)/shard_map/ppermute | solution.py:350
  66.5 7.9 %collective-permute-start.8 = (bf16[256,512]{1,0:T(8,128)(2,1)S(1)}, bf16[256,512]{1,0:T(8,128)(2,1)S(1)}, u32[]{:S(2)}, u32[]{:S(2)}) collective-permute-start(bf16[256,512]{1,0:T(8,128)(2,1)S(1)} %slope.1.refs_0_), channel_id=1, source_target_pairs={{0,3},{1,0},{2,1},{3,2},{4,7},{5,4},{6,5},{7,6},{8,11},{9,8},{10,9... | collective-permute-start | bytes 786440 | tf_op jit(solution)/shard_map/ppermute | solution.py:342
  67.9 9.1 %collective-permute-start.7 = (bf16[256,512]{1,0:T(8,128)(2,1)S(1)}, bf16[256,512]{1,0:T(8,128)(2,1)S(1)}, u32[]{:S(2)}, u32[]{:S(2)}) collective-permute-start(bf16[256,512]{1,0:T(8,128)(2,1)S(1)} %slope.1.refs_0_), channel_id=1, source_target_pairs={{0,2},{1,3},{2,0},{3,1},{4,6},{5,7},{6,4},{7,5},{8,10},{9,11},{10,... | collective-permute-start | bytes 786440 | tf_op jit(solution)/shard_map/ppermute | solution.py:342
  67.9 14.8 %collective-permute-start.6 = (bf16[256,512]{1,0:T(8,128)(2,1)S(1)}, bf16[256,512]{1,0:T(8,128)(2,1)S(1)}, u32[]{:S(2)}, u32[]{:S(2)}) collective-permute-start(bf16[256,512]{1,0:T(8,128)(2,1)S(1)} %slope.1.refs_0_), channel_id=1, source_target_pairs={{0,1},{1,2},{2,3},{3,0},{4,5},{5,6},{6,7},{7,4},{8,9},{9,10},{10,1... | collective-permute-start | bytes 786440 | tf_op jit(solution)/shard_map/ppermute | solution.py:342
  86.8 4.7 %collective-permute-start.14 = (bf16[3,256,512]{2,1,0:T(8,128)(2,1)}, bf16[3,256,512]{2,1,0:T(8,128)(2,1)S(1)}, u32[]{:S(2)}, u32[]{:S(2)}) collective-permute-start(bf16[3,256,512]{2,1,0:T(8,128)(2,1)} %get-tuple-element.81.refs_0_), channel_id=1, source_target_pairs={{0,4},{4,0},{8,12},{12,8},{16,20},{20,16},{24,28},{28,24},{32,36},... | collective-permute-start | bytes 2359304 | tf_op jit(solution)/shard_map/ppermute | solution.py:350
  87.7 21.0 %all-to-all-start.2 = ((bf16[32,16,512]{2,1,0:T(8,128)(2,1)}), bf16[32,16,512]{2,1,0:T(8,128)(2,1)S(1)}, u32[]{:S(2)}, u32[]{:S(2)}) async-start(bf16[32,16,512]{2,1,0:T(8,128)(2,1)} %get-tuple-element.73), calls=%async_computation.2 | async-start | bytes 1048576 | tf_op jit(solution)/shard_map/all_to_all | solution.py:432
  96.9 11.0 %collective-permute-start.15 = (bf16[4,64,512]{2,1,0:T(8,128)(2,1)}, bf16[4,64,512]{2,1,0:T(8,128)(2,1)S(1)}, u32[]{:S(2)}, u32[]{:S(2)}) collective-permute-start(bf16[4,64,512]{2,1,0:T(8,128)(2,1)} %get-tuple-element.90), channel_id=1, source_target_pairs={{0,8},{4,12},{8,16},{12,20},{16,24},{20,28},{24,0},{28,4},{32,40},... | collective-permute-start | bytes 786440 | tf_op jit(solution)/shard_map/ppermute | solution.py:355
  98.1 15.7 %collective-permute-start.16 = (bf16[4,64,512]{2,1,0:T(8,128)(2,1)}, bf16[4,64,512]{2,1,0:T(8,128)(2,1)S(1)}, u32[]{:S(2)}, u32[]{:S(2)}) collective-permute-start(bf16[4,64,512]{2,1,0:T(8,128)(2,1)} %get-tuple-element.91), channel_id=1, source_target_pairs={{0,16},{4,20},{8,24},{12,28},{16,0},{20,4},{24,8},{28,12},{32,48},... | collective-permute-start | bytes 786440 | tf_op jit(solution)/shard_map/ppermute | solution.py:355
  100.5 13.6 %collective-permute-start.17 = (bf16[4,64,512]{2,1,0:T(8,128)(2,1)}, bf16[4,64,512]{2,1,0:T(8,128)(2,1)S(1)}, u32[]{:S(2)}, u32[]{:S(2)}) collective-permute-start(bf16[4,64,512]{2,1,0:T(8,128)(2,1)} %get-tuple-element.92), channel_id=1, source_target_pairs={{0,24},{4,28},{8,0},{12,4},{16,8},{20,12},{24,16},{28,20},{32,56},... | collective-permute-start | bytes 786440 | tf_op jit(solution)/shard_map/ppermute | solution.py:355
  101.7 13.4 %collective-permute-start.18 = (bf16[4,64,512]{2,1,0:T(8,128)(2,1)}, bf16[4,64,512]{2,1,0:T(8,128)(2,1)S(1)}, u32[]{:S(2)}, u32[]{:S(2)}) collective-permute-start(bf16[4,64,512]{2,1,0:T(8,128)(2,1)} %get-tuple-element.94), channel_id=1, source_target_pairs={{0,32},{4,36},{8,40},{12,44},{16,48},{20,52},{24,56},{28,60},{32,6... | collective-permute-start | bytes 786440 | tf_op jit(solution)/shard_map/ppermute | solution.py:364
  102.9 14.2 %collective-permute-start.19 = (bf16[4,64,512]{2,1,0:T(8,128)(2,1)}, bf16[4,64,512]{2,1,0:T(8,128)(2,1)}, u32[]{:S(2)}, u32[]{:S(2)}) collective-permute-start(bf16[4,64,512]{2,1,0:T(8,128)(2,1)} %get-tuple-element.95), channel_id=1, source_target_pairs={{0,64},{4,68},{8,72},{12,76},{16,80},{20,84},{24,88},{28,92},{32,9... | collective-permute-start | bytes 786440 | tf_op jit(solution)/shard_map/ppermute | solution.py:364
  107.9 9.2 %collective-permute-start.20 = (bf16[4,64,512]{2,1,0:T(8,128)(2,1)}, bf16[4,64,512]{2,1,0:T(8,128)(2,1)}, u32[]{:S(2)}, u32[]{:S(2)}) collective-permute-start(bf16[4,64,512]{2,1,0:T(8,128)(2,1)} %get-tuple-element.96), channel_id=1, source_target_pairs={{0,96},{4,100},{8,104},{12,108},{16,112},{20,116},{24,120},{28,124... | collective-permute-start | bytes 786440 | tf_op jit(solution)/shard_map/ppermute | solution.py:364
  113.8 5.9 %collective-permute-start.12 = (bf16[256,256]{1,0:T(8,128)(2,1)S(1)}, bf16[256,256]{1,0:T(8,128)(2,1)S(1)}, u32[]{:S(2)}, u32[]{:S(2)}) collective-permute-start(bf16[256,256]{1,0:T(8,128)(2,1)S(1)} %get-tuple-element.78), channel_id=1, source_target_pairs={{0,2},{1,3},{2,0},{3,1},{4,6},{5,7},{6,4},{7,5},{8,10},{9,11},{10,... | collective-permute-start | bytes 393224 | tf_op jit(solution)/shard_map/ppermute | solution.py:342
  114.1 6.7 %collective-permute-start.13 = (bf16[256,256]{1,0:T(8,128)(2,1)S(1)}, bf16[256,256]{1,0:T(8,128)(2,1)S(1)}, u32[]{:S(2)}, u32[]{:S(2)}) collective-permute-start(bf16[256,256]{1,0:T(8,128)(2,1)S(1)} %get-tuple-element.79), channel_id=1, source_target_pairs={{0,3},{1,0},{2,1},{3,2},{4,7},{5,4},{6,5},{7,6},{8,11},{9,8},{10,9... | collective-permute-start | bytes 393224 | tf_op jit(solution)/shard_map/ppermute | solution.py:342
  115.0 8.1 %collective-permute-start.11 = (bf16[256,256]{1,0:T(8,128)(2,1)S(1)}, bf16[256,256]{1,0:T(8,128)(2,1)S(1)}, u32[]{:S(2)}, u32[]{:S(2)}) collective-permute-start(bf16[256,256]{1,0:T(8,128)(2,1)S(1)} %get-tuple-element.77.refs_2_), channel_id=1, source_target_pairs={{0,1},{1,2},{2,3},{3,0},{4,5},{5,6},{6,7},{7,4},{8,9},{9,10},{10,1... | collective-permute-start | bytes 393224 | tf_op jit(solution)/shard_map/ppermute | solution.py:342
  124.1 27.2 %copy-start.5 = (bf16[256,512]{1,0:T(8,128)(2,1)S(1)}, bf16[256,512]{1,0:T(8,128)(2,1)}, u32[]{:S(2)}) copy-start(bf16[256,512]{1,0:T(8,128)(2,1)} %get-tuple-element.75.refs_3_.refs_1_) | copy-start | bytes 786436
  124.1 27.1 %all-to-all-start.3 = ((bf16[32,144,128]{2,1,0:T(8,128)(2,1)}), bf16[32,144,128]{2,1,0:T(8,128)(2,1)S(1)}, u32[]{:S(2)}, u32[]{:S(2)}) async-start(bf16[32,144,128]{2,1,0:T(8,128)(2,1)} %get-tuple-element.99), calls=%async_computation.3 | async-start | bytes 2359296 | tf_op jit(solution)/shard_map/all_to_all | solution.py:461
  129.0 17.5 %collective-permute-start.21 = (bf16[64,512]{1,0:T(8,128)(2,1)S(1)}, bf16[64,512]{1,0:T(8,128)(2,1)S(1)}, u32[]{:S(2)}, u32[]{:S(2)}) collective-permute-start(bf16[64,512]{1,0:T(8,128)(2,1)S(1)} %get-tuple-element.101), channel_id=1, source_target_pairs={{0,32},{4,36},{8,40},{12,44},{16,48},{20,52},{24,56},{28,60},{32,6... | collective-permute-start | bytes 196616 | tf_op jit(solution)/shard_map/ppermute | solution.py:364
  130.4 18.7 %collective-permute-start.22 = (bf16[64,512]{1,0:T(8,128)(2,1)S(1)}, bf16[64,512]{1,0:T(8,128)(2,1)S(1)}, u32[]{:S(2)}, u32[]{:S(2)}) collective-permute-start(bf16[64,512]{1,0:T(8,128)(2,1)S(1)} %get-tuple-element.102), channel_id=1, source_target_pairs={{0,64},{4,68},{8,72},{12,76},{16,80},{20,84},{24,88},{28,92},{32,9... | collective-permute-start | bytes 196616 | tf_op jit(solution)/shard_map/ppermute | solution.py:364
  132.9 16.2 %collective-permute-start.23 = (bf16[64,512]{1,0:T(8,128)(2,1)S(1)}, bf16[64,512]{1,0:T(8,128)(2,1)S(1)}, u32[]{:S(2)}, u32[]{:S(2)}) collective-permute-start(bf16[64,512]{1,0:T(8,128)(2,1)S(1)} %get-tuple-element.103), channel_id=1, source_target_pairs={{0,96},{4,100},{8,104},{12,108},{16,112},{20,116},{24,120},{28,124... | collective-permute-start | bytes 196616 | tf_op jit(solution)/shard_map/ppermute | solution.py:364
  134.0 15.1 %collective-permute-start.24 = (bf16[64,512]{1,0:T(8,128)(2,1)S(1)}, bf16[64,512]{1,0:T(8,128)(2,1)S(1)}, u32[]{:S(2)}, u32[]{:S(2)}) collective-permute-start(bf16[64,512]{1,0:T(8,128)(2,1)S(1)} %get-tuple-element.105), channel_id=1, source_target_pairs={{0,8},{4,12},{8,16},{12,20},{16,24},{20,28},{24,0},{28,4},{32,40},... | collective-permute-start | bytes 196616 | tf_op jit(solution)/shard_map/ppermute | solution.py:355
  135.2 13.9 %collective-permute-start.25 = (bf16[64,512]{1,0:T(8,128)(2,1)S(1)}, bf16[64,512]{1,0:T(8,128)(2,1)S(1)}, u32[]{:S(2)}, u32[]{:S(2)}) collective-permute-start(bf16[64,512]{1,0:T(8,128)(2,1)S(1)} %get-tuple-element.106), channel_id=1, source_target_pairs={{0,16},{4,20},{8,24},{12,28},{16,0},{20,4},{24,8},{28,12},{32,48},... | collective-permute-start | bytes 196616 | tf_op jit(solution)/shard_map/ppermute | solution.py:355
  146.5 3.9 %collective-permute-start.26 = (bf16[64,512]{1,0:T(8,128)(2,1)S(1)}, bf16[64,512]{1,0:T(8,128)(2,1)S(1)}, u32[]{:S(2)}, u32[]{:S(2)}) collective-permute-start(bf16[64,512]{1,0:T(8,128)(2,1)S(1)} %get-tuple-element.107), channel_id=1, source_target_pairs={{0,24},{4,28},{8,0},{12,4},{16,8},{20,12},{24,16},{28,20},{32,56},... | collective-permute-start | bytes 196616 | tf_op jit(solution)/shard_map/ppermute | solution.py:355
  (11 other events, 34.7 us)

commit v3 on v2

--- a/solution.py
+++ b/solution.py
@@ -48,19 +48,18 @@
     return jnp.where(row == routes, 1.0, 0.0)
 
 
-def pick_kernel(place, f0, f1, f2, f3, sel_ref, full_ref, send_ref):
-    for d, piece in enumerate((f0, f1, f2, f3)):
-        origin = lax.rem(place.hid + HID - d, HID)
-        full_ref[:, pl.ds(pl.multiple_of(origin * LANES, LANES), LANES)] = piece[...]
-    send_ref[...] = mm(sel_ref[...], full_ref[...]).astype(BF16).reshape(PEERS, SLOTS, UNITS)
+def pick_kernel(routes_ref, feat_ref, sel_ref, send_ref):
+    sel = route_rows(routes_ref).T.astype(BF16)
+    sel_ref[...] = sel
+    picked = mm(sel, feat_ref[...]).astype(BF16).reshape(PEERS, SLOTS, LANES)
+    for part in range(HID):
+        send_ref[:, part] = picked
 
 
 def count_kernel(
-    neigh_ref, degree_ref, routes_ref, adj_ref, adjt_ref, inv_ref, sel_ref, selt_ref, key_ref, low_ref, high_ref
+    neigh_ref, degree_ref, routes_ref, adj_ref, adjt_ref, inv_ref, selt_ref, key_ref, low_ref, high_ref
 ):
-    chosen = route_rows(routes_ref)
-    selt_ref[...] = chosen.astype(BF16)
-    sel_ref[...] = chosen.T.astype(BF16)
+    selt_ref[...] = route_rows(routes_ref).astype(BF16)
     inv_ref[...] = 1.0 / jnp.broadcast_to(degree_ref[...].astype(F32), (LANES, ROWS)).T
     entry = neigh_ref[...]
     used = lax.broadcasted_iota(jnp.int32, (KEPT, ROWS), 0) < degree_ref[...]
@@ -98,10 +97,15 @@
         adj_ref[:, rows] = adjt_ref[rows, :].astype(F32).T.astype(BF16)
 
 
-def first_kernel(full_ref, far_ref, adj_ref, inv_ref, w_ref, sel_ref, both_ref, hidden_ref, send_ref):
-    full = full_ref[...]
-    agg = mm(adj_ref[:, :ROWS], full) + mm(adj_ref[:, ROWS:], far_ref[...].reshape(FAR, UNITS))
-    both_ref[:, :UNITS] = full
+def first_kernel(
+    place, f0, f1, f2, f3, far_ref, adj_ref, inv_ref, w_ref, sel_ref, both_ref, hidden_ref, send_ref, far_all
+):
+    for d, piece in enumerate((f0, f1, f2, f3)):
+        origin = lax.rem(place.hid + HID - d, HID)
+        both_ref[:, pl.ds(pl.multiple_of(origin * LANES, LANES), LANES)] = piece[...]
+    for origin in range(HID):
+        far_all[:, origin * LANES : (origin + 1) * LANES] = far_ref[:, origin].reshape(FAR, LANES)
+    agg = mm(adj_ref[:, :ROWS], both_ref[:, :UNITS]) + mm(adj_ref[:, ROWS:], far_all[...])
     both_ref[:, UNITS:] = (agg * wide(inv_ref[...], UNITS)).astype(BF16)
     pre = mm(both_ref[...], w_ref[...])
     sig = 1.0 / (1.0 + jnp.exp(-pre))
@@ -118,92 +122,111 @@
 
 
 def second_kernel(
-    place, hidden_ref, far_ref, adj_ref, inv_ref, w_ref, stacked_ref, own_ref, s1, s2, s3
+    place, hidden_ref, far_ref, adj_ref, inv_ref, w_hbm, stacked_ref,
+    own_a, own_b, s1a, s1b, s2a, s2b, s3a, s3b, w_ref, sems,
 ):
+    order = ((2, s2a, s2b), (1, s1a, s1b), (3, s3a, s3b), (0, own_a, own_b))
+    copies = []
+    for slot, (d, upper, lower) in enumerate(order):
+        target = lax.rem(place.hid + d, HID)
+        cols = pl.ds(pl.multiple_of(target * UNITS, UNITS), UNITS)
+        copies.append(pltpu.make_async_copy(w_hbm.at[:, cols], w_ref.at[slot], sems.at[slot]))
+        copies[-1].start()
     hidden = hidden_ref[...]
     total = mm(adj_ref[:, :ROWS], hidden) + mm(adj_ref[:, ROWS:], far_ref[...].reshape(FAR, UNITS))
     stacked_ref[:, :UNITS] = hidden
     stacked_ref[:, UNITS:] = (total * wide(inv_ref[...], UNITS)).astype(BF16)
-    for d, out in ((2, s2), (1, s1), (3, s3), (0, own_ref)):
-        target = lax.rem(place.hid + d, HID)
-        cols = pl.ds(pl.multiple_of(target * UNITS, UNITS), UNITS)
-        out[...] = mm(stacked_ref[...], w_ref[:, cols]).astype(out.dtype)
-
-
-def slope_kernel(count_ref, own_ref, r1, r2, r3, cot_ref, grad_ref):
+    for slot, (d, upper, lower) in enumerate(order):
+        copies[slot].wait()
+        part = mm(stacked_ref[...], w_ref[slot]).astype(upper.dtype)
+        upper[...] = part[: ROWS // 2]
+        lower[...] = part[ROWS // 2 :]
+
+
+def slope_kernel(first_row, count_ref, own_ref, r1, r2, r3, cot_ref, grad_ref):
     pre = own_ref[...] + r1[...].astype(F32) + r2[...].astype(F32) + r3[...].astype(F32)
     sig = 1.0 / (1.0 + jnp.exp(-pre))
-    slope = cot_ref[...].astype(F32) * (sig * (1.0 + pre * (1.0 - sig)))
-    live = lax.broadcasted_iota(jnp.int32, (ROWS, UNITS), 0) < count_ref[0]
+    slope = cot_ref[first_row : first_row + ROWS // 2, :].astype(F32) * (sig * (1.0 + pre * (1.0 - sig)))
+    live = lax.broadcasted_iota(jnp.int32, pre.shape, 0) + first_row < count_ref[0]
     grad_ref[...] = jnp.where(live, slope, 0.0).astype(BF16)
 
 
-def spread_kernel(place, g0, g1, g2, g3, w_ref, inv_ref, adjt_ref, halo_ref, own_ref, others_ref):
-    order = ((0, g0), (3, g3), (1, g1), (2, g2))
-    for index, grad in enumerate((g1, g2, g3)):
-        others_ref[index] = grad[...]
+def spread_kernel(
+    place, g0a, g0b, g1a, g1b, g2a, g2b, g3a, g3b, w_ref, inv_ref, adjt_ref, halo_ref, own_hbm, others_ref,
+    own_ref, sems,
+):
+    parts = ((g0a, g0b), (g1a, g1b), (g2a, g2b), (g3a, g3b))
+    rows = ROWS // 2
+    copies = [
+        pltpu.make_async_copy(ref, others_ref.at[d, pl.ds(half * rows, rows)], sems.at[2 * d + half])
+        for d, pair in enumerate(parts)
+        for half, ref in enumerate(pair)
+    ]
+    for copy in copies:
+        copy.start()
+    grads = {d: jnp.concatenate([upper[...], lower[...]], axis=0) for d, (upper, lower) in enumerate(parts)}
 
     def back(base):
         total = None
-        for d, grad in order:
+        for d in (0, 3, 1, 2):
             origin = lax.rem(place.hid + HID - d, HID)
             cols = pl.ds(pl.multiple_of(origin * UNITS, UNITS), UNITS)
-            term = mm_last(grad[...], w_ref[base : base + UNITS, cols])
+            term = mm_last(grads[d], w_ref[base : base + UNITS, cols])
             total = term if total is None else total + term
         return total
 
     mean = (back(UNITS) * wide(inv_ref[...], UNITS)).astype(BF16)
+    own_ref[...] = back(0) + mm(adjt_ref[:ROWS, :], mean)
+    copies.append(pltpu.make_async_copy(own_ref, own_hbm, sems.at[8]))
+    copies[-1].start()
     halo_ref[...] = mm(adjt_ref[ROWS:, :], mean).astype(BF16).reshape(PEERS, SLOTS, UNITS)
-    own_ref[...] = back(0) + mm(adjt_ref[:ROWS, :], mean)
+    for copy in copies:
+        copy.wait()
 
 
 def outer_second_kernel(scale, slots, place, grads_ref, mates_ref, stacked_ref, stacked_mate_ref, *refs):
-    a_outs, b_outs, (block_ref, sems) = refs[-10:-6], refs[-6:-2], refs[-2:]
+    outs, (block_ref, sems) = refs[-6:-2], refs[-2:]
     row = lax.broadcasted_iota(jnp.int32, (UNITS, UNITS // 2), 0)
     col = lax.broadcasted_iota(jnp.int32, (UNITS, UNITS // 2), 1)
     wanted = (col >> 6) * 128 + place.core * 64 + (col & 63)
     keep = jnp.where(row == wanted, 1.0, 0.0).astype(BF16)
-    copies = []
     for index, slot in enumerate(slots):
         mine = mm(grads_ref[index], keep).astype(BF16)
         other = mm(mates_ref[index], keep).astype(BF16)
         total = mm_first(mine, stacked_ref[...]) + mm_first(other, stacked_mate_ref[...])
-        total = (total * scale).astype(BF16)
-        block_ref[index, 0] = total[:, :UNITS].reshape(HID, 64, UNITS)
-        block_ref[index, 1] = total[:, UNITS:].reshape(HID, 64, UNITS)
-        for d, out in enumerate(a_outs):
-            copies.append(pltpu.make_async_copy(
-                block_ref.at[index, 0, lax.rem(place.z + d, HID)], out.at[slot], sems.at[index, d]
-            ))
-            copies[-1].start()
+        block_ref[index] = (total * scale).astype(BF16).reshape(HID, 64, 2 * UNITS)
+
+        @pl.when(place.core == 0)
+        def _():
+            for d, out in enumerate(outs):
+                source = block_ref.at[index, lax.rem(place.z + d, HID)]
+                pltpu.make_async_copy(source, out.at[slot], sems.at[index, d]).start()
+
         step = lax.rem(place.hid + 2 * HID - place.x - slot, HID)
-        for d, out in enumerate(b_outs):
-
-            @pl.when(step == d)
+        for d, out in enumerate(outs):
+
+            @pl.when((place.core == 1) & (step == d))
             def _():
-                pltpu.make_async_copy(block_ref.at[index, 1], out, sems.at[index, HID]).start()
+                for z in range(HID):
+                    pltpu.make_async_copy(block_ref.at[index, z], out.at[z], sems.at[index, z]).start()
 
     for index, slot in enumerate(slots):
-        pltpu.make_async_copy(block_ref.at[index, 1], b_outs[0], sems.at[index, HID]).wait()
-    for copy in copies:
-        copy.wait()
-
-
-def middle_kernel(place, a0, a1, a2, a3, b0, b1, b2, b3, c0, c1, c2, c3, d0, d1, d2, d3, total_ref):
-    total_ref[0] = a0[...].astype(F32) + a1[...].astype(F32) + a2[...].astype(F32) + a3[...].astype(F32)
-    total_ref[1] = b0[...].astype(F32) + b1[...].astype(F32) + b2[...].astype(F32) + b3[...].astype(F32)
-    for d, out in enumerate((c0, c1, c2, c3)):
-        out[...] = total_ref[0, lax.rem(place.hid + 2 * HID - place.x - d, HID)].astype(out.dtype)
-    for d, out in enumerate((d0, d1, d2, d3)):
-        out[...] = total_ref[1, lax.rem(place.z + d, HID)].astype(out.dtype)
-
-
-def last_second_kernel(c0, c1, c2, c3, d0, d1, d2, d3, out_ref):
-    for half, parts in enumerate(((c0, c1, c2, c3), (d0, d1, d2, d3))):
-        total = parts[0][...]
-        for part in parts[1:]:
-            total = total + part[...].astype(F32)
-        out_ref[:, half, :] = total
+        for d, out in enumerate(outs):
+            pltpu.make_async_copy(block_ref.at[index, d], out.at[slot], sems.at[index, d]).wait()
+
+
+def along_kernel(place, z0, z1, z2, z3, x0, x1, x2, x3):
+    for d, out in enumerate((x0, x1, x2, x3)):
+        by_x = lax.rem(place.hid + 2 * HID - place.x - d, HID)
+        at = jnp.where(place.core == 0, by_x, lax.rem(place.z + d, HID))
+        total = z0[at].astype(F32) + z1[at].astype(F32) + z2[at].astype(F32) + z3[at].astype(F32)
+        out[...] = total.astype(out.dtype)
+
+
+def last_second_kernel(x0, x1, x2, x3, out_ref):
+    total = x0[...] + x1[...].astype(F32) + x2[...].astype(F32) + x3[...].astype(F32)
+    out_ref[:, 0, :] = total[:, :UNITS]
+    out_ref[:, 1, :] = total[:, UNITS:]
 
 
 def settle_kernel(
@@ -350,19 +373,13 @@
     return lax.ppermute(value, "nodes", [(i, i ^ 1) for i in range(PEERS)])
 
 
-def along_z(values):
+def near(values, turned):
+    def target(x, z, core, d):
+        return node_at(x, z + d, core) if (core == 0) != turned else node_at(x + d, z, core)
+
     return [
         lax.ppermute(v, "nodes", [
-            (node_at(x, z, c), node_at(x, z + d, c)) for x in range(4) for z in range(4) for c in range(2)
-        ])
-        for d, v in values
-    ]
-
-
-def along_x(values):
-    return [
-        lax.ppermute(v, "nodes", [
-            (node_at(x, z, c), node_at(x + d, z, c)) for x in range(4) for z in range(4) for c in range(2)
+            (node_at(x, z, c), target(x, z, c, d)) for x in range(4) for z in range(4) for c in range(2)
         ])
         for d, v in values
     ]
@@ -377,97 +394,102 @@
 
     wide_chunk = ((ROWS, UNITS), F32)
     halo = ((PEERS, SLOTS, UNITS), BF16)
+    sel, send_feat = call(
+        pick_kernel, "pick", (routes, features),
+        [((FAR, ROWS), BF16), ((PEERS, HID, SLOTS, LANES), BF16)], late=(0, 1), work=1,
+    )
+    far_feat = lax.all_to_all(
+        send_feat.reshape(PEERS * HID, SLOTS, LANES), ("nodes", "hid"), 0, 0, tiled=True
+    ).reshape(PEERS, HID, SLOTS, LANES)
     f2, f1, f3 = around([(2, features), (1, features), (3, features)])
-    adj, adjt, inv, sel, selt = call(
+    adj, adjt, inv, selt = call(
         count_kernel, "count", (jnp.swapaxes(neighbors, 0, 1), degree.reshape(1, ROWS), routes),
         [
-            ((ROWS, ROWS + FAR), BF16), ((ROWS + FAR, ROWS), BF16), ((ROWS, LANES), F32),
-            ((FAR, ROWS), BF16), ((ROWS, FAR), BF16),
+            ((ROWS, ROWS + FAR), BF16), ((ROWS + FAR, ROWS), BF16), ((ROWS, LANES), F32), ((ROWS, FAR), BF16),
         ],
-        scratch=[pltpu.VMEM((KEPT, ROWS), jnp.int32)] * 3, late=(2, 1, 0), stored=(4,), work=8,
-    )
-    full, send_feat = call(
-        pick_kernel, "pick", (features, f1, f2, f3, sel), [chunk, halo], placed=True,
-    )
-    far_feat = lax.all_to_all(send_feat, "nodes", 0, 0, tiled=True)
+        scratch=[pltpu.VMEM((KEPT, ROWS), jnp.int32)] * 3, late=(2, 1, 0), stored=(3,), work=8, after=(sel,),
+    )
     both, hidden, send_hidden = call(
-        first_kernel, "first", (full, far_feat, adj, inv, w1, sel),
-        [((ROWS, 2 * UNITS), BF16), chunk, halo], work=6,
+        first_kernel, "first", (features, f1, f2, f3, far_feat, adj, inv, w1, sel),
+        [((ROWS, 2 * UNITS), BF16), chunk, halo], work=6, placed=True,
+        scratch=[pltpu.VMEM((FAR, UNITS), BF16)],
     )
     far_hidden = lax.all_to_all(send_hidden, "nodes", 0, 0, tiled=True)
-    stacked, own_pre, s1, s2, s3 = call(
+    half_chunk = ((ROWS // 2, UNITS), BF16)
+    stacked, own_a, own_b, s1a, s1b, s2a, s2b, s3a, s3b = call(
         second_kernel, "second", (hidden, far_hidden, adj, inv, w2),
-        [((ROWS, 2 * UNITS), BF16), wide_chunk] + [chunk] * 3, placed=True, work=10,
-    )
-    r2, r1, r3 = around([(2, s2), (1, s1), (3, s3)])
+        [((ROWS, 2 * UNITS), BF16)] + [((ROWS // 2, UNITS), F32)] * 2 + [half_chunk] * 6,
+        scratch=[pltpu.VMEM((HID, 2 * UNITS, UNITS), BF16), pltpu.SemaphoreType.DMA((HID,))],
+        placed=True, work=10, held=(4,),
+    )
+    r2a, r1a, r3a = around([(2, s2a), (1, s1a), (3, s3a)])
+    r2b, r1b, r3b = around([(2, s2b), (1, s1b), (3, s3b)])
     slope, saved = call(
         gate_kernel, "gate", (both, stacked, w1), [wide_chunk, ((ROWS, 2 * UNITS), BF16)],
-        after=(s1,), late=(2,), stored=(0, 1), work=2,
+        after=(s1a,), late=(2,), stored=(0, 1), work=2,
     )
     saved_mate = swap(saved)
-    g0 = call(
-        slope_kernel, "slope", (node_count, own_pre, r1, r2, r3, cotangent), [chunk], scalars=1,
-        after=(in_hbm(slope),),
-    )
-    g2, g1, g3 = around([(2, g0), (1, g0), (3, g0)])
-
-    def outer(slots, grads, held):
+    def gradient(first_row, own, parts):
+        return call(
+            lambda *refs: slope_kernel(first_row, *refs), "slope", (node_count, own, *parts, cotangent),
+            [half_chunk], scalars=1, after=(in_hbm(slope),),
+        )
+
+    g0a = gradient(0, own_a, (r1a, r2a, r3a))
+    g2a, g1a, g3a = around([(2, g0a), (1, g0a), (3, g0a)])
+    g0b = gradient(ROWS // 2, own_b, (r1b, r2b, r3b))
+    g2b, g1b, g3b = around([(2, g0b), (1, g0b), (3, g0b)])
+
+    def outer(slots, grads, held, late):
         return tuple(call(
             lambda *refs: outer_second_kernel(scale, slots, *refs), "outer_second",
             (grads, swap(grads), saved, saved_mate, *held),
-            [((HID, 64, UNITS), BF16)] * 8,
+            [((HID, 64, 2 * UNITS), BF16)] * HID,
             scratch=[
-                pltpu.VMEM((len(slots), 2, HID, 64, UNITS), BF16),
-                pltpu.SemaphoreType.DMA((len(slots), HID + 1)),
+                pltpu.VMEM((len(slots), HID, 64, 2 * UNITS), BF16),
+                pltpu.SemaphoreType.DMA((len(slots), HID)),
             ],
-            placed=True, loose=tuple(range(8)), late=(2, 0, 3, 1),
-            aliases={4 + index: index for index in range(8)} if held else None, work=3 * len(slots),
+            placed=True, loose=tuple(range(HID)), late=late,
+            aliases={4 + index: index for index in range(HID)} if held else None, work=3 * len(slots),
         ))
 
-    z = outer((0,), g0.reshape(1, ROWS, UNITS), ())
     halo_hidden, own_hidden, others = call(
-        spread_kernel, "spread", (g0, g1, g2, g3, w2, inv, adjt),
-        [halo, wide_chunk, ((3, ROWS, UNITS), BF16)], placed=True, after=(in_hbm(z[0]),), work=10, stored=(2,),
+        spread_kernel, "spread", (g0a, g0b, g1a, g1b, g2a, g2b, g3a, g3b, w2, inv, adjt),
+        [halo, wide_chunk, ((HID, ROWS, UNITS), BF16)], placed=True, work=10, loose=(1, 2),
+        scratch=[pltpu.VMEM((ROWS, UNITS), F32), pltpu.SemaphoreType.DMA((9,))],
     )
     back_hidden = lax.all_to_all(halo_hidden, "nodes", 0, 0, tiled=True)
-    z = outer((1, 2, 3), others, z)
-    a0, a1, a2, a3, b0, b1, b2, b3 = z
-    a2, b2, a1, b1, a3, b3 = (
-        along_z([(2, a2)]) + along_x([(2, b2)]) + along_z([(1, a1)]) + along_x([(1, b1)])
-        + along_z([(3, a3)]) + along_x([(3, b3)])
-    )
-    c0, c1, c2, c3, d0, d1, d2, d3 = call(
-        middle_kernel, "middle", (a0, a1, a2, a3, b0, b1, b2, b3),
-        ([((64, UNITS), F32)] + [((64, UNITS), BF16)] * 3) * 2,
-        scratch=[pltpu.VMEM((2, HID, 64, UNITS), F32)], placed=True, late=tuple(range(8)),
-    )
+    z0, z1, z2, z3 = outer((0, 1, 2, 3), others, (), (0, 2, 3))
+    outer_done = in_hbm(z0)
+    z2, z1, z3 = near([(2, z2), (1, z1), (3, z3)], False)
     grad, mine, s1, s2, s3 = call(
         settle_kernel, "settle",
         (back_hidden, own_hidden, slope, selt, w1),
         [chunk, ((ROWS, 2 * LANES), F32)] + [((ROWS, 2 * LANES), BF16)] * 3,
-        scratch=[pltpu.VMEM((ROWS, 2 * UNITS), F32)], placed=True, late=(3, 2, 4), work=6,
+        scratch=[pltpu.VMEM((ROWS, 2 * UNITS), F32)], placed=True, late=(3, 1, 2, 4), work=6, after=(outer_done,),
     )
     r2, r1, r3 = around([(2, s2), (1, s1), (3, s3)])
     merged = call(
         lambda *refs: outer_first_kernel(scale, *refs), "outer_first", (both, grad),
         [((PEERS, LANES + SLOTS, LANES), BF16)], after=(s1,), stored=(0,), work=2,
     )
+    x0, x1, x2, x3 = call(
+        along_kernel, "along", (z0, z1, z2, z3),
+        [((64, 2 * UNITS), F32)] + [((64, 2 * UNITS), BF16)] * 3, placed=True, late=(0,), after=(s1,),
+    )
     base, merged = call(
         return_kernel, "return", (mine, r1, r2, r3, inv, adjt, merged),
         [((ROWS, LANES), F32), ((PEERS, LANES + SLOTS, LANES), BF16)],
         scratch=[pltpu.VMEM((PEERS, SLOTS, LANES), BF16), pltpu.SemaphoreType.DMA],
-        loose=(1,), aliases={6: 1}, after=(c0,),
+        loose=(1,), aliases={6: 1}, after=(x0,),
     )
     parts = lax.all_to_all(merged, "nodes", 0, 0, tiled=True)
-    c2, d2, c1, d1, c3, d3 = (
-        along_x([(2, c2)]) + along_z([(2, d2)]) + along_x([(1, c1)]) + along_z([(1, d1)])
-        + along_x([(3, c3)]) + along_z([(3, d3)])
-    )
+    x2, x1, x3 = near([(2, x2), (1, x1), (3, x3)], True)
     grad_features, grad_w_first = call(
         final_kernel, "final", (base, selt, parts),
         [((ROWS, LANES), F32), ((SLOTS, 2, UNITS), F32)],
     )
-    grad_w_second = call(last_second_kernel, "last_second", (c0, c1, c2, c3, d0, d1, d2, d3), [((64, 2, UNITS), F32)])
+    grad_w_second = call(last_second_kernel, "last_second", (x0, x1, x2, x3), [((64, 2, UNITS), F32)])
     return grad_w_first, grad_w_second, grad_features
 
 

time: 153 us -> 139 us (0.908)
  blocking collectives: 36.2 us -> 16.8 us
  starting transfers between devices: 43.2 us -> 54.6 us
  local copies, waits for them, and re-layouts: 3.35 us -> 0.03 us
  waiting for transfers between devices: 39.2 us -> 36.4 us
    all_to_all x1 -> x0, blocking collectives: 21.1 us -> none  [on_device(): far_feat = lax.all_to_all(send_feat, 'nodes', 0, 0, tiled=True)]
    all_to_all x0 -> x1, starting transfers between devices: none -> 11.5 us  [on_device(): lax.all_to_all(send_feat.reshape(PEERS * HID, SLOTS, LANES), ('nodes', 'h...]
    ppermute x12 -> x6, starting transfers between devices: 20.5 us -> 10.1 us  [near(): lax.ppermute(v, 'nodes', [(node_at(x, z, c), target(x, z, c, d)) for x in...]
    ppermute x12 -> x18, waiting for transfers between devices: 23.5 us -> 14.9 us  [around(): lax.ppermute(v, 'hid', [(i, (i + d) % HID) for i in range(HID)])]
    ppermute x12 -> x18, starting transfers between devices: 12.2 us -> 19 us  [around(): lax.ppermute(v, 'hid', [(i, (i + d) % HID) for i in range(HID)])]
    unnamed x28 -> x12, local copies, waits for them, and re-layouts: 3.35 us -> 0.03 us
    all_to_all x1, starting transfers between devices: 4.88 us -> 7.52 us  [on_device(): parts = lax.all_to_all(merged, 'nodes', 0, 0, tiled=True)]
    ppermute x12 -> x6, waiting for transfers between devices: 15.7 us -> 18.1 us  [near(): lax.ppermute(v, 'nodes', [(node_at(x, z, c), target(x, z, c, d)) for x in...]
  transfers between devices with their start and end apart: 29 -> 29, of which waited for: 13 -> 13; matrix products, arithmetic and copies ran while one was open for 0% -> 0% of each run, Pallas kernels for 14% -> 13%
where the time goes in v3:
time: 139 us; the launch traced here: 138 us
  starting transfers between devices  54.6 us (39%)
  waiting for transfers between devices  36.4 us (26%)
  Pallas kernels  29 us (21%)
  blocking collectives  16.8 us (12%)
  between operations  1.54 us (1%)
    pallas_call x15, Pallas kernels, call(): pl.pallas_call(body, out_shape=shapes, in_specs=in_specs, out_specs=out_s...  29 us
    ppermute x18, starting transfers between devices, around(): lax.ppermute(v, 'hid', [(i, (i + d) % HID) for i in range(HID)])  19 us
    ppermute x6, waiting for transfers between devices, near(): lax.ppermute(v, 'nodes', [(node_at(x, z, c), target(x, z, c, d)) for x in...  18.1 us
    all_to_all x1, blocking collectives, on_device(): far_hidden = lax.all_to_all(send_hidden, 'nodes', 0, 0, tiled=True)  16.8 us
    ppermute x18, waiting for transfers between devices, around(): lax.ppermute(v, 'hid', [(i, (i + d) % HID) for i in range(HID)])  14.9 us
    all_to_all x1, starting transfers between devices, on_device(): lax.all_to_all(send_feat.reshape(PEERS * HID, SLOTS, LANES), ('nodes', 'h...  11.5 us
    ppermute x6, starting transfers between devices, near(): lax.ppermute(v, 'nodes', [(node_at(x, z, c), target(x, z, c, d)) for x in...  10.1 us
    all_to_all x1, starting transfers between devices, on_device(): parts = lax.all_to_all(merged, 'nodes', 0, 0, tiled=True)  7.52 us
  transfers between devices with their start and end apart: 29, of which 13 were waited for; matrix products, arithmetic and copies ran while one was open for 0% of the time, Pallas kernels for 13%

profile of v3, /device:TPU:1, one launch (start us, length us, event | category | flops | bytes accessed | tf_op | source)
XLA Modules:
  0.0 138.4 jit_solution(18234946066553727519)
XLA Ops:
  0.6 2.0 %pick.1 = (bf16[512,256]{1,0:T(8,128)(2,1)S(1)}, bf16[32,4,16,128]{3,2,1,0:T(8,128)(2,1)}) custom-call(s32[16,32]{1,0:T(8,128)} %bitcast.16, bf16[256,128]{1,0:T(8,128)(2,1)} %refs_0_.3), custom_call_target="tpu_custom_call" | custom-call | flops 134217728 | bytes 854016 | tf_op jit(solution)/shard_map/pick/pallas_call | solution.py:350
  2.7 11.5 %all-to-all-start = ((bf16[128,16,128]{2,1,0:T(8,128)(2,1)}), bf16[128,16,128]{2,1,0:T(8,128)(2,1)S(1)}, u32[]{:S(2)}, u32[]{:S(2)}) async-start(bf16[128,16,128]{2,1,0:T(8,128)(2,1)} %bitcast.2), calls=%async_computation | async-start | bytes 1048576 | tf_op jit(solution)/shard_map/all_to_all | solution.py:401
  14.2 2.7 %collective-permute-start.2 = (bf16[256,128]{1,0:T(8,128)(2,1)S(1)}, bf16[256,128]{1,0:T(8,128)(2,1)S(1)}, u32[]{:S(2)}, u32[]{:S(2)}) collective-permute-start(bf16[256,128]{1,0:T(8,128)(2,1)S(1)} %copy-done.4), channel_id=1, source_target_pairs={{0,3},{1,0},{2,1},{3,2},{4,7},{5,4},{6,5},{7,6},{8,11},{9,8},{10,9... | collective-permute-start | bytes 196616 | tf_op jit(solution)/shard_map/ppermute | solution.py:365
  18.0 4.0 %count.1 = (bf16[256,768]{1,0:T(8,128)(2,1)S(1)}, bf16[768,256]{1,0:T(8,128)(2,1)S(1)}, f32[256,128]{1,0:T(8,128)S(1)}, bf16[256,512]{1,0:T(8,128)(2,1)}) custom-call(s32[80,256]{1,0:T(8,128)} %bitcast.15, s32[1,256]{1,0:T(1,128)} %bitcast.18, s32[16,32]{1,0:T(8,128)} %bitcast.17, bf16[512,256]{1,0:T(8,128)(2,1)S(1)} %get-tuple-element.44.refs_3_.refs_8_), custom_call_target="tpu_custom_call" | custom-call | flops 1073741824 | bytes 1264640 | tf_op jit(solution)/shard_map/count/pallas_call | solution.py:350
  22.1 3.2 %collective-permute-done.1.refs_2_ = bf16[256,128]{1,0:T(8,128)(2,1)S(1)} collective-permute-done((bf16[256,128]{1,0:T(8,128)(2,1)S(1)}, bf16[256,128]{1,0:T(8,128)(2,1)S(1)}, u32[]{:S(2)}, u32[]{:S(2)}) %collective-permute-start.1) | collective-permute-done | bytes 65568 | tf_op jit(solution)/shard_map/ppermute | solution.py:365
  25.2 1.6 %collective-permute-done.refs_1_ = bf16[256,128]{1,0:T(8,128)(2,1)S(1)} collective-permute-done((bf16[256,128]{1,0:T(8,128)(2,1)S(1)}, bf16[256,128]{1,0:T(8,128)(2,1)S(1)}, u32[]{:S(2)}, u32[]{:S(2)}) %collective-permute-start) | collective-permute-done | bytes 65568 | tf_op jit(solution)/shard_map/ppermute | solution.py:365
  26.9 1.5 %all-to-all-done = bf16[128,16,128]{2,1,0:T(8,128)(2,1)S(1)} async-done(((bf16[128,16,128]{2,1,0:T(8,128)(2,1)}), bf16[128,16,128]{2,1,0:T(8,128)(2,1)S(1)}, u32[]{:S(2)}, u32[]{:S(2)}) %all-to-all-start) | async-done | bytes 524320 | tf_op jit(solution)/shard_map/all_to_all | solution.py:401
  29.4 16.8 %all_to_all.20.refs_1_ = bf16[32,16,512]{2,1,0:T(8,128)(2,1)S(1)} all-to-all(bf16[32,16,512]{2,1,0:T(8,128)(2,1)S(1)} %get-tuple-element.48), channel_id=1, replica_groups=mesh['nodes'=32,'hid'=4] {'nodes'}, dimensions={0} | all-to-all | bytes 1048576 | tf_op jit(solution)/shard_map/all_to_all | solution.py:417
  46.2 3.2 %second.1 = (bf16[256,1024]{1,0:T(8,128)(2,1)S(1)}, f32[128,512]{1,0:T(8,128)S(1)}, f32[128,512]{1,0:T(8,128)S(1)}, bf16[128,512]{1,0:T(8,128)(2,1)S(1)}, bf16[1...) custom-call(bf16[256,512]{1,0:T(8,128)(2,1)S(1)} %get-tuple-element., ...), custom_call_target="tpu_custom_call" | custom-call | flops 1342177280 | bytes 7340032 | tf_op jit(solution)/shard_map/second/pallas_call | solution.py:350
  49.8 2.5 %collective-permute-start.5 = (bf16[128,512]{1,0:T(8,128)(2,1)S(1)}, bf16[128,512]{1,0:T(8,128)(2,1)S(1)}, u32[]{:S(2)}, u32[]{:S(2)}) collective-permute-start(bf16[128,512]{1,0:T(8,128)(2,1)S(1)} %get-tuple-element.52), channel_id=1, source_target_pairs={{0,3},{1,0},{2,1},{3,2},{4,7},{5,4},{6,5},{7,6},{8,11},{9,8},{10,9... | collective-permute-start | bytes 393224 | tf_op jit(solution)/shard_map/ppermute | solution.py:365
  53.2 3.7 %collective-permute-start.7 = (bf16[128,512]{1,0:T(8,128)(2,1)S(1)}, bf16[128,512]{1,0:T(8,128)(2,1)S(1)}, u32[]{:S(2)}, u32[]{:S(2)}) collective-permute-start(bf16[128,512]{1,0:T(8,128)(2,1)S(1)} %get-tuple-element.58), channel_id=1, source_target_pairs={{0,2},{1,3},{2,0},{3,1},{4,6},{5,7},{6,4},{7,5},{8,10},{9,11},{10,... | collective-permute-start | bytes 393224 | tf_op jit(solution)/shard_map/ppermute | solution.py:365
  57.0 2.8 %gate.1 = (f32[256,512]{1,0:T(8,128)}, bf16[256,1024]{1,0:T(8,128)(2,1)}) custom-call(bf16[256,1024]{1,0:T(8,128)(2,1)S(1)} %get-tuple-element.53.refs_0_, bf16[256,1024]{1,0:T(8,128)(2,1)S(1)} %get-tuple-element.54.refs_1_, bf16[1024,512]{1,0:T(8,128)(2,1)} %bitcast.11, bf16[128,512]{1,0:T(8,128)(2,1)S(1)} %get-tuple-element.50.refs_3_), custom_call_target="tpu_custom_call" | custom-call | flops 268435456 | bytes 3145728 | tf_op jit(solution)/shard_map/gate/pallas_call | solution.py:350
  60.5 2.8 %collective-permute-start.11 = (bf16[128,512]{1,0:T(8,128)(2,1)S(1)}, bf16[128,512]{1,0:T(8,128)(2,1)S(1)}, u32[]{:S(2)}, u32[]{:S(2)}) collective-permute-start(bf16[128,512]{1,0:T(8,128)(2,1)S(1)} %slope.2.refs_0_), channel_id=1, source_target_pairs={{0,2},{1,3},{2,0},{3,1},{4,6},{5,7},{6,4},{7,5},{8,10},{9,11},{10,... | collective-permute-start | bytes 393224 | tf_op jit(solution)/shard_map/ppermute | solution.py:365
  67.5 1.9 %collective-permute-done.9.refs_2_ = bf16[128,512]{1,0:T(8,128)(2,1)S(1)} collective-permute-done((bf16[128,512]{1,0:T(8,128)(2,1)S(1)}, bf16[128,512]{1,0:T(8,128)(2,1)S(1)}, u32[]{:S(2)}, u32[]{:S(2)}) %collective-permute-start.9) | collective-permute-done | bytes 131104 | tf_op jit(solution)/shard_map/ppermute | solution.py:365
  69.4 2.7 %collective-permute-done.14.refs_7_ = bf16[128,512]{1,0:T(8,128)(2,1)S(1)} collective-permute-done((bf16[128,512]{1,0:T(8,128)(2,1)S(1)}, bf16[128,512]{1,0:T(8,128)(2,1)S(1)}, u32[]{:S(2)}, u32[]{:S(2)}) %collective-permute-start.14) | collective-permute-done | bytes 131104 | tf_op jit(solution)/shard_map/ppermute | solution.py:365
  72.1 3.5 %collective-permute-done.10.refs_3_ = bf16[128,512]{1,0:T(8,128)(2,1)S(1)} collective-permute-done((bf16[128,512]{1,0:T(8,128)(2,1)S(1)}, bf16[128,512]{1,0:T(8,128)(2,1)S(1)}, u32[]{:S(2)}, u32[]{:S(2)}) %collective-permute-start.10) | collective-permute-done | bytes 131104 | tf_op jit(solution)/shard_map/ppermute | solution.py:365
  75.6 3.0 %spread.1 = (bf16[32,16,512]{2,1,0:T(8,128)(2,1)}, f32[256,512]{1,0:T(8,128)}, bf16[4,256,512]{2,1,0:T(8,128)(2,1)}) custom-call(bf16[128,512]{1,0:T(8,128)(2,1)S(1)} %slope.2.refs_0_, bf16[128,512]{1,0:T(8,128)(2,1)S(1)} %slope.3.refs_1_, bf16[128,512]{1,0:T(8,128)(2,1)S(1)} %collective-permute-done.9.refs_2_, ...), custom_call_target="tpu_custom_call" | custom-call | flops 1342177280 | bytes 7864320 | tf_op jit(solution)/shard_map/spread/pallas_call | solution.py:350
  78.7 1.6 %collective-permute-start.15 = (bf16[4,256,512]{2,1,0:T(8,128)(2,1)}, bf16[4,256,512]{2,1,0:T(8,128)(2,1)S(1)}, u32[]{:S(2)}, u32[]{:S(2)}) collective-permute-start(bf16[4,256,512]{2,1,0:T(8,128)(2,1)} %get-tuple-element.64.refs_0_), channel_id=1, source_target_pairs={{0,4},{4,0},{8,12},{12,8},{16,20},{20,16},{24,28},{28,24},{32,36},... | collective-permute-start | bytes 3145736 | tf_op jit(solution)/shard_map/ppermute | solution.py:373
  80.6 4.5 %all-to-all-start.2 = ((bf16[32,16,512]{2,1,0:T(8,128)(2,1)}), bf16[32,16,512]{2,1,0:T(8,128)(2,1)S(1)}, u32[]{:S(2)}, u32[]{:S(2)}) async-start(bf16[32,16,512]{2,1,0:T(8,128)(2,1)} %get-tuple-element.61), calls=%async_computation.2 | async-start | bytes 1048576 | tf_op jit(solution)/shard_map/all_to_all | solution.py:461
  85.2 4.7 %outer_second.1 = (bf16[4,64,1024]{2,1,0:T(8,128)(2,1)}, bf16[4,64,1024]{2,1,0:T(8,128)(2,1)}, bf16[4,64,1024]{2,1,0:T(8,128)(2,1)}, bf16[4,64,1024]{2,1,0:T(8,128)(2,1)}) custom-call(bf16[4,256,512]{2,1,0:T(8,128)(2,1)} %get-tuple-element.64.refs_0_, bf16[4,256,512]{2,1,0:T(8,128)(2,1)S(1)} %collective-permute-done.15.refs_1_, ...), custom_call_target="tpu_custom_call" | custom-call | flops 1610612736 | bytes 5242880 | tf_op jit(solution)/shard_map/outer_second/pallas_call | solution.py:350
  89.9 1.4 %collective-permute-start.20 = (bf16[4,64,1024]{2,1,0:T(8,128)(2,1)}, bf16[4,64,1024]{2,1,0:T(8,128)(2,1)S(1)}, u32[]{:S(2)}, u32[]{:S(2)}) collective-permute-start(bf16[4,64,1024]{2,1,0:T(8,128)(2,1)} %get-tuple-element.72), channel_id=1, source_target_pairs={{0,8},{4,36},{8,16},{12,44},{16,24},{20,52},{24,0},{28,60},{32,40}... | collective-permute-start | bytes 1572872 | tf_op jit(solution)/shard_map/ppermute | solution.py:381
  91.4 2.4 %collective-permute-start.21 = (bf16[4,64,1024]{2,1,0:T(8,128)(2,1)}, bf16[4,64,1024]{2,1,0:T(8,128)(2,1)S(1)}, u32[]{:S(2)}, u32[]{:S(2)}) collective-permute-start(bf16[4,64,1024]{2,1,0:T(8,128)(2,1)} %get-tuple-element.73), channel_id=1, source_target_pairs={{0,16},{4,68},{8,24},{12,76},{16,0},{20,84},{24,8},{28,92},{32,48}... | collective-permute-start | bytes 1572872 | tf_op jit(solution)/shard_map/ppermute | solution.py:381
  94.9 1.9 %all-to-all-done.2.refs_0_ = bf16[32,16,512]{2,1,0:T(8,128)(2,1)S(1)} async-done(((bf16[32,16,512]{2,1,0:T(8,128)(2,1)}), bf16[32,16,512]{2,1,0:T(8,128)(2,1)S(1)}, u32[]{:S(2)}, u32[]{:S(2)}) %all-to-all-start.2) | async-done | bytes 524320 | tf_op jit(solution)/shard_map/all_to_all | solution.py:461
  96.8 2.3 %settle.1 = (bf16[256,512]{1,0:T(8,128)(2,1)S(1)}, f32[256,256]{1,0:T(8,128)S(1)}, bf16[256,256]{1,0:T(8,128)(2,1)S(1)}, bf16[256,256]{1,0:T(8,128)(2,1)S(1)}, bf16[256,256]{1,0:T(8,128)(2,1)S(1)}) custom-call(bf16[32,16,512]{2,1,0:T(8,128)(2,1)S(1)} %all-to-all-done.2.refs_0_, f32[256,512]{1,0:T(8,128)} %get-tuple-element.62.refs_1_, ...), custom_call_target="tpu_custom_call" | custom-call | flops 805306368 | bytes 3801088 | tf_op jit(solution)/shard_map/settle/pallas_call | solution.py:350
  100.0 1.5 %collective-permute-start.19 = (bf16[256,256]{1,0:T(8,128)(2,1)S(1)}, bf16[256,256]{1,0:T(8,128)(2,1)S(1)}, u32[]{:S(2)}, u32[]{:S(2)}) collective-permute-start(bf16[256,256]{1,0:T(8,128)(2,1)S(1)} %get-tuple-element.70), channel_id=1, source_target_pairs={{0,3},{1,0},{2,1},{3,2},{4,7},{5,4},{6,5},{7,6},{8,11},{9,8},{10,9... | collective-permute-start | bytes 393224 | tf_op jit(solution)/shard_map/ppermute | solution.py:365
  101.5 1.5 %outer_first.1.refs_6_ = bf16[32,144,128]{2,1,0:T(8,128)(2,1)} custom-call(bf16[256,1024]{1,0:T(8,128)(2,1)S(1)} %get-tuple-element.53.refs_0_, bf16[256,512]{1,0:T(8,128)(2,1)S(1)} %get-tuple-element.71.refs_1_, bf16[256,256]{1,0:T(8,128)(2,1)S(1)} %get-tuple-element.68.refs_2_.refs_4_), custom_call_target="tpu_custom_call" | custom-call | flops 268435456 | bytes 1966080 | tf_op jit(solution)/shard_map/outer_first/pallas_call | solution.py:350
  103.0 3.5 %collective-permute-done.21.refs_2_ = bf16[4,64,1024]{2,1,0:T(8,128)(2,1)S(1)} collective-permute-done((bf16[4,64,1024]{2,1,0:T(8,128)(2,1)}, bf16[4,64,1024]{2,1,0:T(8,128)(2,1)S(1)}, u32[]{:S(2)}, u32[]{:S(2)}) %collective-permute-start.21) | collective-permute-done | bytes 524320 | tf_op jit(solution)/shard_map/ppermute | solution.py:381
  109.4 7.5 %all-to-all-start.3 = ((bf16[32,144,128]{2,1,0:T(8,128)(2,1)}), bf16[32,144,128]{2,1,0:T(8,128)(2,1)S(1)}, u32[]{:S(2)}, u32[]{:S(2)}) async-start(bf16[32,144,128]{2,1,0:T(8,128)(2,1)} %get-tuple-element.77), calls=%async_computation.3 | async-start | bytes 2359296 | tf_op jit(solution)/shard_map/all_to_all | solution.py:486
  117.0 1.5 %collective-permute-start.23 = (bf16[64,1024]{1,0:T(8,128)(2,1)S(1)}, bf16[64,1024]{1,0:T(8,128)(2,1)S(1)}, u32[]{:S(2)}, u32[]{:S(2)}) collective-permute-start(bf16[64,1024]{1,0:T(8,128)(2,1)S(1)} %get-tuple-element.79), channel_id=1, source_target_pairs={{0,32},{4,12},{8,40},{12,20},{16,48},{20,28},{24,56},{28,4},{32,64... | collective-permute-start | bytes 393224 | tf_op jit(solution)/shard_map/ppermute | solution.py:381
  118.4 2.4 %collective-permute-start.24 = (bf16[64,1024]{1,0:T(8,128)(2,1)S(1)}, bf16[64,1024]{1,0:T(8,128)(2,1)S(1)}, u32[]{:S(2)}, u32[]{:S(2)}) collective-permute-start(bf16[64,1024]{1,0:T(8,128)(2,1)S(1)} %get-tuple-element.80), channel_id=1, source_target_pairs={{0,64},{4,20},{8,72},{12,28},{16,80},{20,4},{24,88},{28,12},{32,96... | collective-permute-start | bytes 393224 | tf_op jit(solution)/shard_map/ppermute | solution.py:381
  122.0 11.1 %collective-permute-done.23.refs_1_ = bf16[64,1024]{1,0:T(8,128)(2,1)S(1)} collective-permute-done((bf16[64,1024]{1,0:T(8,128)(2,1)S(1)}, bf16[64,1024]{1,0:T(8,128)(2,1)S(1)}, u32[]{:S(2)}, u32[]{:S(2)}) %collective-permute-start.23) | collective-permute-done | bytes 131104 | tf_op jit(solution)/shard_map/ppermute | solution.py:381
  133.1 3.5 %collective-permute-done.24.refs_2_ = bf16[64,1024]{1,0:T(8,128)(2,1)S(1)} collective-permute-done((bf16[64,1024]{1,0:T(8,128)(2,1)S(1)}, bf16[64,1024]{1,0:T(8,128)(2,1)S(1)}, u32[]{:S(2)}, u32[]{:S(2)}) %collective-permute-start.24) | collective-permute-done | bytes 131104 | tf_op jit(solution)/shard_map/ppermute | solution.py:381
  (54 shorter events, 15.9 us)
Async XLA Ops:
  0.6 13.6 %copy-start.4 = (bf16[256,128]{1,0:T(8,128)(2,1)S(1)}, bf16[256,128]{1,0:T(8,128)(2,1)}, u32[]{:S(2)}) copy-start(bf16[256,128]{1,0:T(8,128)(2,1)} %refs_0_.3) | copy-start | bytes 196612
  2.7 25.6 %all-to-all-start = ((bf16[128,16,128]{2,1,0:T(8,128)(2,1)}), bf16[128,16,128]{2,1,0:T(8,128)(2,1)S(1)}, u32[]{:S(2)}, u32[]{:S(2)}) async-start(bf16[128,16,128]{2,1,0:T(8,128)(2,1)} %bitcast.2), calls=%async_computation | async-start | bytes 1048576 | tf_op jit(solution)/shard_map/all_to_all | solution.py:401
  14.2 7.9 %collective-permute-start.2 = (bf16[256,128]{1,0:T(8,128)(2,1)S(1)}, bf16[256,128]{1,0:T(8,128)(2,1)S(1)}, u32[]{:S(2)}, u32[]{:S(2)}) collective-permute-start(bf16[256,128]{1,0:T(8,128)(2,1)S(1)} %copy-done.4), channel_id=1, source_target_pairs={{0,3},{1,0},{2,1},{3,2},{4,7},{5,4},{6,5},{7,6},{8,11},{9,8},{10,9... | collective-permute-start | bytes 196616 | tf_op jit(solution)/shard_map/ppermute | solution.py:365
  16.9 8.3 %collective-permute-start.1 = (bf16[256,128]{1,0:T(8,128)(2,1)S(1)}, bf16[256,128]{1,0:T(8,128)(2,1)S(1)}, u32[]{:S(2)}, u32[]{:S(2)}) collective-permute-start(bf16[256,128]{1,0:T(8,128)(2,1)S(1)} %copy-done.4), channel_id=1, source_target_pairs={{0,2},{1,3},{2,0},{3,1},{4,6},{5,7},{6,4},{7,5},{8,10},{9,11},{10,... | collective-permute-start | bytes 196616 | tf_op jit(solution)/shard_map/ppermute | solution.py:365
  17.5 9.4 %collective-permute-start = (bf16[256,128]{1,0:T(8,128)(2,1)S(1)}, bf16[256,128]{1,0:T(8,128)(2,1)S(1)}, u32[]{:S(2)}, u32[]{:S(2)}) collective-permute-start(bf16[256,128]{1,0:T(8,128)(2,1)S(1)} %copy-done.4), channel_id=1, source_target_pairs={{0,1},{1,2},{2,3},{3,0},{4,5},{5,6},{6,7},{7,4},{8,9},{9,10},{10,1... | collective-permute-start | bytes 196616 | tf_op jit(solution)/shard_map/ppermute | solution.py:365
  49.4 10.3 %collective-permute-start.4 = (bf16[128,512]{1,0:T(8,128)(2,1)S(1)}, bf16[128,512]{1,0:T(8,128)(2,1)S(1)}, u32[]{:S(2)}, u32[]{:S(2)}) collective-permute-start(bf16[128,512]{1,0:T(8,128)(2,1)S(1)} %get-tuple-element.51), channel_id=1, source_target_pairs={{0,2},{1,3},{2,0},{3,1},{4,6},{5,7},{6,4},{7,5},{8,10},{9,11},{10,... | collective-permute-start | bytes 393224 | tf_op jit(solution)/shard_map/ppermute | solution.py:365
  49.8 10.0 %collective-permute-start.5 = (bf16[128,512]{1,0:T(8,128)(2,1)S(1)}, bf16[128,512]{1,0:T(8,128)(2,1)S(1)}, u32[]{:S(2)}, u32[]{:S(2)}) collective-permute-start(bf16[128,512]{1,0:T(8,128)(2,1)S(1)} %get-tuple-element.52), channel_id=1, source_target_pairs={{0,3},{1,0},{2,1},{3,2},{4,7},{5,4},{6,5},{7,6},{8,11},{9,8},{10,9... | collective-permute-start | bytes 393224 | tf_op jit(solution)/shard_map/ppermute | solution.py:365
  52.4 7.5 %collective-permute-start.3 = (bf16[128,512]{1,0:T(8,128)(2,1)S(1)}, bf16[128,512]{1,0:T(8,128)(2,1)S(1)}, u32[]{:S(2)}, u32[]{:S(2)}) collective-permute-start(bf16[128,512]{1,0:T(8,128)(2,1)S(1)} %get-tuple-element.50.refs_3_), channel_id=1, source_target_pairs={{0,1},{1,2},{2,3},{3,0},{4,5},{5,6},{6,7},{7,4},{8,9},{9,10},{10,1... | collective-permute-start | bytes 393224 | tf_op jit(solution)/shard_map/ppermute | solution.py:365
  53.0 10.3 %collective-permute-start.6 = (bf16[128,512]{1,0:T(8,128)(2,1)S(1)}, bf16[128,512]{1,0:T(8,128)(2,1)S(1)}, u32[]{:S(2)}, u32[]{:S(2)}) collective-permute-start(bf16[128,512]{1,0:T(8,128)(2,1)S(1)} %get-tuple-element.57), channel_id=1, source_target_pairs={{0,1},{1,2},{2,3},{3,0},{4,5},{5,6},{6,7},{7,4},{8,9},{9,10},{10,1... | collective-permute-start | bytes 393224 | tf_op jit(solution)/shard_map/ppermute | solution.py:365
  53.2 11.5 %collective-permute-start.7 = (bf16[128,512]{1,0:T(8,128)(2,1)S(1)}, bf16[128,512]{1,0:T(8,128)(2,1)S(1)}, u32[]{:S(2)}, u32[]{:S(2)}) collective-permute-start(bf16[128,512]{1,0:T(8,128)(2,1)S(1)} %get-tuple-element.58), channel_id=1, source_target_pairs={{0,2},{1,3},{2,0},{3,1},{4,6},{5,7},{6,4},{7,5},{8,10},{9,11},{10,... | collective-permute-start | bytes 393224 | tf_op jit(solution)/shard_map/ppermute | solution.py:365
  57.0 18.7 %copy-start = (bf16[2,512,2048]{2,1,0:T(8,128)(2,1)S(1)}, bf16[2,512,2048]{2,1,0:T(8,128)(2,1)}, u32[]{:S(2)}) copy-start(bf16[2,512,2048]{2,1,0:T(8,128)(2,1)} %param.14) | copy-start | bytes 12582916
  59.8 4.9 %collective-permute-start.8 = (bf16[128,512]{1,0:T(8,128)(2,1)S(1)}, bf16[128,512]{1,0:T(8,128)(2,1)S(1)}, u32[]{:S(2)}, u32[]{:S(2)}) collective-permute-start(bf16[128,512]{1,0:T(8,128)(2,1)S(1)} %get-tuple-element.59), channel_id=1, source_target_pairs={{0,3},{1,0},{2,1},{3,2},{4,7},{5,4},{6,5},{7,6},{8,11},{9,8},{10,9... | collective-permute-start | bytes 393224 | tf_op jit(solution)/shard_map/ppermute | solution.py:365
  60.0 6.7 %collective-permute-start.13 = (bf16[128,512]{1,0:T(8,128)(2,1)S(1)}, bf16[128,512]{1,0:T(8,128)(2,1)S(1)}, u32[]{:S(2)}, u32[]{:S(2)}) collective-permute-start(bf16[128,512]{1,0:T(8,128)(2,1)S(1)} %slope.2.refs_0_), channel_id=1, source_target_pairs={{0,3},{1,0},{2,1},{3,2},{4,7},{5,4},{6,5},{7,6},{8,11},{9,8},{10,9... | collective-permute-start | bytes 393224 | tf_op jit(solution)/shard_map/ppermute | solution.py:365
  60.5 6.9 %collective-permute-start.11 = (bf16[128,512]{1,0:T(8,128)(2,1)S(1)}, bf16[128,512]{1,0:T(8,128)(2,1)S(1)}, u32[]{:S(2)}, u32[]{:S(2)}) collective-permute-start(bf16[128,512]{1,0:T(8,128)(2,1)S(1)} %slope.2.refs_0_), channel_id=1, source_target_pairs={{0,2},{1,3},{2,0},{3,1},{4,6},{5,7},{6,4},{7,5},{8,10},{9,11},{10,... | collective-permute-start | bytes 393224 | tf_op jit(solution)/shard_map/ppermute | solution.py:365
  63.3 6.1 %collective-permute-start.9 = (bf16[128,512]{1,0:T(8,128)(2,1)S(1)}, bf16[128,512]{1,0:T(8,128)(2,1)S(1)}, u32[]{:S(2)}, u32[]{:S(2)}) collective-permute-start(bf16[128,512]{1,0:T(8,128)(2,1)S(1)} %slope.2.refs_0_), channel_id=1, source_target_pairs={{0,1},{1,2},{2,3},{3,0},{4,5},{5,6},{6,7},{7,4},{8,9},{9,10},{10,1... | collective-permute-start | bytes 393224 | tf_op jit(solution)/shard_map/ppermute | solution.py:365
  64.9 7.2 %collective-permute-start.14 = (bf16[128,512]{1,0:T(8,128)(2,1)S(1)}, bf16[128,512]{1,0:T(8,128)(2,1)S(1)}, u32[]{:S(2)}, u32[]{:S(2)}) collective-permute-start(bf16[128,512]{1,0:T(8,128)(2,1)S(1)} %slope.3.refs_1_), channel_id=1, source_target_pairs={{0,3},{1,0},{2,1},{3,2},{4,7},{5,4},{6,5},{7,6},{8,11},{9,8},{10,9... | collective-permute-start | bytes 393224 | tf_op jit(solution)/shard_map/ppermute | solution.py:365
  66.3 5.8 %collective-permute-start.12 = (bf16[128,512]{1,0:T(8,128)(2,1)S(1)}, bf16[128,512]{1,0:T(8,128)(2,1)S(1)}, u32[]{:S(2)}, u32[]{:S(2)}) collective-permute-start(bf16[128,512]{1,0:T(8,128)(2,1)S(1)} %slope.3.refs_1_), channel_id=1, source_target_pairs={{0,2},{1,3},{2,0},{3,1},{4,6},{5,7},{6,4},{7,5},{8,10},{9,11},{10,... | collective-permute-start | bytes 393224 | tf_op jit(solution)/shard_map/ppermute | solution.py:365
  66.7 8.9 %collective-permute-start.10 = (bf16[128,512]{1,0:T(8,128)(2,1)S(1)}, bf16[128,512]{1,0:T(8,128)(2,1)S(1)}, u32[]{:S(2)}, u32[]{:S(2)}) collective-permute-start(bf16[128,512]{1,0:T(8,128)(2,1)S(1)} %slope.3.refs_1_), channel_id=1, source_target_pairs={{0,1},{1,2},{2,3},{3,0},{4,5},{5,6},{6,7},{7,4},{8,9},{9,10},{10,1... | collective-permute-start | bytes 393224 | tf_op jit(solution)/shard_map/ppermute | solution.py:365
  78.7 6.5 %collective-permute-start.15 = (bf16[4,256,512]{2,1,0:T(8,128)(2,1)}, bf16[4,256,512]{2,1,0:T(8,128)(2,1)S(1)}, u32[]{:S(2)}, u32[]{:S(2)}) collective-permute-start(bf16[4,256,512]{2,1,0:T(8,128)(2,1)} %get-tuple-element.64.refs_0_), channel_id=1, source_target_pairs={{0,4},{4,0},{8,12},{12,8},{16,20},{20,16},{24,28},{28,24},{32,36},... | collective-permute-start | bytes 3145736 | tf_op jit(solution)/shard_map/ppermute | solution.py:373
  80.3 4.8 %collective-permute-start.16 = (bf16[256,1024]{1,0:T(8,128)(2,1)S(1)}, bf16[256,1024]{1,0:T(8,128)(2,1)}, u32[]{:S(2)}, u32[]{:S(2)}) collective-permute-start(bf16[256,1024]{1,0:T(8,128)(2,1)S(1)} %copy-done.5), channel_id=1, source_target_pairs={{0,4},{4,0},{8,12},{12,8},{16,20},{20,16},{24,28},{28,24},{32,36},... | collective-permute-start | bytes 1572872 | tf_op jit(solution)/shard_map/ppermute | solution.py:373
  80.6 16.2 %all-to-all-start.2 = ((bf16[32,16,512]{2,1,0:T(8,128)(2,1)}), bf16[32,16,512]{2,1,0:T(8,128)(2,1)S(1)}, u32[]{:S(2)}, u32[]{:S(2)}) async-start(bf16[32,16,512]{2,1,0:T(8,128)(2,1)} %get-tuple-element.61), calls=%async_computation.2 | async-start | bytes 1048576 | tf_op jit(solution)/shard_map/all_to_all | solution.py:461
  89.9 11.6 %collective-permute-start.20 = (bf16[4,64,1024]{2,1,0:T(8,128)(2,1)}, bf16[4,64,1024]{2,1,0:T(8,128)(2,1)S(1)}, u32[]{:S(2)}, u32[]{:S(2)}) collective-permute-start(bf16[4,64,1024]{2,1,0:T(8,128)(2,1)} %get-tuple-element.72), channel_id=1, source_target_pairs={{0,8},{4,36},{8,16},{12,44},{16,24},{20,52},{24,0},{28,60},{32,40}... | collective-permute-start | bytes 1572872 | tf_op jit(solution)/shard_map/ppermute | solution.py:381
  91.4 15.1 %collective-permute-start.21 = (bf16[4,64,1024]{2,1,0:T(8,128)(2,1)}, bf16[4,64,1024]{2,1,0:T(8,128)(2,1)S(1)}, u32[]{:S(2)}, u32[]{:S(2)}) collective-permute-start(bf16[4,64,1024]{2,1,0:T(8,128)(2,1)} %get-tuple-element.73), channel_id=1, source_target_pairs={{0,16},{4,68},{8,24},{12,76},{16,0},{20,84},{24,8},{28,92},{32,48}... | collective-permute-start | bytes 1572872 | tf_op jit(solution)/shard_map/ppermute | solution.py:381
  93.8 12.7 %collective-permute-start.22 = (bf16[4,64,1024]{2,1,0:T(8,128)(2,1)}, bf16[4,64,1024]{2,1,0:T(8,128)(2,1)S(1)}, u32[]{:S(2)}, u32[]{:S(2)}) collective-permute-start(bf16[4,64,1024]{2,1,0:T(8,128)(2,1)} %get-tuple-element.74), channel_id=1, source_target_pairs={{0,24},{4,100},{8,0},{12,108},{16,8},{20,116},{24,16},{28,124},{32... | collective-permute-start | bytes 1572872 | tf_op jit(solution)/shard_map/ppermute | solution.py:381
  99.1 8.7 %collective-permute-start.18 = (bf16[256,256]{1,0:T(8,128)(2,1)S(1)}, bf16[256,256]{1,0:T(8,128)(2,1)S(1)}, u32[]{:S(2)}, u32[]{:S(2)}) collective-permute-start(bf16[256,256]{1,0:T(8,128)(2,1)S(1)} %get-tuple-element.69), channel_id=1, source_target_pairs={{0,2},{1,3},{2,0},{3,1},{4,6},{5,7},{6,4},{7,5},{8,10},{9,11},{10,... | collective-permute-start | bytes 393224 | tf_op jit(solution)/shard_map/ppermute | solution.py:365
  100.0 8.0 %collective-permute-start.19 = (bf16[256,256]{1,0:T(8,128)(2,1)S(1)}, bf16[256,256]{1,0:T(8,128)(2,1)S(1)}, u32[]{:S(2)}, u32[]{:S(2)}) collective-permute-start(bf16[256,256]{1,0:T(8,128)(2,1)S(1)} %get-tuple-element.70), channel_id=1, source_target_pairs={{0,3},{1,0},{2,1},{3,2},{4,7},{5,4},{6,5},{7,6},{8,11},{9,8},{10,9... | collective-permute-start | bytes 393224 | tf_op jit(solution)/shard_map/ppermute | solution.py:365
  101.5 7.0 %collective-permute-start.17 = (bf16[256,256]{1,0:T(8,128)(2,1)S(1)}, bf16[256,256]{1,0:T(8,128)(2,1)S(1)}, u32[]{:S(2)}, u32[]{:S(2)}) collective-permute-start(bf16[256,256]{1,0:T(8,128)(2,1)S(1)} %get-tuple-element.68.refs_2_.refs_4_), channel_id=1, source_target_pairs={{0,1},{1,2},{2,3},{3,0},{4,5},{5,6},{6,7},{7,4},{8,9},{9,10},{10,1... | collective-permute-start | bytes 393224 | tf_op jit(solution)/shard_map/ppermute | solution.py:365
  109.4 28.0 %copy-start.3 = (bf16[256,512]{1,0:T(8,128)(2,1)S(1)}, bf16[256,512]{1,0:T(8,128)(2,1)}, u32[]{:S(2)}) copy-start(bf16[256,512]{1,0:T(8,128)(2,1)} %get-tuple-element.63.refs_3_.refs_1_) | copy-start | bytes 786436
  109.4 28.0 %all-to-all-start.3 = ((bf16[32,144,128]{2,1,0:T(8,128)(2,1)}), bf16[32,144,128]{2,1,0:T(8,128)(2,1)S(1)}, u32[]{:S(2)}, u32[]{:S(2)}) async-start(bf16[32,144,128]{2,1,0:T(8,128)(2,1)} %get-tuple-element.77), calls=%async_computation.3 | async-start | bytes 2359296 | tf_op jit(solution)/shard_map/all_to_all | solution.py:486
  117.0 16.2 %collective-permute-start.23 = (bf16[64,1024]{1,0:T(8,128)(2,1)S(1)}, bf16[64,1024]{1,0:T(8,128)(2,1)S(1)}, u32[]{:S(2)}, u32[]{:S(2)}) collective-permute-start(bf16[64,1024]{1,0:T(8,128)(2,1)S(1)} %get-tuple-element.79), channel_id=1, source_target_pairs={{0,32},{4,12},{8,40},{12,20},{16,48},{20,28},{24,56},{28,4},{32,64... | collective-permute-start | bytes 393224 | tf_op jit(solution)/shard_map/ppermute | solution.py:381
  118.4 18.2 %collective-permute-start.24 = (bf16[64,1024]{1,0:T(8,128)(2,1)S(1)}, bf16[64,1024]{1,0:T(8,128)(2,1)S(1)}, u32[]{:S(2)}, u32[]{:S(2)}) collective-permute-start(bf16[64,1024]{1,0:T(8,128)(2,1)S(1)} %get-tuple-element.80), channel_id=1, source_target_pairs={{0,64},{4,20},{8,72},{12,28},{16,80},{20,4},{24,88},{28,12},{32,96... | collective-permute-start | bytes 393224 | tf_op jit(solution)/shard_map/ppermute | solution.py:381
  120.8 15.8 %collective-permute-start.25 = (bf16[64,1024]{1,0:T(8,128)(2,1)S(1)}, bf16[64,1024]{1,0:T(8,128)(2,1)S(1)}, u32[]{:S(2)}, u32[]{:S(2)}) collective-permute-start(bf16[64,1024]{1,0:T(8,128)(2,1)S(1)} %get-tuple-element.81), channel_id=1, source_target_pairs={{0,96},{4,28},{8,104},{12,4},{16,112},{20,12},{24,120},{28,20},{32... | collective-permute-start | bytes 393224 | tf_op jit(solution)/shard_map/ppermute | solution.py:381
  (3 other events, 25.5 us)

commit v4 on v3

--- a/solution.py
+++ b/solution.py
@@ -17,6 +17,7 @@
 LANES = 128
 UNITS = 512
 KEPT = 80
+CHIPS = 16
 BIG = 2 * ROWS * UNITS * UNITS
 
 
@@ -57,9 +58,8 @@
 
 
 def count_kernel(
-    neigh_ref, degree_ref, routes_ref, adj_ref, adjt_ref, inv_ref, selt_ref, key_ref, low_ref, high_ref
+    neigh_ref, degree_ref, adj_ref, adjt_ref, inv_ref, key_ref, low_ref, high_ref
 ):
-    selt_ref[...] = route_rows(routes_ref).astype(BF16)
     inv_ref[...] = 1.0 / jnp.broadcast_to(degree_ref[...].astype(F32), (LANES, ROWS)).T
     entry = neigh_ref[...]
     used = lax.broadcasted_iota(jnp.int32, (KEPT, ROWS), 0) < degree_ref[...]
@@ -114,7 +114,8 @@
     send_ref[...] = mm(sel_ref[...], hidden).astype(BF16).reshape(PEERS, SLOTS, UNITS)
 
 
-def gate_kernel(both_ref, stacked_ref, w1_ref, slope_ref, saved_ref):
+def gate_kernel(both_ref, stacked_ref, w1_ref, routes_ref, slope_ref, saved_ref, selt_ref):
+    selt_ref[...] = route_rows(routes_ref).astype(BF16)
     saved_ref[...] = stacked_ref[...]
     pre = mm(both_ref[...], w1_ref[...])
     sig = 1.0 / (1.0 + jnp.exp(-pre))
@@ -126,21 +127,35 @@
     own_a, own_b, s1a, s1b, s2a, s2b, s3a, s3b, w_ref, sems,
 ):
     order = ((2, s2a, s2b), (1, s1a, s1b), (3, s3a, s3b), (0, own_a, own_b))
+    pieces, tall = 4, 2 * UNITS // 4
     copies = []
     for slot, (d, upper, lower) in enumerate(order):
         target = lax.rem(place.hid + d, HID)
         cols = pl.ds(pl.multiple_of(target * UNITS, UNITS), UNITS)
-        copies.append(pltpu.make_async_copy(w_hbm.at[:, cols], w_ref.at[slot], sems.at[slot]))
-        copies[-1].start()
+        for piece in range(pieces):
+            rows = pl.ds(piece * tall, tall)
+            copies.append(pltpu.make_async_copy(w_hbm.at[rows, cols], w_ref.at[slot, rows], sems.at[slot, piece]))
+            copies[-1].start()
     hidden = hidden_ref[...]
     total = mm(adj_ref[:, :ROWS], hidden) + mm(adj_ref[:, ROWS:], far_ref[...].reshape(FAR, UNITS))
     stacked_ref[:, :UNITS] = hidden
     stacked_ref[:, UNITS:] = (total * wide(inv_ref[...], UNITS)).astype(BF16)
     for slot, (d, upper, lower) in enumerate(order):
-        copies[slot].wait()
+        for copy in copies[slot * pieces : (slot + 1) * pieces]:
+            copy.wait()
         part = mm(stacked_ref[...], w_ref[slot]).astype(upper.dtype)
         upper[...] = part[: ROWS // 2]
         lower[...] = part[ROWS // 2 :]
+
+
+def choose_kernel(place, both_ref, mine_ref, give_ref):
+    row = lax.broadcasted_iota(jnp.int32, (UNITS, UNITS // 2), 0)
+    col = lax.broadcasted_iota(jnp.int32, (UNITS, UNITS // 2), 1)
+    for core, out in ((place.core, mine_ref), (1 - place.core, give_ref)):
+        keep = jnp.where(row == (col >> 4) * 32 + core * 16 + (col & 15), 1.0, 0.0).astype(BF16)
+        for kind in range(2):
+            cols = slice(kind * UNITS, (kind + 1) * UNITS)
+            out[:, kind * UNITS // 2 : (kind + 1) * UNITS // 2] = mm(both_ref[:, cols], keep).astype(BF16)
 
 
 def slope_kernel(first_row, count_ref, own_ref, r1, r2, r3, cot_ref, grad_ref):
@@ -184,17 +199,31 @@
         copy.wait()
 
 
-def outer_second_kernel(scale, slots, place, grads_ref, mates_ref, stacked_ref, stacked_mate_ref, *refs):
-    outs, (block_ref, sems) = refs[-6:-2], refs[-2:]
+def outer_second_kernel(slots, place, grads_hbm, mates_ref, stacked_hbm, mate_ref, *refs):
+    outs, (block_ref, grads_ref, mine_ref, load_sems, sems) = refs[:4], refs[4:]
+    loads = [pltpu.make_async_copy(grads_hbm.at[0], grads_ref.at[0], load_sems.at[0])]
+    for source, target, base in ((stacked_hbm, mine_ref, 4),):
+        for piece in range(2):
+            rows = pl.ds(piece * ROWS // 2, ROWS // 2)
+            loads.append(pltpu.make_async_copy(source.at[rows], target.at[rows], load_sems.at[base + piece]))
+    loads += [
+        pltpu.make_async_copy(grads_hbm.at[index], grads_ref.at[index], load_sems.at[index]) for index in (1, 2, 3)
+    ]
+    for load in loads:
+        load.start()
     row = lax.broadcasted_iota(jnp.int32, (UNITS, UNITS // 2), 0)
     col = lax.broadcasted_iota(jnp.int32, (UNITS, UNITS // 2), 1)
     wanted = (col >> 6) * 128 + place.core * 64 + (col & 63)
     keep = jnp.where(row == wanted, 1.0, 0.0).astype(BF16)
     for index, slot in enumerate(slots):
+        other = mm(mates_ref[index], keep).astype(BF16)
+        loads[index + 2 if index else 0].wait()
         mine = mm(grads_ref[index], keep).astype(BF16)
-        other = mm(mates_ref[index], keep).astype(BF16)
-        total = mm_first(mine, stacked_ref[...]) + mm_first(other, stacked_mate_ref[...])
-        block_ref[index] = (total * scale).astype(BF16).reshape(HID, 64, 2 * UNITS)
+        if index == 0:
+            for load in loads[1:3]:
+                load.wait()
+        total = mm_first(mine, mine_ref[...]) + mm_first(other, mate_ref[...])
+        block_ref[index] = total.astype(BF16).reshape(HID, 64, 2 * UNITS)
 
         @pl.when(place.core == 0)
         def _():
@@ -223,8 +252,9 @@
         out[...] = total.astype(out.dtype)
 
 
-def last_second_kernel(x0, x1, x2, x3, out_ref):
+def last_second_kernel(scale, x0, x1, x2, x3, out_ref):
     total = x0[...] + x1[...].astype(F32) + x2[...].astype(F32) + x3[...].astype(F32)
+    total = total * scale
     out_ref[:, 0, :] = total[:, :UNITS]
     out_ref[:, 1, :] = total[:, UNITS:]
 
@@ -244,9 +274,9 @@
             out[:, half * LANES : (half + 1) * LANES] = full_ref[:, cols].astype(out.dtype)
 
 
-def outer_first_kernel(scale, both_ref, grad_ref, out_ref):
-    product = (mm_first(both_ref[...], grad_ref[...]) * scale).astype(BF16)
-    product = product.reshape(2, PEERS, SLOTS, UNITS)
+def outer_first_kernel(grad_ref, grad_mate_ref, mine_ref, mate_ref, out_ref):
+    product = mm_first(mine_ref[...], grad_ref[...]) + mm_first(mate_ref[...], grad_mate_ref[...])
+    product = product.astype(BF16).reshape(2, CHIPS, SLOTS, UNITS)
     for part in range(HID):
         for kind in range(2):
             start = (part * 2 + kind) * SLOTS
@@ -256,23 +286,32 @@
 def return_kernel(mine_ref, r1, r2, r3, inv_ref, adjt_ref, merged_ref, base_ref, out_ref, halo_ref, sem):
     total = mine_ref[...] + r1[...].astype(F32) + r2[...].astype(F32) + r3[...].astype(F32)
     mean = (total[:, :LANES] * inv_ref[...]).astype(BF16)
-    halo_ref[...] = mm(adjt_ref[ROWS:, :], mean).astype(BF16).reshape(PEERS, SLOTS, LANES)
-    copy = pltpu.make_async_copy(halo_ref, out_ref.at[:, pl.ds(LANES, SLOTS), :], sem)
+    halo_ref[...] = mm(adjt_ref[ROWS:, :], mean).astype(BF16).reshape(CHIPS, 2 * SLOTS, LANES)
+    copy = pltpu.make_async_copy(halo_ref, out_ref.at[:, pl.ds(LANES, 2 * SLOTS), :], sem)
     copy.start()
     base_ref[...] = total[:, LANES:] + mm(adjt_ref[:ROWS, :], mean)
     copy.wait()
 
 
-def final_kernel(base_ref, selt_ref, parts_ref, feat_ref, weight_ref):
-    back = parts_ref[:, LANES:].reshape(FAR, LANES)
-    feat_ref[...] = base_ref[...] + mm(selt_ref[...], back)
+def hand_kernel(place, parts_ref, mine_ref, give_ref):
+    for core, out in ((place.core, mine_ref), (1 - place.core, give_ref)):
+        out[...] = parts_ref[:, pl.ds(pl.multiple_of(LANES + core * SLOTS, SLOTS), SLOTS), :]
+
+
+def weights_kernel(scale, parts_ref, weight_ref):
     total = parts_ref[0, :LANES].astype(F32)
-    for index in range(1, PEERS):
+    for index in range(1, CHIPS):
         total = total + parts_ref[index, :LANES].astype(F32)
     for part in range(HID):
         for kind in range(2):
             start = (part * 2 + kind) * SLOTS
-            weight_ref[:, kind, part * LANES : (part + 1) * LANES] = total[start : start + SLOTS]
+            weight_ref[:, kind, part * LANES : (part + 1) * LANES] = total[start : start + SLOTS] * scale
+
+
+def final_kernel(place, base_ref, selt_ref, mine_ref, mate_ref, feat_ref, back_ref):
+    back_ref[:, place.core] = mine_ref[...]
+    back_ref[:, 1 - place.core] = mate_ref[...]
+    feat_ref[...] = base_ref[...] + mm(selt_ref[...], back_ref[...].reshape(FAR, LANES))
 
 
 class Place:
@@ -305,12 +344,13 @@
 
 def call(
     kernel, name, operands, outs, scratch=(), placed=False, scalars=0, after=(), late=(), held=(), stored=(),
-    loose=(), aliases=None, work=1,
+    loose=(), pinned=(), aliases=None, work=1,
 ):
-    shapes = [
-        pltpu.HBM(shape, dtype) if index in (*stored, *loose) else jax.ShapeDtypeStruct(shape, dtype)
-        for index, (shape, dtype) in enumerate(outs)
-    ]
+    shapes = [jax.ShapeDtypeStruct(shape, dtype) for shape, dtype in outs]
+    for index in (*stored, *loose):
+        shapes[index] = pltpu.HBM(*outs[index])
+    for index in pinned:
+        shapes[index] = pltpu.VMEM(*outs[index])
     operands = [in_hbm(o) if index in (*late, *held) else o for index, o in enumerate(operands)]
     count = len(operands)
     in_specs = [
@@ -402,12 +442,10 @@
         send_feat.reshape(PEERS * HID, SLOTS, LANES), ("nodes", "hid"), 0, 0, tiled=True
     ).reshape(PEERS, HID, SLOTS, LANES)
     f2, f1, f3 = around([(2, features), (1, features), (3, features)])
-    adj, adjt, inv, selt = call(
-        count_kernel, "count", (jnp.swapaxes(neighbors, 0, 1), degree.reshape(1, ROWS), routes),
-        [
-            ((ROWS, ROWS + FAR), BF16), ((ROWS + FAR, ROWS), BF16), ((ROWS, LANES), F32), ((ROWS, FAR), BF16),
-        ],
-        scratch=[pltpu.VMEM((KEPT, ROWS), jnp.int32)] * 3, late=(2, 1, 0), stored=(3,), work=8, after=(sel,),
+    adj, adjt, inv = call(
+        count_kernel, "count", (jnp.swapaxes(neighbors, 0, 1), degree.reshape(1, ROWS)),
+        [((ROWS, ROWS + FAR), BF16), ((ROWS + FAR, ROWS), BF16), ((ROWS, LANES), F32)],
+        scratch=[pltpu.VMEM((KEPT, ROWS), jnp.int32)] * 3, late=(1, 0), work=8, after=(sel,),
     )
     both, hidden, send_hidden = call(
         first_kernel, "first", (features, f1, f2, f3, far_feat, adj, inv, w1, sel),
@@ -419,14 +457,15 @@
     stacked, own_a, own_b, s1a, s1b, s2a, s2b, s3a, s3b = call(
         second_kernel, "second", (hidden, far_hidden, adj, inv, w2),
         [((ROWS, 2 * UNITS), BF16)] + [((ROWS // 2, UNITS), F32)] * 2 + [half_chunk] * 6,
-        scratch=[pltpu.VMEM((HID, 2 * UNITS, UNITS), BF16), pltpu.SemaphoreType.DMA((HID,))],
+        scratch=[pltpu.VMEM((HID, 2 * UNITS, UNITS), BF16), pltpu.SemaphoreType.DMA((HID, 4))],
         placed=True, work=10, held=(4,),
     )
     r2a, r1a, r3a = around([(2, s2a), (1, s1a), (3, s3a)])
     r2b, r1b, r3b = around([(2, s2b), (1, s1b), (3, s3b)])
-    slope, saved = call(
-        gate_kernel, "gate", (both, stacked, w1), [wide_chunk, ((ROWS, 2 * UNITS), BF16)],
-        after=(s1a,), late=(2,), stored=(0, 1), work=2,
+    slope, saved, selt = call(
+        gate_kernel, "gate", (both, stacked, w1, routes),
+        [wide_chunk, ((ROWS, 2 * UNITS), BF16), ((ROWS, FAR), BF16)],
+        after=(s1a,), late=(2, 3), stored=(0, 1, 2), work=2,
     )
     saved_mate = swap(saved)
     def gradient(first_row, own, parts):
@@ -440,26 +479,27 @@
     g0b = gradient(ROWS // 2, own_b, (r1b, r2b, r3b))
     g2b, g1b, g3b = around([(2, g0b), (1, g0b), (3, g0b)])
 
-    def outer(slots, grads, held, late):
-        return tuple(call(
-            lambda *refs: outer_second_kernel(scale, slots, *refs), "outer_second",
-            (grads, swap(grads), saved, saved_mate, *held),
-            [((HID, 64, 2 * UNITS), BF16)] * HID,
-            scratch=[
-                pltpu.VMEM((len(slots), HID, 64, 2 * UNITS), BF16),
-                pltpu.SemaphoreType.DMA((len(slots), HID)),
-            ],
-            placed=True, loose=tuple(range(HID)), late=late,
-            aliases={4 + index: index for index in range(HID)} if held else None, work=3 * len(slots),
-        ))
-
+    mine_rows, give_rows = call(
+        choose_kernel, "choose", (both,), [chunk, chunk], placed=True, stored=(0, 1), work=4, after=(g0b,),
+    )
+    mate_rows = swap(give_rows)
     halo_hidden, own_hidden, others = call(
         spread_kernel, "spread", (g0a, g0b, g1a, g1b, g2a, g2b, g3a, g3b, w2, inv, adjt),
-        [halo, wide_chunk, ((HID, ROWS, UNITS), BF16)], placed=True, work=10, loose=(1, 2),
+        [halo, wide_chunk, ((HID, ROWS, UNITS), BF16)], placed=True, work=10, loose=(1, 2), after=(in_hbm(mine_rows),),
         scratch=[pltpu.VMEM((ROWS, UNITS), F32), pltpu.SemaphoreType.DMA((9,))],
     )
     back_hidden = lax.all_to_all(halo_hidden, "nodes", 0, 0, tiled=True)
-    z0, z1, z2, z3 = outer((0, 1, 2, 3), others, (), (0, 2, 3))
+    slots = (0, 1, 2, 3)
+    z0, z1, z2, z3 = call(
+        lambda *refs: outer_second_kernel(slots, *refs), "outer_second",
+        (others, swap(others), saved, saved_mate), [((HID, 64, 2 * UNITS), BF16)] * HID,
+        scratch=[
+            pltpu.VMEM((HID, HID, 64, 2 * UNITS), BF16), pltpu.VMEM((HID, ROWS, UNITS), BF16),
+            pltpu.VMEM((ROWS, 2 * UNITS), BF16), pltpu.SemaphoreType.DMA((8,)),
+            pltpu.SemaphoreType.DMA((HID, HID)),
+        ],
+        placed=True, loose=slots, held=(0, 2), work=12,
+    )
     outer_done = in_hbm(z0)
     z2, z1, z3 = near([(2, z2), (1, z1), (3, z3)], False)
     grad, mine, s1, s2, s3 = call(
@@ -470,8 +510,8 @@
     )
     r2, r1, r3 = around([(2, s2), (1, s1), (3, s3)])
     merged = call(
-        lambda *refs: outer_first_kernel(scale, *refs), "outer_first", (both, grad),
-        [((PEERS, LANES + SLOTS, LANES), BF16)], after=(s1,), stored=(0,), work=2,
+        outer_first_kernel, "outer_first", (grad, swap(grad), mine_rows, mate_rows),
+        [((CHIPS, LANES + 2 * SLOTS, LANES), BF16)], after=(s1,), late=(2,), stored=(0,), work=2,
     )
     x0, x1, x2, x3 = call(
         along_kernel, "along", (z0, z1, z2, z3),
@@ -479,17 +519,27 @@
     )
     base, merged = call(
         return_kernel, "return", (mine, r1, r2, r3, inv, adjt, merged),
-        [((ROWS, LANES), F32), ((PEERS, LANES + SLOTS, LANES), BF16)],
-        scratch=[pltpu.VMEM((PEERS, SLOTS, LANES), BF16), pltpu.SemaphoreType.DMA],
+        [((ROWS, LANES), F32), ((CHIPS, LANES + 2 * SLOTS, LANES), BF16)],
+        scratch=[pltpu.VMEM((CHIPS, 2 * SLOTS, LANES), BF16), pltpu.SemaphoreType.DMA],
         loose=(1,), aliases={6: 1}, after=(x0,),
     )
-    parts = lax.all_to_all(merged, "nodes", 0, 0, tiled=True)
+    same_core = [[2 * chip + core for chip in range(CHIPS)] for core in range(2)]
+    parts = lax.all_to_all(merged, "nodes", 0, 0, tiled=True, axis_index_groups=same_core)
+    block = ((CHIPS, SLOTS, LANES), BF16)
+    mine_back, give_back = call(hand_kernel, "hand", (parts,), [block, block], placed=True)
+    mate_back = swap(give_back)
     x2, x1, x3 = near([(2, x2), (1, x1), (3, x3)], True)
-    grad_features, grad_w_first = call(
-        final_kernel, "final", (base, selt, parts),
-        [((ROWS, LANES), F32), ((SLOTS, 2, UNITS), F32)],
-    )
-    grad_w_second = call(last_second_kernel, "last_second", (x0, x1, x2, x3), [((64, 2, UNITS), F32)])
+    grad_w_first = call(
+        lambda *refs: weights_kernel(scale, *refs), "weights", (parts,), [((SLOTS, 2, UNITS), F32)],
+        after=(give_back,),
+    )
+    grad_features = call(
+        final_kernel, "final", (base, selt, mine_back, mate_back), [((ROWS, LANES), F32)],
+        placed=True, scratch=[pltpu.VMEM((CHIPS, 2, SLOTS, LANES), BF16)],
+    )
+    grad_w_second = call(
+        lambda *refs: last_second_kernel(scale, *refs), "last_second", (x0, x1, x2, x3), [((64, 2, UNITS), F32)],
+    )
     return grad_w_first, grad_w_second, grad_features
 
 

time: 139 us -> 134 us (0.964)
  waiting for transfers between devices: 36.4 us -> 24.9 us
  starting transfers between devices: 54.6 us -> 57.7 us
  Pallas kernels: 29 us -> 31.1 us
    ppermute x6, waiting for transfers between devices: 18.1 us -> 2.28 us  [near(): lax.ppermute(v, 'nodes', [(node_at(x, z, c), target(x, z, c, d)) for x in...]
    all_to_all x1, waiting for transfers between devices: 0.01 us -> 5.76 us  [on_device(): lax.all_to_all(merged, 'nodes', 0, 0, tiled=True, axis_index_groups=same_...]
    ppermute x2 -> x5, starting transfers between devices: 1.93 us -> 6.55 us  [swap(): return lax.ppermute(value, 'nodes', [(i, i ^ 1) for i in range(PEERS)])]
    pallas_call x15 -> x18, Pallas kernels: 29 us -> 31.1 us  [call(): pl.pallas_call(body, out_shape=shapes, in_specs=in_specs, out_specs=out_s...]
    all_to_all x1, starting transfers between devices: 7.52 us -> 5.85 us  [on_device(): lax.all_to_all(merged, 'nodes', 0, 0, tiled=True, axis_index_groups=same_...]
    all_to_all x1, waiting for transfers between devices: 1.86 us -> 0.46 us  [on_device(): back_hidden = lax.all_to_all(halo_hidden, 'nodes', 0, 0, tiled=True)]
  transfers between devices with their start and end apart: 29 -> 32, of which waited for: 13 -> 14; matrix products, arithmetic and copies ran while one was open for 0% -> 0% of each run, Pallas kernels for 13% -> 15%
where the time goes in v4:
time: 134 us; the launch traced here: 133 us
  starting transfers between devices  57.7 us (43%)
  Pallas kernels  31.1 us (23%)
  waiting for transfers between devices  24.9 us (19%)
  blocking collectives  16.9 us (13%)
  between operations  1.6 us (1%)
    pallas_call x18, Pallas kernels, call(): pl.pallas_call(body, out_shape=shapes, in_specs=in_specs, out_specs=out_s...  31.1 us
    ppermute x18, starting transfers between devices, around(): lax.ppermute(v, 'hid', [(i, (i + d) % HID) for i in range(HID)])  19 us
    all_to_all x1, blocking collectives, on_device(): far_hidden = lax.all_to_all(send_hidden, 'nodes', 0, 0, tiled=True)  16.9 us
    ppermute x18, waiting for transfers between devices, around(): lax.ppermute(v, 'hid', [(i, (i + d) % HID) for i in range(HID)])  14.1 us
    all_to_all x1, starting transfers between devices, on_device(): lax.all_to_all(send_feat.reshape(PEERS * HID, SLOTS, LANES), ('nodes', 'h...  11.5 us
    ppermute x6, starting transfers between devices, near(): lax.ppermute(v, 'nodes', [(node_at(x, z, c), target(x, z, c, d)) for x in...  9.99 us
    ppermute x5, starting transfers between devices, swap(): return lax.ppermute(value, 'nodes', [(i, i ^ 1) for i in range(PEERS)])  6.55 us
    all_to_all x1, starting transfers between devices, on_device(): lax.all_to_all(merged, 'nodes', 0, 0, tiled=True, axis_index_groups=same_...  5.85 us
  transfers between devices with their start and end apart: 32, of which 14 were waited for; matrix products, arithmetic and copies ran while one was open for 0% of the time, Pallas kernels for 15%

profile of v4, /device:TPU:1, one launch (start us, length us, event | category | flops | bytes accessed | tf_op | source)
XLA Modules:
  0.0 132.9 jit_solution(17754970542812622172)
XLA Ops:
  0.7 2.1 %pick.1 = (bf16[512,256]{1,0:T(8,128)(2,1)S(1)}, bf16[32,4,16,128]{3,2,1,0:T(8,128)(2,1)}) custom-call(s32[16,32]{1,0:T(8,128)} %bitcast.15, bf16[256,128]{1,0:T(8,128)(2,1)} %refs_0_.3), custom_call_target="tpu_custom_call" | custom-call | flops 134217728 | bytes 854016 | tf_op jit(solution)/shard_map/pick/pallas_call | solution.py:390
  2.8 11.5 %all-to-all-start = ((bf16[128,16,128]{2,1,0:T(8,128)(2,1)}), bf16[128,16,128]{2,1,0:T(8,128)(2,1)S(1)}, u32[]{:S(2)}, u32[]{:S(2)}) async-start(bf16[128,16,128]{2,1,0:T(8,128)(2,1)} %bitcast.2), calls=%async_computation | async-start | bytes 1048576 | tf_op jit(solution)/shard_map/all_to_all | solution.py:441
  14.3 2.7 %collective-permute-start.2 = (bf16[256,128]{1,0:T(8,128)(2,1)}, bf16[256,128]{1,0:T(8,128)(2,1)S(1)}, u32[]{:S(2)}, u32[]{:S(2)}) collective-permute-start(bf16[256,128]{1,0:T(8,128)(2,1)} %refs_0_.3), channel_id=1, source_target_pairs={{0,3},{1,0},{2,1},{3,2},{4,7},{5,4},{6,5},{7,6},{8,11},{9,8},{10,9... | collective-permute-start | bytes 196616 | tf_op jit(solution)/shard_map/ppermute | solution.py:405
  18.1 3.2 %count.1 = (bf16[256,768]{1,0:T(8,128)(2,1)S(1)}, bf16[768,256]{1,0:T(8,128)(2,1)S(1)}, f32[256,128]{1,0:T(8,128)S(1)}) custom-call(s32[80,256]{1,0:T(8,128)} %bitcast.17, s32[1,256]{1,0:T(1,128)} %bitcast.18, bf16[512,256]{1,0:T(8,128)(2,1)S(1)} %get-tuple-element.46.refs_2_.refs_8_), custom_call_target="tpu_custom_call" | custom-call | flops 1073741824 | bytes 1000448 | tf_op jit(solution)/shard_map/count/pallas_call | solution.py:390
  21.4 4.1 %collective-permute-done.1.refs_2_ = bf16[256,128]{1,0:T(8,128)(2,1)S(1)} collective-permute-done((bf16[256,128]{1,0:T(8,128)(2,1)}, bf16[256,128]{1,0:T(8,128)(2,1)S(1)}, u32[]{:S(2)}, u32[]{:S(2)}) %collective-permute-start.1) | collective-permute-done | bytes 65568 | tf_op jit(solution)/shard_map/ppermute | solution.py:405
  25.5 1.4 %collective-permute-done.refs_1_ = bf16[256,128]{1,0:T(8,128)(2,1)S(1)} collective-permute-done((bf16[256,128]{1,0:T(8,128)(2,1)}, bf16[256,128]{1,0:T(8,128)(2,1)S(1)}, u32[]{:S(2)}, u32[]{:S(2)}) %collective-permute-start) | collective-permute-done | bytes 65568 | tf_op jit(solution)/shard_map/ppermute | solution.py:405
  26.9 1.5 %all-to-all-done = bf16[128,16,128]{2,1,0:T(8,128)(2,1)S(1)} async-done(((bf16[128,16,128]{2,1,0:T(8,128)(2,1)}), bf16[128,16,128]{2,1,0:T(8,128)(2,1)S(1)}, u32[]{:S(2)}, u32[]{:S(2)}) %all-to-all-start) | async-done | bytes 524320 | tf_op jit(solution)/shard_map/all_to_all | solution.py:441
  29.5 16.9 %all_to_all.20.refs_1_ = bf16[32,16,512]{2,1,0:T(8,128)(2,1)S(1)} all-to-all(bf16[32,16,512]{2,1,0:T(8,128)(2,1)S(1)} %get-tuple-element.50), channel_id=1, replica_groups=mesh['nodes'=32,'hid'=4] {'nodes'}, dimensions={0} | all-to-all | bytes 1048576 | tf_op jit(solution)/shard_map/all_to_all | solution.py:455
  46.5 3.3 %second.1 = (bf16[256,1024]{1,0:T(8,128)(2,1)S(1)}, f32[128,512]{1,0:T(8,128)S(1)}, f32[128,512]{1,0:T(8,128)S(1)}, bf16[128,512]{1,0:T(8,128)(2,1)S(1)}, bf16[1...) custom-call(bf16[256,512]{1,0:T(8,128)(2,1)S(1)} %get-tuple-element., ...), custom_call_target="tpu_custom_call" | custom-call | flops 1342177280 | bytes 7340032 | tf_op jit(solution)/shard_map/second/pallas_call | solution.py:390
  50.2 2.5 %collective-permute-start.5 = (bf16[128,512]{1,0:T(8,128)(2,1)S(1)}, bf16[128,512]{1,0:T(8,128)(2,1)S(1)}, u32[]{:S(2)}, u32[]{:S(2)}) collective-permute-start(bf16[128,512]{1,0:T(8,128)(2,1)S(1)} %get-tuple-element.54), channel_id=1, source_target_pairs={{0,3},{1,0},{2,1},{3,2},{4,7},{5,4},{6,5},{7,6},{8,11},{9,8},{10,9... | collective-permute-start | bytes 393224 | tf_op jit(solution)/shard_map/ppermute | solution.py:405
  53.5 3.7 %collective-permute-start.7 = (bf16[128,512]{1,0:T(8,128)(2,1)S(1)}, bf16[128,512]{1,0:T(8,128)(2,1)S(1)}, u32[]{:S(2)}, u32[]{:S(2)}) collective-permute-start(bf16[128,512]{1,0:T(8,128)(2,1)S(1)} %get-tuple-element.60), channel_id=1, source_target_pairs={{0,2},{1,3},{2,0},{3,1},{4,6},{5,7},{6,4},{7,5},{8,10},{9,11},{10,... | collective-permute-start | bytes 393224 | tf_op jit(solution)/shard_map/ppermute | solution.py:405
  57.3 2.7 %gate.1 = (f32[256,512]{1,0:T(8,128)}, bf16[256,1024]{1,0:T(8,128)(2,1)}, bf16[256,512]{1,0:T(8,128)(2,1)}) custom-call(bf16[256,1024]{1,0:T(8,128)(2,1)S(1)} %get-tuple-element.55.refs_0_, bf16[256,1024]{1,0:T(8,128)(2,1)S(1)} %get-tuple-element.56.refs_1_, bf16[1024,512]{1,0:T(8,128)(2,1)} %bitcast.11, s32[16,32]{1,0:T(8,128)} %bitcast.16, ...), custom_call_target="tpu_custom_call" | custom-call | flops 268435456 | bytes 3409920 | tf_op jit(solution)/shard_map/gate/pallas_call | solution.py:390
  60.9 2.7 %collective-permute-start.11 = (bf16[128,512]{1,0:T(8,128)(2,1)S(1)}, bf16[128,512]{1,0:T(8,128)(2,1)S(1)}, u32[]{:S(2)}, u32[]{:S(2)}) collective-permute-start(bf16[128,512]{1,0:T(8,128)(2,1)S(1)} %slope.2.refs_0_), channel_id=1, source_target_pairs={{0,2},{1,3},{2,0},{3,1},{4,6},{5,7},{6,4},{7,5},{8,10},{9,11},{10,... | collective-permute-start | bytes 393224 | tf_op jit(solution)/shard_map/ppermute | solution.py:405
  63.5 1.5 %collective-permute-done.7.refs_3_ = bf16[128,512]{1,0:T(8,128)(2,1)S(1)} collective-permute-done((bf16[128,512]{1,0:T(8,128)(2,1)S(1)}, bf16[128,512]{1,0:T(8,128)(2,1)S(1)}, u32[]{:S(2)}, u32[]{:S(2)}) %collective-permute-start.7) | collective-permute-done | bytes 131104 | tf_op jit(solution)/shard_map/ppermute | solution.py:405
  69.6 2.6 %collective-permute-done.14.refs_7_ = bf16[128,512]{1,0:T(8,128)(2,1)S(1)} collective-permute-done((bf16[128,512]{1,0:T(8,128)(2,1)S(1)}, bf16[128,512]{1,0:T(8,128)(2,1)S(1)}, u32[]{:S(2)}, u32[]{:S(2)}) %collective-permute-start.14) | collective-permute-done | bytes 131104 | tf_op jit(solution)/shard_map/ppermute | solution.py:405
  72.2 3.5 %collective-permute-done.10.refs_3_ = bf16[128,512]{1,0:T(8,128)(2,1)S(1)} collective-permute-done((bf16[128,512]{1,0:T(8,128)(2,1)S(1)}, bf16[128,512]{1,0:T(8,128)(2,1)S(1)}, u32[]{:S(2)}, u32[]{:S(2)}) %collective-permute-start.10) | collective-permute-done | bytes 131104 | tf_op jit(solution)/shard_map/ppermute | solution.py:405
  75.8 3.0 %spread.1 = (bf16[32,16,512]{2,1,0:T(8,128)(2,1)}, f32[256,512]{1,0:T(8,128)}, bf16[4,256,512]{2,1,0:T(8,128)(2,1)}) custom-call(bf16[128,512]{1,0:T(8,128)(2,1)S(1)} %slope.2.refs_0_, bf16[128,512]{1,0:T(8,128)(2,1)S(1)} %slope.3.refs_1_, bf16[128,512]{1,0:T(8,128)(2,1)S(1)} %collective-permute-done.9.refs_2_, ...), custom_call_target="tpu_custom_call" | custom-call | flops 1342177280 | bytes 7864320 | tf_op jit(solution)/shard_map/spread/pallas_call | solution.py:390
  78.8 1.8 %collective-permute-start.15 = (bf16[4,256,512]{2,1,0:T(8,128)(2,1)}, bf16[4,256,512]{2,1,0:T(8,128)(2,1)S(1)}, u32[]{:S(2)}, u32[]{:S(2)}) collective-permute-start(bf16[4,256,512]{2,1,0:T(8,128)(2,1)} %get-tuple-element.67.refs_0_), channel_id=1, source_target_pairs={{0,4},{4,0},{8,12},{12,8},{16,20},{20,16},{24,28},{28,24},{32,36},... | collective-permute-start | bytes 3145736 | tf_op jit(solution)/shard_map/ppermute | solution.py:413
  80.8 4.9 %all-to-all-start.2 = ((bf16[32,16,512]{2,1,0:T(8,128)(2,1)}), bf16[32,16,512]{2,1,0:T(8,128)(2,1)S(1)}, u32[]{:S(2)}, u32[]{:S(2)}) async-start(bf16[32,16,512]{2,1,0:T(8,128)(2,1)} %get-tuple-element.64), calls=%async_computation.2 | async-start | bytes 1048576 | tf_op jit(solution)/shard_map/all_to_all | solution.py:491
  85.7 4.9 %outer_second.1 = (bf16[4,64,1024]{2,1,0:T(8,128)(2,1)}, bf16[4,64,1024]{2,1,0:T(8,128)(2,1)}, bf16[4,64,1024]{2,1,0:T(8,128)(2,1)}, bf16[4,64,1024]{2,1,0:T(8,128)(2,1)}) custom-call(bf16[4,256,512]{2,1,0:T(8,128)(2,1)} %get-tuple-element.67.refs_0_, bf16[4,256,512]{2,1,0:T(8,128)(2,1)S(1)} %collective-permute-done.15.refs_1_, ...), custom_call_target="tpu_custom_call" | custom-call | flops 1610612736 | bytes 5242880 | tf_op jit(solution)/shard_map/outer_second/pallas_call | solution.py:390
  90.6 1.5 %collective-permute-start.22 = (bf16[4,64,1024]{2,1,0:T(8,128)(2,1)}, bf16[4,64,1024]{2,1,0:T(8,128)(2,1)S(1)}, u32[]{:S(2)}, u32[]{:S(2)}) collective-permute-start(bf16[4,64,1024]{2,1,0:T(8,128)(2,1)} %get-tuple-element.76), channel_id=1, source_target_pairs={{0,8},{4,36},{8,16},{12,44},{16,24},{20,52},{24,0},{28,60},{32,40}... | collective-permute-start | bytes 1572872 | tf_op jit(solution)/shard_map/ppermute | solution.py:421
  92.0 2.4 %collective-permute-start.23 = (bf16[4,64,1024]{2,1,0:T(8,128)(2,1)}, bf16[4,64,1024]{2,1,0:T(8,128)(2,1)S(1)}, u32[]{:S(2)}, u32[]{:S(2)}) collective-permute-start(bf16[4,64,1024]{2,1,0:T(8,128)(2,1)} %get-tuple-element.77), channel_id=1, source_target_pairs={{0,16},{4,68},{8,24},{12,76},{16,0},{20,84},{24,8},{28,92},{32,48}... | collective-permute-start | bytes 1572872 | tf_op jit(solution)/shard_map/ppermute | solution.py:421
  97.3 2.3 %settle.1 = (bf16[256,512]{1,0:T(8,128)(2,1)S(1)}, f32[256,256]{1,0:T(8,128)S(1)}, bf16[256,256]{1,0:T(8,128)(2,1)S(1)}, bf16[256,256]{1,0:T(8,128)(2,1)S(1)}, bf16[256,256]{1,0:T(8,128)(2,1)S(1)}) custom-call(bf16[32,16,512]{2,1,0:T(8,128)(2,1)S(1)} %all-to-all-done.2.refs_0_, f32[256,512]{1,0:T(8,128)} %get-tuple-element.65.refs_1_, ...), custom_call_target="tpu_custom_call" | custom-call | flops 805306368 | bytes 3801088 | tf_op jit(solution)/shard_map/settle/pallas_call | solution.py:390
  101.2 1.4 %collective-permute-start.19 = (bf16[256,256]{1,0:T(8,128)(2,1)S(1)}, bf16[256,256]{1,0:T(8,128)(2,1)S(1)}, u32[]{:S(2)}, u32[]{:S(2)}) collective-permute-start(bf16[256,256]{1,0:T(8,128)(2,1)S(1)} %get-tuple-element.73), channel_id=1, source_target_pairs={{0,3},{1,0},{2,1},{3,2},{4,7},{5,4},{6,5},{7,6},{8,11},{9,8},{10,9... | collective-permute-start | bytes 393224 | tf_op jit(solution)/shard_map/ppermute | solution.py:405
  102.7 2.3 %outer_first.1.refs_6_ = bf16[16,160,128]{2,1,0:T(8,128)(2,1)} custom-call(bf16[256,512]{1,0:T(8,128)(2,1)S(1)} %get-tuple-element.74.refs_0_, bf16[256,512]{1,0:T(8,128)(2,1)S(1)} %collective-permute-done.20.refs_1_, bf16[256,512]{1,0:T(8,128)(2,1)} %get-tuple-element.63.refs_11_.refs_2_, bf16[256,512]{1,0:T(8,128)(2,1)S(1)} %collective-permute-done.21.refs_3_, ...), custom_call_target="tpu_custom_call" | custom-call | flops 268435456 | bytes 1703936 | tf_op jit(solution)/shard_map/outer_first/pallas_call | solution.py:390
  105.0 2.2 %collective-permute-done.23.refs_2_ = bf16[4,64,1024]{2,1,0:T(8,128)(2,1)S(1)} collective-permute-done((bf16[4,64,1024]{2,1,0:T(8,128)(2,1)}, bf16[4,64,1024]{2,1,0:T(8,128)(2,1)S(1)}, u32[]{:S(2)}, u32[]{:S(2)}) %collective-permute-start.23) | collective-permute-done | bytes 524320 | tf_op jit(solution)/shard_map/ppermute | solution.py:421
  107.2 1.3 along.1
  110.4 5.9 %all-to-all-start.3 = ((bf16[16,160,128]{2,1,0:T(8,128)(2,1)}), bf16[16,160,128]{2,1,0:T(8,128)(2,1)S(1)}, u32[]{:S(2)}, u32[]{:S(2)}) async-start(bf16[16,160,128]{2,1,0:T(8,128)(2,1)} %get-tuple-element.80), calls=%async_computation.3 | async-start | bytes 1310720 | tf_op jit(solution)/shard_map/all_to_all | solution.py:527
  116.3 1.4 %collective-permute-start.25 = (bf16[64,1024]{1,0:T(8,128)(2,1)}, bf16[64,1024]{1,0:T(8,128)(2,1)S(1)}, u32[]{:S(2)}, u32[]{:S(2)}) collective-permute-start(bf16[64,1024]{1,0:T(8,128)(2,1)} %copy-done.5), channel_id=1, source_target_pairs={{0,32},{4,12},{8,40},{12,20},{16,48},{20,28},{24,56},{28,4},{32,64... | collective-permute-start | bytes 393224 | tf_op jit(solution)/shard_map/ppermute | solution.py:421
  117.7 2.4 %collective-permute-start.26 = (bf16[64,1024]{1,0:T(8,128)(2,1)}, bf16[64,1024]{1,0:T(8,128)(2,1)S(1)}, u32[]{:S(2)}, u32[]{:S(2)}) collective-permute-start(bf16[64,1024]{1,0:T(8,128)(2,1)} %copy-done.4), channel_id=1, source_target_pairs={{0,64},{4,20},{8,72},{12,28},{16,80},{20,4},{24,88},{28,12},{32,96... | collective-permute-start | bytes 393224 | tf_op jit(solution)/shard_map/ppermute | solution.py:421
  121.2 5.8 %all-to-all-done.3.refs_0_ = bf16[16,160,128]{2,1,0:T(8,128)(2,1)S(1)} async-done(((bf16[16,160,128]{2,1,0:T(8,128)(2,1)}), bf16[16,160,128]{2,1,0:T(8,128)(2,1)S(1)}, u32[]{:S(2)}, u32[]{:S(2)}) %all-to-all-start.3) | async-done | bytes 655392 | tf_op jit(solution)/shard_map/all_to_all | solution.py:527
  127.0 3.3 %collective-permute-start.28 = (bf16[16,16,128]{2,1,0:T(8,128)(2,1)S(1)}, bf16[16,16,128]{2,1,0:T(8,128)(2,1)S(1)}, u32[]{:S(2)}, u32[]{:S(2)}) collective-permute-start(bf16[16,16,128]{2,1,0:T(8,128)(2,1)S(1)} %get-tuple-element.81.refs_1_), channel_id=1, source_target_pairs={{0,4},{4,0},{8,12},{12,8},{16,20},{20,16},{24,28},{28,24},{32,36},... | collective-permute-start | bytes 196616 | tf_op jit(solution)/shard_map/ppermute | solution.py:413
  (69 shorter events, 18.7 us)
Async XLA Ops:
  2.8 25.7 %all-to-all-start = ((bf16[128,16,128]{2,1,0:T(8,128)(2,1)}), bf16[128,16,128]{2,1,0:T(8,128)(2,1)S(1)}, u32[]{:S(2)}, u32[]{:S(2)}) async-start(bf16[128,16,128]{2,1,0:T(8,128)(2,1)} %bitcast.2), calls=%async_computation | async-start | bytes 1048576 | tf_op jit(solution)/shard_map/all_to_all | solution.py:441
  14.3 7.2 %collective-permute-start.2 = (bf16[256,128]{1,0:T(8,128)(2,1)}, bf16[256,128]{1,0:T(8,128)(2,1)S(1)}, u32[]{:S(2)}, u32[]{:S(2)}) collective-permute-start(bf16[256,128]{1,0:T(8,128)(2,1)} %refs_0_.3), channel_id=1, source_target_pairs={{0,3},{1,0},{2,1},{3,2},{4,7},{5,4},{6,5},{7,6},{8,11},{9,8},{10,9... | collective-permute-start | bytes 196616 | tf_op jit(solution)/shard_map/ppermute | solution.py:405
  17.0 8.5 %collective-permute-start.1 = (bf16[256,128]{1,0:T(8,128)(2,1)}, bf16[256,128]{1,0:T(8,128)(2,1)S(1)}, u32[]{:S(2)}, u32[]{:S(2)}) collective-permute-start(bf16[256,128]{1,0:T(8,128)(2,1)} %refs_0_.3), channel_id=1, source_target_pairs={{0,2},{1,3},{2,0},{3,1},{4,6},{5,7},{6,4},{7,5},{8,10},{9,11},{10,... | collective-permute-start | bytes 196616 | tf_op jit(solution)/shard_map/ppermute | solution.py:405
  17.5 9.4 %collective-permute-start = (bf16[256,128]{1,0:T(8,128)(2,1)}, bf16[256,128]{1,0:T(8,128)(2,1)S(1)}, u32[]{:S(2)}, u32[]{:S(2)}) collective-permute-start(bf16[256,128]{1,0:T(8,128)(2,1)} %refs_0_.3), channel_id=1, source_target_pairs={{0,1},{1,2},{2,3},{3,0},{4,5},{5,6},{6,7},{7,4},{8,9},{9,10},{10,1... | collective-permute-start | bytes 196616 | tf_op jit(solution)/shard_map/ppermute | solution.py:405
  49.7 10.2 %collective-permute-start.4 = (bf16[128,512]{1,0:T(8,128)(2,1)S(1)}, bf16[128,512]{1,0:T(8,128)(2,1)S(1)}, u32[]{:S(2)}, u32[]{:S(2)}) collective-permute-start(bf16[128,512]{1,0:T(8,128)(2,1)S(1)} %get-tuple-element.53), channel_id=1, source_target_pairs={{0,2},{1,3},{2,0},{3,1},{4,6},{5,7},{6,4},{7,5},{8,10},{9,11},{10,... | collective-permute-start | bytes 393224 | tf_op jit(solution)/shard_map/ppermute | solution.py:405
  50.2 9.9 %collective-permute-start.5 = (bf16[128,512]{1,0:T(8,128)(2,1)S(1)}, bf16[128,512]{1,0:T(8,128)(2,1)S(1)}, u32[]{:S(2)}, u32[]{:S(2)}) collective-permute-start(bf16[128,512]{1,0:T(8,128)(2,1)S(1)} %get-tuple-element.54), channel_id=1, source_target_pairs={{0,3},{1,0},{2,1},{3,2},{4,7},{5,4},{6,5},{7,6},{8,11},{9,8},{10,9... | collective-permute-start | bytes 393224 | tf_op jit(solution)/shard_map/ppermute | solution.py:405
  52.7 7.4 %collective-permute-start.3 = (bf16[128,512]{1,0:T(8,128)(2,1)S(1)}, bf16[128,512]{1,0:T(8,128)(2,1)S(1)}, u32[]{:S(2)}, u32[]{:S(2)}) collective-permute-start(bf16[128,512]{1,0:T(8,128)(2,1)S(1)} %get-tuple-element.52.refs_4_), channel_id=1, source_target_pairs={{0,1},{1,2},{2,3},{3,0},{4,5},{5,6},{6,7},{7,4},{8,9},{9,10},{10,1... | collective-permute-start | bytes 393224 | tf_op jit(solution)/shard_map/ppermute | solution.py:405
  53.3 10.2 %collective-permute-start.6 = (bf16[128,512]{1,0:T(8,128)(2,1)S(1)}, bf16[128,512]{1,0:T(8,128)(2,1)S(1)}, u32[]{:S(2)}, u32[]{:S(2)}) collective-permute-start(bf16[128,512]{1,0:T(8,128)(2,1)S(1)} %get-tuple-element.59), channel_id=1, source_target_pairs={{0,1},{1,2},{2,3},{3,0},{4,5},{5,6},{6,7},{7,4},{8,9},{9,10},{10,1... | collective-permute-start | bytes 393224 | tf_op jit(solution)/shard_map/ppermute | solution.py:405
  53.5 11.5 %collective-permute-start.7 = (bf16[128,512]{1,0:T(8,128)(2,1)S(1)}, bf16[128,512]{1,0:T(8,128)(2,1)S(1)}, u32[]{:S(2)}, u32[]{:S(2)}) collective-permute-start(bf16[128,512]{1,0:T(8,128)(2,1)S(1)} %get-tuple-element.60), channel_id=1, source_target_pairs={{0,2},{1,3},{2,0},{3,1},{4,6},{5,7},{6,4},{7,5},{8,10},{9,11},{10,... | collective-permute-start | bytes 393224 | tf_op jit(solution)/shard_map/ppermute | solution.py:405
  59.9 5.1 %collective-permute-start.8 = (bf16[128,512]{1,0:T(8,128)(2,1)S(1)}, bf16[128,512]{1,0:T(8,128)(2,1)S(1)}, u32[]{:S(2)}, u32[]{:S(2)}) collective-permute-start(bf16[128,512]{1,0:T(8,128)(2,1)S(1)} %get-tuple-element.61), channel_id=1, source_target_pairs={{0,3},{1,0},{2,1},{3,2},{4,7},{5,4},{6,5},{7,6},{8,11},{9,8},{10,9... | collective-permute-start | bytes 393224 | tf_op jit(solution)/shard_map/ppermute | solution.py:405
  60.2 6.9 %collective-permute-start.13 = (bf16[128,512]{1,0:T(8,128)(2,1)S(1)}, bf16[128,512]{1,0:T(8,128)(2,1)S(1)}, u32[]{:S(2)}, u32[]{:S(2)}) collective-permute-start(bf16[128,512]{1,0:T(8,128)(2,1)S(1)} %slope.2.refs_0_), channel_id=1, source_target_pairs={{0,3},{1,0},{2,1},{3,2},{4,7},{5,4},{6,5},{7,6},{8,11},{9,8},{10,9... | collective-permute-start | bytes 393224 | tf_op jit(solution)/shard_map/ppermute | solution.py:405
  60.9 8.2 %collective-permute-start.11 = (bf16[128,512]{1,0:T(8,128)(2,1)S(1)}, bf16[128,512]{1,0:T(8,128)(2,1)S(1)}, u32[]{:S(2)}, u32[]{:S(2)}) collective-permute-start(bf16[128,512]{1,0:T(8,128)(2,1)S(1)} %slope.2.refs_0_), channel_id=1, source_target_pairs={{0,2},{1,3},{2,0},{3,1},{4,6},{5,7},{6,4},{7,5},{8,10},{9,11},{10,... | collective-permute-start | bytes 393224 | tf_op jit(solution)/shard_map/ppermute | solution.py:405
  63.5 6.1 %collective-permute-start.9 = (bf16[128,512]{1,0:T(8,128)(2,1)S(1)}, bf16[128,512]{1,0:T(8,128)(2,1)S(1)}, u32[]{:S(2)}, u32[]{:S(2)}) collective-permute-start(bf16[128,512]{1,0:T(8,128)(2,1)S(1)} %slope.2.refs_0_), channel_id=1, source_target_pairs={{0,1},{1,2},{2,3},{3,0},{4,5},{5,6},{6,7},{7,4},{8,9},{9,10},{10,1... | collective-permute-start | bytes 393224 | tf_op jit(solution)/shard_map/ppermute | solution.py:405
  65.2 7.0 %collective-permute-start.14 = (bf16[128,512]{1,0:T(8,128)(2,1)S(1)}, bf16[128,512]{1,0:T(8,128)(2,1)S(1)}, u32[]{:S(2)}, u32[]{:S(2)}) collective-permute-start(bf16[128,512]{1,0:T(8,128)(2,1)S(1)} %slope.3.refs_1_), channel_id=1, source_target_pairs={{0,3},{1,0},{2,1},{3,2},{4,7},{5,4},{6,5},{7,6},{8,11},{9,8},{10,9... | collective-permute-start | bytes 393224 | tf_op jit(solution)/shard_map/ppermute | solution.py:405
  66.5 5.8 %collective-permute-start.12 = (bf16[128,512]{1,0:T(8,128)(2,1)S(1)}, bf16[128,512]{1,0:T(8,128)(2,1)S(1)}, u32[]{:S(2)}, u32[]{:S(2)}) collective-permute-start(bf16[128,512]{1,0:T(8,128)(2,1)S(1)} %slope.3.refs_1_), channel_id=1, source_target_pairs={{0,2},{1,3},{2,0},{3,1},{4,6},{5,7},{6,4},{7,5},{8,10},{9,11},{10,... | collective-permute-start | bytes 393224 | tf_op jit(solution)/shard_map/ppermute | solution.py:405
  67.2 8.6 %collective-permute-start.10 = (bf16[128,512]{1,0:T(8,128)(2,1)S(1)}, bf16[128,512]{1,0:T(8,128)(2,1)S(1)}, u32[]{:S(2)}, u32[]{:S(2)}) collective-permute-start(bf16[128,512]{1,0:T(8,128)(2,1)S(1)} %slope.3.refs_1_), channel_id=1, source_target_pairs={{0,1},{1,2},{2,3},{3,0},{4,5},{5,6},{6,7},{7,4},{8,9},{9,10},{10,1... | collective-permute-start | bytes 393224 | tf_op jit(solution)/shard_map/ppermute | solution.py:405
  78.8 6.8 %collective-permute-start.15 = (bf16[4,256,512]{2,1,0:T(8,128)(2,1)}, bf16[4,256,512]{2,1,0:T(8,128)(2,1)S(1)}, u32[]{:S(2)}, u32[]{:S(2)}) collective-permute-start(bf16[4,256,512]{2,1,0:T(8,128)(2,1)} %get-tuple-element.67.refs_0_), channel_id=1, source_target_pairs={{0,4},{4,0},{8,12},{12,8},{16,20},{20,16},{24,28},{28,24},{32,36},... | collective-permute-start | bytes 3145736 | tf_op jit(solution)/shard_map/ppermute | solution.py:413
  80.7 5.0 %collective-permute-start.16 = (bf16[256,1024]{1,0:T(8,128)(2,1)S(1)}, bf16[256,1024]{1,0:T(8,128)(2,1)S(1)}, u32[]{:S(2)}, u32[]{:S(2)}) collective-permute-start(bf16[256,1024]{1,0:T(8,128)(2,1)S(1)} %copy-done.7), channel_id=1, source_target_pairs={{0,4},{4,0},{8,12},{12,8},{16,20},{20,16},{24,28},{28,24},{32,36},... | collective-permute-start | bytes 1572872 | tf_op jit(solution)/shard_map/ppermute | solution.py:413
  80.8 16.5 %all-to-all-start.2 = ((bf16[32,16,512]{2,1,0:T(8,128)(2,1)}), bf16[32,16,512]{2,1,0:T(8,128)(2,1)S(1)}, u32[]{:S(2)}, u32[]{:S(2)}) async-start(bf16[32,16,512]{2,1,0:T(8,128)(2,1)} %get-tuple-element.64), calls=%async_computation.2 | async-start | bytes 1048576 | tf_op jit(solution)/shard_map/all_to_all | solution.py:491
  90.6 12.1 %collective-permute-start.22 = (bf16[4,64,1024]{2,1,0:T(8,128)(2,1)}, bf16[4,64,1024]{2,1,0:T(8,128)(2,1)S(1)}, u32[]{:S(2)}, u32[]{:S(2)}) collective-permute-start(bf16[4,64,1024]{2,1,0:T(8,128)(2,1)} %get-tuple-element.76), channel_id=1, source_target_pairs={{0,8},{4,36},{8,16},{12,44},{16,24},{20,52},{24,0},{28,60},{32,40}... | collective-permute-start | bytes 1572872 | tf_op jit(solution)/shard_map/ppermute | solution.py:421
  92.0 15.1 %collective-permute-start.23 = (bf16[4,64,1024]{2,1,0:T(8,128)(2,1)}, bf16[4,64,1024]{2,1,0:T(8,128)(2,1)S(1)}, u32[]{:S(2)}, u32[]{:S(2)}) collective-permute-start(bf16[4,64,1024]{2,1,0:T(8,128)(2,1)} %get-tuple-element.77), channel_id=1, source_target_pairs={{0,16},{4,68},{8,24},{12,76},{16,0},{20,84},{24,8},{28,92},{32,48}... | collective-permute-start | bytes 1572872 | tf_op jit(solution)/shard_map/ppermute | solution.py:421
  94.5 12.7 %collective-permute-start.24 = (bf16[4,64,1024]{2,1,0:T(8,128)(2,1)}, bf16[4,64,1024]{2,1,0:T(8,128)(2,1)S(1)}, u32[]{:S(2)}, u32[]{:S(2)}) collective-permute-start(bf16[4,64,1024]{2,1,0:T(8,128)(2,1)} %get-tuple-element.78), channel_id=1, source_target_pairs={{0,24},{4,100},{8,0},{12,108},{16,8},{20,116},{24,16},{28,124},{32... | collective-permute-start | bytes 1572872 | tf_op jit(solution)/shard_map/ppermute | solution.py:421
  95.6 4.1 %collective-permute-start.21 = (bf16[256,512]{1,0:T(8,128)(2,1)S(1)}, bf16[256,512]{1,0:T(8,128)(2,1)S(1)}, u32[]{:S(2)}, u32[]{:S(2)}) collective-permute-start(bf16[256,512]{1,0:T(8,128)(2,1)S(1)} %copy-done.8), channel_id=1, source_target_pairs={{0,4},{4,0},{8,12},{12,8},{16,20},{20,16},{24,28},{28,24},{32,36},... | collective-permute-start | bytes 786440 | tf_op jit(solution)/shard_map/ppermute | solution.py:413
  99.6 1.6 %collective-permute-start.20 = (bf16[256,512]{1,0:T(8,128)(2,1)S(1)}, bf16[256,512]{1,0:T(8,128)(2,1)S(1)}, u32[]{:S(2)}, u32[]{:S(2)}) collective-permute-start(bf16[256,512]{1,0:T(8,128)(2,1)S(1)} %get-tuple-element.74.refs_0_), channel_id=1, source_target_pairs={{0,4},{4,0},{8,12},{12,8},{16,20},{20,16},{24,28},{28,24},{32,36},... | collective-permute-start | bytes 786440 | tf_op jit(solution)/shard_map/ppermute | solution.py:413
  99.7 9.4 %collective-permute-start.18 = (bf16[256,256]{1,0:T(8,128)(2,1)S(1)}, bf16[256,256]{1,0:T(8,128)(2,1)S(1)}, u32[]{:S(2)}, u32[]{:S(2)}) collective-permute-start(bf16[256,256]{1,0:T(8,128)(2,1)S(1)} %get-tuple-element.72), channel_id=1, source_target_pairs={{0,2},{1,3},{2,0},{3,1},{4,6},{5,7},{6,4},{7,5},{8,10},{9,11},{10,... | collective-permute-start | bytes 393224 | tf_op jit(solution)/shard_map/ppermute | solution.py:405
  101.2 7.9 %collective-permute-start.19 = (bf16[256,256]{1,0:T(8,128)(2,1)S(1)}, bf16[256,256]{1,0:T(8,128)(2,1)S(1)}, u32[]{:S(2)}, u32[]{:S(2)}) collective-permute-start(bf16[256,256]{1,0:T(8,128)(2,1)S(1)} %get-tuple-element.73), channel_id=1, source_target_pairs={{0,3},{1,0},{2,1},{3,2},{4,7},{5,4},{6,5},{7,6},{8,11},{9,8},{10,9... | collective-permute-start | bytes 393224 | tf_op jit(solution)/shard_map/ppermute | solution.py:405
  102.6 6.8 %collective-permute-start.17 = (bf16[256,256]{1,0:T(8,128)(2,1)S(1)}, bf16[256,256]{1,0:T(8,128)(2,1)S(1)}, u32[]{:S(2)}, u32[]{:S(2)}) collective-permute-start(bf16[256,256]{1,0:T(8,128)(2,1)S(1)} %get-tuple-element.71.refs_4_), channel_id=1, source_target_pairs={{0,1},{1,2},{2,3},{3,0},{4,5},{5,6},{6,7},{7,4},{8,9},{9,10},{10,1... | collective-permute-start | bytes 393224 | tf_op jit(solution)/shard_map/ppermute | solution.py:405
  110.4 16.6 %all-to-all-start.3 = ((bf16[16,160,128]{2,1,0:T(8,128)(2,1)}), bf16[16,160,128]{2,1,0:T(8,128)(2,1)S(1)}, u32[]{:S(2)}, u32[]{:S(2)}) async-start(bf16[16,160,128]{2,1,0:T(8,128)(2,1)} %get-tuple-element.80), calls=%async_computation.3 | async-start | bytes 1310720 | tf_op jit(solution)/shard_map/all_to_all | solution.py:527
  116.3 14.0 %collective-permute-start.25 = (bf16[64,1024]{1,0:T(8,128)(2,1)}, bf16[64,1024]{1,0:T(8,128)(2,1)S(1)}, u32[]{:S(2)}, u32[]{:S(2)}) collective-permute-start(bf16[64,1024]{1,0:T(8,128)(2,1)} %copy-done.5), channel_id=1, source_target_pairs={{0,32},{4,12},{8,40},{12,20},{16,48},{20,28},{24,56},{28,4},{32,64... | collective-permute-start | bytes 393224 | tf_op jit(solution)/shard_map/ppermute | solution.py:421
  117.7 12.8 %collective-permute-start.26 = (bf16[64,1024]{1,0:T(8,128)(2,1)}, bf16[64,1024]{1,0:T(8,128)(2,1)S(1)}, u32[]{:S(2)}, u32[]{:S(2)}) collective-permute-start(bf16[64,1024]{1,0:T(8,128)(2,1)} %copy-done.4), channel_id=1, source_target_pairs={{0,64},{4,20},{8,72},{12,28},{16,80},{20,4},{24,88},{28,12},{32,96... | collective-permute-start | bytes 393224 | tf_op jit(solution)/shard_map/ppermute | solution.py:421
  120.1 10.4 %collective-permute-start.27 = (bf16[64,1024]{1,0:T(8,128)(2,1)S(1)}, bf16[64,1024]{1,0:T(8,128)(2,1)S(1)}, u32[]{:S(2)}, u32[]{:S(2)}) collective-permute-start(bf16[64,1024]{1,0:T(8,128)(2,1)S(1)} %get-tuple-element.84), channel_id=1, source_target_pairs={{0,96},{4,28},{8,104},{12,4},{16,112},{20,12},{24,120},{28,20},{32... | collective-permute-start | bytes 393224 | tf_op jit(solution)/shard_map/ppermute | solution.py:421
  127.0 5.0 %collective-permute-start.28 = (bf16[16,16,128]{2,1,0:T(8,128)(2,1)S(1)}, bf16[16,16,128]{2,1,0:T(8,128)(2,1)S(1)}, u32[]{:S(2)}, u32[]{:S(2)}) collective-permute-start(bf16[16,16,128]{2,1,0:T(8,128)(2,1)S(1)} %get-tuple-element.81.refs_1_), channel_id=1, source_target_pairs={{0,4},{4,0},{8,12},{12,8},{16,20},{20,16},{24,28},{28,24},{32,36},... | collective-permute-start | bytes 196616 | tf_op jit(solution)/shard_map/ppermute | solution.py:413
  (9 other events, 173.4 us)

commit v5 on v4

--- a/solution.py
+++ b/solution.py
@@ -50,7 +50,14 @@
 
 
 def pick_kernel(routes_ref, feat_ref, sel_ref, send_ref):
-    sel = route_rows(routes_ref).T.astype(BF16)
+    row_peer = lax.broadcasted_iota(jnp.int32, (FAR, PEERS), 0) >> 4
+    peer = lax.broadcasted_iota(jnp.int32, (FAR, PEERS), 1)
+    by_slot = mm_last(jnp.where(row_peer == peer, 1.0, 0.0).astype(BF16), routes_ref[...].astype(F32).astype(BF16))
+    row_slot = lax.broadcasted_iota(jnp.int32, (FAR, SLOTS), 0) & (SLOTS - 1)
+    slot = lax.broadcasted_iota(jnp.int32, (FAR, SLOTS), 1)
+    routes = jnp.sum(jnp.where(row_slot == slot, by_slot, 0.0), axis=1, keepdims=True)
+    row = lax.broadcasted_iota(jnp.int32, (FAR, ROWS), 1).astype(F32)
+    sel = jnp.where(row == routes, 1.0, 0.0).astype(BF16)
     sel_ref[...] = sel
     picked = mm(sel, feat_ref[...]).astype(BF16).reshape(PEERS, SLOTS, LANES)
     for part in range(HID):
@@ -123,27 +130,16 @@
 
 
 def second_kernel(
-    place, hidden_ref, far_ref, adj_ref, inv_ref, w_hbm, stacked_ref,
-    own_a, own_b, s1a, s1b, s2a, s2b, s3a, s3b, w_ref, sems,
+    place, hidden_ref, far_ref, adj_ref, inv_ref, w_ref, stacked_ref, own_a, own_b, s1a, s1b, s2a, s2b, s3a, s3b
 ):
-    order = ((2, s2a, s2b), (1, s1a, s1b), (3, s3a, s3b), (0, own_a, own_b))
-    pieces, tall = 4, 2 * UNITS // 4
-    copies = []
-    for slot, (d, upper, lower) in enumerate(order):
-        target = lax.rem(place.hid + d, HID)
-        cols = pl.ds(pl.multiple_of(target * UNITS, UNITS), UNITS)
-        for piece in range(pieces):
-            rows = pl.ds(piece * tall, tall)
-            copies.append(pltpu.make_async_copy(w_hbm.at[rows, cols], w_ref.at[slot, rows], sems.at[slot, piece]))
-            copies[-1].start()
     hidden = hidden_ref[...]
     total = mm(adj_ref[:, :ROWS], hidden) + mm(adj_ref[:, ROWS:], far_ref[...].reshape(FAR, UNITS))
     stacked_ref[:, :UNITS] = hidden
     stacked_ref[:, UNITS:] = (total * wide(inv_ref[...], UNITS)).astype(BF16)
-    for slot, (d, upper, lower) in enumerate(order):
-        for copy in copies[slot * pieces : (slot + 1) * pieces]:
-            copy.wait()
-        part = mm(stacked_ref[...], w_ref[slot]).astype(upper.dtype)
+    for d, upper, lower in ((2, s2a, s2b), (1, s1a, s1b), (3, s3a, s3b), (0, own_a, own_b)):
+        target = lax.rem(place.hid + d, HID)
+        cols = pl.ds(pl.multiple_of(target * UNITS, UNITS), UNITS)
+        part = mm(stacked_ref[...], w_ref[:, cols]).astype(upper.dtype)
         upper[...] = part[: ROWS // 2]
         lower[...] = part[ROWS // 2 :]
 
@@ -252,13 +248,6 @@
         out[...] = total.astype(out.dtype)
 
 
-def last_second_kernel(scale, x0, x1, x2, x3, out_ref):
-    total = x0[...] + x1[...].astype(F32) + x2[...].astype(F32) + x3[...].astype(F32)
-    total = total * scale
-    out_ref[:, 0, :] = total[:, :UNITS]
-    out_ref[:, 1, :] = total[:, UNITS:]
-
-
 def settle_kernel(
     place, back_ref, own_ref, slope_ref, selt_ref, w_ref, grad_ref, mine_ref, s1, s2, s3, full_ref
 ):
@@ -298,14 +287,18 @@
         out[...] = parts_ref[:, pl.ds(pl.multiple_of(LANES + core * SLOTS, SLOTS), SLOTS), :]
 
 
-def weights_kernel(scale, parts_ref, weight_ref):
+def weights_kernel(scale, x0, x1, x2, x3, parts_ref, second_ref, first_ref):
     total = parts_ref[0, :LANES].astype(F32)
     for index in range(1, CHIPS):
         total = total + parts_ref[index, :LANES].astype(F32)
+    total = total * scale
     for part in range(HID):
         for kind in range(2):
             start = (part * 2 + kind) * SLOTS
-            weight_ref[:, kind, part * LANES : (part + 1) * LANES] = total[start : start + SLOTS] * scale
+            first_ref[:, kind, part * LANES : (part + 1) * LANES] = total[start : start + SLOTS]
+    total = (x0[...] + x1[...].astype(F32) + x2[...].astype(F32) + x3[...].astype(F32)) * scale
+    second_ref[:, 0, :] = total[:, :UNITS]
+    second_ref[:, 1, :] = total[:, UNITS:]
 
 
 def final_kernel(place, base_ref, selt_ref, mine_ref, mate_ref, feat_ref, back_ref):
@@ -449,7 +442,7 @@
     )
     both, hidden, send_hidden = call(
         first_kernel, "first", (features, f1, f2, f3, far_feat, adj, inv, w1, sel),
-        [((ROWS, 2 * UNITS), BF16), chunk, halo], work=6, placed=True,
+        [((ROWS, 2 * UNITS), BF16), chunk, halo], work=60, placed=True,
         scratch=[pltpu.VMEM((FAR, UNITS), BF16)],
     )
     far_hidden = lax.all_to_all(send_hidden, "nodes", 0, 0, tiled=True)
@@ -457,8 +450,7 @@
     stacked, own_a, own_b, s1a, s1b, s2a, s2b, s3a, s3b = call(
         second_kernel, "second", (hidden, far_hidden, adj, inv, w2),
         [((ROWS, 2 * UNITS), BF16)] + [((ROWS // 2, UNITS), F32)] * 2 + [half_chunk] * 6,
-        scratch=[pltpu.VMEM((HID, 2 * UNITS, UNITS), BF16), pltpu.SemaphoreType.DMA((HID, 4))],
-        placed=True, work=10, held=(4,),
+        placed=True, work=10,
     )
     r2a, r1a, r3a = around([(2, s2a), (1, s1a), (3, s3a)])
     r2b, r1b, r3b = around([(2, s2b), (1, s1b), (3, s3b)])
@@ -515,7 +507,7 @@
     )
     x0, x1, x2, x3 = call(
         along_kernel, "along", (z0, z1, z2, z3),
-        [((64, 2 * UNITS), F32)] + [((64, 2 * UNITS), BF16)] * 3, placed=True, late=(0,), after=(s1,),
+        [((64, 2 * UNITS), F32)] + [((64, 2 * UNITS), BF16)] * 3, placed=True, after=(s1,),
     )
     base, merged = call(
         return_kernel, "return", (mine, r1, r2, r3, inv, adjt, merged),
@@ -529,16 +521,13 @@
     mine_back, give_back = call(hand_kernel, "hand", (parts,), [block, block], placed=True)
     mate_back = swap(give_back)
     x2, x1, x3 = near([(2, x2), (1, x1), (3, x3)], True)
-    grad_w_first = call(
-        lambda *refs: weights_kernel(scale, *refs), "weights", (parts,), [((SLOTS, 2, UNITS), F32)],
-        after=(give_back,),
+    grad_w_second, grad_w_first = call(
+        lambda *refs: weights_kernel(scale, *refs), "weights", (x0, x1, x2, x3, parts),
+        [((64, 2, UNITS), F32), ((SLOTS, 2, UNITS), F32)], after=(give_back,),
     )
     grad_features = call(
         final_kernel, "final", (base, selt, mine_back, mate_back), [((ROWS, LANES), F32)],
         placed=True, scratch=[pltpu.VMEM((CHIPS, 2, SLOTS, LANES), BF16)],
-    )
-    grad_w_second = call(
-        lambda *refs: last_second_kernel(scale, *refs), "last_second", (x0, x1, x2, x3), [((64, 2, UNITS), F32)],
     )
     return grad_w_first, grad_w_second, grad_features
 

time: 134 us -> 130 us (0.970)
  Pallas kernels: 31.1 us -> 27.7 us
    pallas_call x18 -> x17, Pallas kernels: 31.1 us -> 27.7 us  [call(): pl.pallas_call(body, out_shape=shapes, in_specs=in_specs, out_specs=out_s...]
  transfers between devices with their start and end apart: 32 -> 32, of which waited for: 14 -> 14; matrix products, arithmetic and copies ran while one was open for 0% -> 0% of each run, Pallas kernels for 15% -> 14%
where the time goes in v5:
time: 130 us; the launch traced here: 129 us
  starting transfers between devices  56.7 us (44%)
  Pallas kernels  27.7 us (21%)
  waiting for transfers between devices  25.9 us (20%)
  blocking collectives  16.9 us (13%)
  between operations  1.59 us (1%)
    pallas_call x17, Pallas kernels, call(): pl.pallas_call(body, out_shape=shapes, in_specs=in_specs, out_specs=out_s...  27.7 us
    ppermute x18, starting transfers between devices, around(): lax.ppermute(v, 'hid', [(i, (i + d) % HID) for i in range(HID)])  19 us
    all_to_all x1, blocking collectives, on_device(): far_hidden = lax.all_to_all(send_hidden, 'nodes', 0, 0, tiled=True)  16.9 us
    ppermute x18, waiting for transfers between devices, around(): lax.ppermute(v, 'hid', [(i, (i + d) % HID) for i in range(HID)])  15.1 us
    all_to_all x1, starting transfers between devices, on_device(): lax.all_to_all(send_feat.reshape(PEERS * HID, SLOTS, LANES), ('nodes', 'h...  11.5 us
    ppermute x6, starting transfers between devices, near(): lax.ppermute(v, 'nodes', [(node_at(x, z, c), target(x, z, c, d)) for x in...  9.97 us
    ppermute x5, starting transfers between devices, swap(): return lax.ppermute(value, 'nodes', [(i, i ^ 1) for i in range(PEERS)])  6.6 us
    all_to_all x1, waiting for transfers between devices, on_device(): lax.all_to_all(merged, 'nodes', 0, 0, tiled=True, axis_index_groups=same_...  5.72 us
  transfers between devices with their start and end apart: 32, of which 14 were waited for; matrix products, arithmetic and copies ran while one was open for 0% of the time, Pallas kernels for 14%

profile of v5, /device:TPU:1, one launch (start us, length us, event | category | flops | bytes accessed | tf_op | source)
XLA Modules:
  0.0 129.5 jit_solution(6212322236551087648)
XLA Ops:
  0.7 2.1 %pick.1 = (bf16[512,256]{1,0:T(8,128)(2,1)S(1)}, bf16[32,4,16,128]{3,2,1,0:T(8,128)(2,1)}) custom-call(s32[16,32]{1,0:T(8,128)} %bitcast.15, bf16[256,128]{1,0:T(8,128)(2,1)} %refs_0_.3), custom_call_target="tpu_custom_call" | custom-call | flops 134217728 | bytes 854016 | tf_op jit(solution)/shard_map/pick/pallas_call | solution.py:383
  2.8 11.5 %all-to-all-start = ((bf16[128,16,128]{2,1,0:T(8,128)(2,1)}), bf16[128,16,128]{2,1,0:T(8,128)(2,1)S(1)}, u32[]{:S(2)}, u32[]{:S(2)}) async-start(bf16[128,16,128]{2,1,0:T(8,128)(2,1)} %bitcast.2), calls=%async_computation | async-start | bytes 1048576 | tf_op jit(solution)/shard_map/all_to_all | solution.py:434
  14.3 2.7 %collective-permute-start.2 = (bf16[256,128]{1,0:T(8,128)(2,1)}, bf16[256,128]{1,0:T(8,128)(2,1)S(1)}, u32[]{:S(2)}, u32[]{:S(2)}) collective-permute-start(bf16[256,128]{1,0:T(8,128)(2,1)} %refs_0_.3), channel_id=1, source_target_pairs={{0,3},{1,0},{2,1},{3,2},{4,7},{5,4},{6,5},{7,6},{8,11},{9,8},{10,9... | collective-permute-start | bytes 196616 | tf_op jit(solution)/shard_map/ppermute | solution.py:398
  18.1 3.2 %count.1 = (bf16[256,768]{1,0:T(8,128)(2,1)S(1)}, bf16[768,256]{1,0:T(8,128)(2,1)S(1)}, f32[256,128]{1,0:T(8,128)S(1)}) custom-call(s32[80,256]{1,0:T(8,128)} %bitcast.17, s32[1,256]{1,0:T(1,128)} %bitcast.18, bf16[512,256]{1,0:T(8,128)(2,1)S(1)} %get-tuple-element.48.refs_2_.refs_8_), custom_call_target="tpu_custom_call" | custom-call | flops 1073741824 | bytes 1000448 | tf_op jit(solution)/shard_map/count/pallas_call | solution.py:383
  21.5 4.1 %collective-permute-done.1.refs_2_ = bf16[256,128]{1,0:T(8,128)(2,1)S(1)} collective-permute-done((bf16[256,128]{1,0:T(8,128)(2,1)}, bf16[256,128]{1,0:T(8,128)(2,1)S(1)}, u32[]{:S(2)}, u32[]{:S(2)}) %collective-permute-start.1) | collective-permute-done | bytes 65568 | tf_op jit(solution)/shard_map/ppermute | solution.py:398
  25.5 1.4 %collective-permute-done.refs_1_ = bf16[256,128]{1,0:T(8,128)(2,1)S(1)} collective-permute-done((bf16[256,128]{1,0:T(8,128)(2,1)}, bf16[256,128]{1,0:T(8,128)(2,1)S(1)}, u32[]{:S(2)}, u32[]{:S(2)}) %collective-permute-start) | collective-permute-done | bytes 65568 | tf_op jit(solution)/shard_map/ppermute | solution.py:398
  27.0 1.5 %all-to-all-done = bf16[128,16,128]{2,1,0:T(8,128)(2,1)S(1)} async-done(((bf16[128,16,128]{2,1,0:T(8,128)(2,1)}), bf16[128,16,128]{2,1,0:T(8,128)(2,1)S(1)}, u32[]{:S(2)}, u32[]{:S(2)}) %all-to-all-start) | async-done | bytes 524320 | tf_op jit(solution)/shard_map/all_to_all | solution.py:434
  29.6 16.9 %all_to_all.20.refs_1_ = bf16[32,16,512]{2,1,0:T(8,128)(2,1)S(1)} all-to-all(bf16[32,16,512]{2,1,0:T(8,128)(2,1)S(1)} %get-tuple-element.52), channel_id=1, replica_groups=mesh['nodes'=32,'hid'=4] {'nodes'}, dimensions={0} | all-to-all | bytes 1048576 | tf_op jit(solution)/shard_map/all_to_all | solution.py:448
  46.5 1.5 %second.1 = (bf16[256,1024]{1,0:T(8,128)(2,1)S(1)}, f32[128,512]{1,0:T(8,128)S(1)}, f32[128,512]{1,0:T(8,128)S(1)}, bf16[128,512]{1,0:T(8,128)(2,1)S(1)}, bf16[1...) custom-call(bf16[256,512]{1,0:T(8,128)(2,1)S(1)} %get-tuple-element., ...), custom_call_target="tpu_custom_call" | custom-call | flops 1342177280 | bytes 7340032 | tf_op jit(solution)/shard_map/second/pallas_call | solution.py:383
  48.4 2.5 %collective-permute-start.5 = (bf16[128,512]{1,0:T(8,128)(2,1)S(1)}, bf16[128,512]{1,0:T(8,128)(2,1)S(1)}, u32[]{:S(2)}, u32[]{:S(2)}) collective-permute-start(bf16[128,512]{1,0:T(8,128)(2,1)S(1)} %get-tuple-element.56), channel_id=1, source_target_pairs={{0,3},{1,0},{2,1},{3,2},{4,7},{5,4},{6,5},{7,6},{8,11},{9,8},{10,9... | collective-permute-start | bytes 393224 | tf_op jit(solution)/shard_map/ppermute | solution.py:398
  51.8 3.7 %collective-permute-start.7 = (bf16[128,512]{1,0:T(8,128)(2,1)S(1)}, bf16[128,512]{1,0:T(8,128)(2,1)S(1)}, u32[]{:S(2)}, u32[]{:S(2)}) collective-permute-start(bf16[128,512]{1,0:T(8,128)(2,1)S(1)} %get-tuple-element.62), channel_id=1, source_target_pairs={{0,2},{1,3},{2,0},{3,1},{4,6},{5,7},{6,4},{7,5},{8,10},{9,11},{10,... | collective-permute-start | bytes 393224 | tf_op jit(solution)/shard_map/ppermute | solution.py:398
  55.5 2.7 %gate.1 = (f32[256,512]{1,0:T(8,128)}, bf16[256,1024]{1,0:T(8,128)(2,1)}, bf16[256,512]{1,0:T(8,128)(2,1)}) custom-call(bf16[256,1024]{1,0:T(8,128)(2,1)S(1)} %get-tuple-element.57.refs_0_, bf16[256,1024]{1,0:T(8,128)(2,1)S(1)} %get-tuple-element.58.refs_1_, bf16[1024,512]{1,0:T(8,128)(2,1)} %bitcast.11, s32[16,32]{1,0:T(8,128)} %bitcast.16, ...), custom_call_target="tpu_custom_call" | custom-call | flops 268435456 | bytes 3409920 | tf_op jit(solution)/shard_map/gate/pallas_call | solution.py:383
  59.1 2.7 %collective-permute-start.11 = (bf16[128,512]{1,0:T(8,128)(2,1)S(1)}, bf16[128,512]{1,0:T(8,128)(2,1)S(1)}, u32[]{:S(2)}, u32[]{:S(2)}) collective-permute-start(bf16[128,512]{1,0:T(8,128)(2,1)S(1)} %slope.2.refs_0_), channel_id=1, source_target_pairs={{0,2},{1,3},{2,0},{3,1},{4,6},{5,7},{6,4},{7,5},{8,10},{9,11},{10,... | collective-permute-start | bytes 393224 | tf_op jit(solution)/shard_map/ppermute | solution.py:398
  61.8 1.5 %collective-permute-done.7.refs_3_ = bf16[128,512]{1,0:T(8,128)(2,1)S(1)} collective-permute-done((bf16[128,512]{1,0:T(8,128)(2,1)S(1)}, bf16[128,512]{1,0:T(8,128)(2,1)S(1)}, u32[]{:S(2)}, u32[]{:S(2)}) %collective-permute-start.7) | collective-permute-done | bytes 131104 | tf_op jit(solution)/shard_map/ppermute | solution.py:398
  67.9 2.6 %collective-permute-done.14.refs_7_ = bf16[128,512]{1,0:T(8,128)(2,1)S(1)} collective-permute-done((bf16[128,512]{1,0:T(8,128)(2,1)S(1)}, bf16[128,512]{1,0:T(8,128)(2,1)S(1)}, u32[]{:S(2)}, u32[]{:S(2)}) %collective-permute-start.14) | collective-permute-done | bytes 131104 | tf_op jit(solution)/shard_map/ppermute | solution.py:398
  70.5 3.5 %collective-permute-done.10.refs_3_ = bf16[128,512]{1,0:T(8,128)(2,1)S(1)} collective-permute-done((bf16[128,512]{1,0:T(8,128)(2,1)S(1)}, bf16[128,512]{1,0:T(8,128)(2,1)S(1)}, u32[]{:S(2)}, u32[]{:S(2)}) %collective-permute-start.10) | collective-permute-done | bytes 131104 | tf_op jit(solution)/shard_map/ppermute | solution.py:398
  74.0 3.0 %spread.1 = (bf16[32,16,512]{2,1,0:T(8,128)(2,1)}, f32[256,512]{1,0:T(8,128)}, bf16[4,256,512]{2,1,0:T(8,128)(2,1)}) custom-call(bf16[128,512]{1,0:T(8,128)(2,1)S(1)} %slope.2.refs_0_, bf16[128,512]{1,0:T(8,128)(2,1)S(1)} %slope.3.refs_1_, bf16[128,512]{1,0:T(8,128)(2,1)S(1)} %collective-permute-done.9.refs_2_, ...), custom_call_target="tpu_custom_call" | custom-call | flops 1342177280 | bytes 7864320 | tf_op jit(solution)/shard_map/spread/pallas_call | solution.py:383
  77.1 1.8 %collective-permute-start.15 = (bf16[4,256,512]{2,1,0:T(8,128)(2,1)}, bf16[4,256,512]{2,1,0:T(8,128)(2,1)S(1)}, u32[]{:S(2)}, u32[]{:S(2)}) collective-permute-start(bf16[4,256,512]{2,1,0:T(8,128)(2,1)} %get-tuple-element.66.refs_0_), channel_id=1, source_target_pairs={{0,4},{4,0},{8,12},{12,8},{16,20},{20,16},{24,28},{28,24},{32,36},... | collective-permute-start | bytes 3145736 | tf_op jit(solution)/shard_map/ppermute | solution.py:406
  79.0 4.9 %all-to-all-start.2 = ((bf16[32,16,512]{2,1,0:T(8,128)(2,1)}), bf16[32,16,512]{2,1,0:T(8,128)(2,1)S(1)}, u32[]{:S(2)}, u32[]{:S(2)}) async-start(bf16[32,16,512]{2,1,0:T(8,128)(2,1)} %get-tuple-element.72), calls=%async_computation.2 | async-start | bytes 1048576 | tf_op jit(solution)/shard_map/all_to_all | solution.py:483
  83.9 4.9 %outer_second.1 = (bf16[4,64,1024]{2,1,0:T(8,128)(2,1)}, bf16[4,64,1024]{2,1,0:T(8,128)(2,1)}, bf16[4,64,1024]{2,1,0:T(8,128)(2,1)}, bf16[4,64,1024]{2,1,0:T(8,128)(2,1)}) custom-call(bf16[4,256,512]{2,1,0:T(8,128)(2,1)} %get-tuple-element.66.refs_0_, bf16[4,256,512]{2,1,0:T(8,128)(2,1)S(1)} %collective-permute-done.15.refs_1_, ...), custom_call_target="tpu_custom_call" | custom-call | flops 1610612736 | bytes 5242880 | tf_op jit(solution)/shard_map/outer_second/pallas_call | solution.py:383
  88.8 1.5 %collective-permute-start.17 = (bf16[4,64,1024]{2,1,0:T(8,128)(2,1)}, bf16[4,64,1024]{2,1,0:T(8,128)(2,1)S(1)}, u32[]{:S(2)}, u32[]{:S(2)}) collective-permute-start(bf16[4,64,1024]{2,1,0:T(8,128)(2,1)} %get-tuple-element.69), channel_id=1, source_target_pairs={{0,8},{4,36},{8,16},{12,44},{16,24},{20,52},{24,0},{28,60},{32,40}... | collective-permute-start | bytes 1572872 | tf_op jit(solution)/shard_map/ppermute | solution.py:414
  90.3 2.4 %collective-permute-start.18 = (bf16[4,64,1024]{2,1,0:T(8,128)(2,1)}, bf16[4,64,1024]{2,1,0:T(8,128)(2,1)S(1)}, u32[]{:S(2)}, u32[]{:S(2)}) collective-permute-start(bf16[4,64,1024]{2,1,0:T(8,128)(2,1)} %get-tuple-element.70), channel_id=1, source_target_pairs={{0,16},{4,68},{8,24},{12,76},{16,0},{20,84},{24,8},{28,92},{32,48}... | collective-permute-start | bytes 1572872 | tf_op jit(solution)/shard_map/ppermute | solution.py:414
  95.5 2.3 %settle.1 = (bf16[256,512]{1,0:T(8,128)(2,1)S(1)}, f32[256,256]{1,0:T(8,128)S(1)}, bf16[256,256]{1,0:T(8,128)(2,1)S(1)}, bf16[256,256]{1,0:T(8,128)(2,1)S(1)}, bf16[256,256]{1,0:T(8,128)(2,1)S(1)}) custom-call(bf16[32,16,512]{2,1,0:T(8,128)(2,1)S(1)} %all-to-all-done.2.refs_0_, f32[256,512]{1,0:T(8,128)} %get-tuple-element.73.refs_1_, ...), custom_call_target="tpu_custom_call" | custom-call | flops 805306368 | bytes 3801088 | tf_op jit(solution)/shard_map/settle/pallas_call | solution.py:383
  99.4 1.4 %collective-permute-start.25 = (bf16[256,256]{1,0:T(8,128)(2,1)S(1)}, bf16[256,256]{1,0:T(8,128)(2,1)S(1)}, u32[]{:S(2)}, u32[]{:S(2)}) collective-permute-start(bf16[256,256]{1,0:T(8,128)(2,1)S(1)} %get-tuple-element.82), channel_id=1, source_target_pairs={{0,3},{1,0},{2,1},{3,2},{4,7},{5,4},{6,5},{7,6},{8,11},{9,8},{10,9... | collective-permute-start | bytes 393224 | tf_op jit(solution)/shard_map/ppermute | solution.py:398
  100.9 2.3 %outer_first.1.refs_6_ = bf16[16,160,128]{2,1,0:T(8,128)(2,1)} custom-call(bf16[256,512]{1,0:T(8,128)(2,1)S(1)} %get-tuple-element.83.refs_0_, bf16[256,512]{1,0:T(8,128)(2,1)S(1)} %collective-permute-done.26.refs_1_, bf16[256,512]{1,0:T(8,128)(2,1)} %get-tuple-element.65.refs_11_.refs_2_, bf16[256,512]{1,0:T(8,128)(2,1)S(1)} %collective-permute-done.27.refs_3_, ...), custom_call_target="tpu_custom_call" | custom-call | flops 268435456 | bytes 1703936 | tf_op jit(solution)/shard_map/outer_first/pallas_call | solution.py:383
  103.2 2.2 %collective-permute-done.18.refs_2_ = bf16[4,64,1024]{2,1,0:T(8,128)(2,1)S(1)} collective-permute-done((bf16[4,64,1024]{2,1,0:T(8,128)(2,1)}, bf16[4,64,1024]{2,1,0:T(8,128)(2,1)S(1)}, u32[]{:S(2)}, u32[]{:S(2)}) %collective-permute-start.18) | collective-permute-done | bytes 524320 | tf_op jit(solution)/shard_map/ppermute | solution.py:414
  106.3 1.4 %collective-permute-done.23.refs_1_ = bf16[256,256]{1,0:T(8,128)(2,1)S(1)} collective-permute-done((bf16[256,256]{1,0:T(8,128)(2,1)S(1)}, bf16[256,256]{1,0:T(8,128)(2,1)S(1)}, u32[]{:S(2)}, u32[]{:S(2)}) %collective-permute-start.23) | collective-permute-done | bytes 131104 | tf_op jit(solution)/shard_map/ppermute | solution.py:398
  108.7 4.8 %all-to-all-start.3 = ((bf16[16,160,128]{2,1,0:T(8,128)(2,1)}), bf16[16,160,128]{2,1,0:T(8,128)(2,1)S(1)}, u32[]{:S(2)}, u32[]{:S(2)}) async-start(bf16[16,160,128]{2,1,0:T(8,128)(2,1)} %get-tuple-element.85), calls=%async_computation.3 | async-start | bytes 1310720 | tf_op jit(solution)/shard_map/all_to_all | solution.py:519
  113.5 1.4 %collective-permute-start.20 = (bf16[64,1024]{1,0:T(8,128)(2,1)}, bf16[64,1024]{1,0:T(8,128)(2,1)S(1)}, u32[]{:S(2)}, u32[]{:S(2)}) collective-permute-start(bf16[64,1024]{1,0:T(8,128)(2,1)} %copy-done.6), channel_id=1, source_target_pairs={{0,32},{4,12},{8,40},{12,20},{16,48},{20,28},{24,56},{28,4},{32,64... | collective-permute-start | bytes 393224 | tf_op jit(solution)/shard_map/ppermute | solution.py:414
  114.9 2.4 %collective-permute-start.21 = (bf16[64,1024]{1,0:T(8,128)(2,1)}, bf16[64,1024]{1,0:T(8,128)(2,1)S(1)}, u32[]{:S(2)}, u32[]{:S(2)}) collective-permute-start(bf16[64,1024]{1,0:T(8,128)(2,1)} %copy-done.5), channel_id=1, source_target_pairs={{0,64},{4,20},{8,72},{12,28},{16,80},{20,4},{24,88},{28,12},{32,96... | collective-permute-start | bytes 393224 | tf_op jit(solution)/shard_map/ppermute | solution.py:414
  118.5 5.7 %all-to-all-done.3.refs_0_.refs_4_ = bf16[16,160,128]{2,1,0:T(8,128)(2,1)S(1)} async-done(((bf16[16,160,128]{2,1,0:T(8,128)(2,1)}), bf16[16,160,128]{2,1,0:T(8,128)(2,1)S(1)}, u32[]{:S(2)}, u32[]{:S(2)}) %all-to-all-start.3) | async-done | bytes 655392 | tf_op jit(solution)/shard_map/all_to_all | solution.py:519
  124.2 3.4 %collective-permute-start.28 = (bf16[16,16,128]{2,1,0:T(8,128)(2,1)S(1)}, bf16[16,16,128]{2,1,0:T(8,128)(2,1)S(1)}, u32[]{:S(2)}, u32[]{:S(2)}) collective-permute-start(bf16[16,16,128]{2,1,0:T(8,128)(2,1)S(1)} %get-tuple-element.86.refs_5_), channel_id=1, source_target_pairs={{0,4},{4,0},{8,12},{12,8},{16,20},{20,16},{24,28},{28,24},{32,36},... | collective-permute-start | bytes 196616 | tf_op jit(solution)/shard_map/ppermute | solution.py:406
  (68 shorter events, 18.0 us)
Async XLA Ops:
  2.8 25.7 %all-to-all-start = ((bf16[128,16,128]{2,1,0:T(8,128)(2,1)}), bf16[128,16,128]{2,1,0:T(8,128)(2,1)S(1)}, u32[]{:S(2)}, u32[]{:S(2)}) async-start(bf16[128,16,128]{2,1,0:T(8,128)(2,1)} %bitcast.2), calls=%async_computation | async-start | bytes 1048576 | tf_op jit(solution)/shard_map/all_to_all | solution.py:434
  14.3 7.2 %collective-permute-start.2 = (bf16[256,128]{1,0:T(8,128)(2,1)}, bf16[256,128]{1,0:T(8,128)(2,1)S(1)}, u32[]{:S(2)}, u32[]{:S(2)}) collective-permute-start(bf16[256,128]{1,0:T(8,128)(2,1)} %refs_0_.3), channel_id=1, source_target_pairs={{0,3},{1,0},{2,1},{3,2},{4,7},{5,4},{6,5},{7,6},{8,11},{9,8},{10,9... | collective-permute-start | bytes 196616 | tf_op jit(solution)/shard_map/ppermute | solution.py:398
  17.0 8.5 %collective-permute-start.1 = (bf16[256,128]{1,0:T(8,128)(2,1)}, bf16[256,128]{1,0:T(8,128)(2,1)S(1)}, u32[]{:S(2)}, u32[]{:S(2)}) collective-permute-start(bf16[256,128]{1,0:T(8,128)(2,1)} %refs_0_.3), channel_id=1, source_target_pairs={{0,2},{1,3},{2,0},{3,1},{4,6},{5,7},{6,4},{7,5},{8,10},{9,11},{10,... | collective-permute-start | bytes 196616 | tf_op jit(solution)/shard_map/ppermute | solution.py:398
  17.6 9.4 %collective-permute-start = (bf16[256,128]{1,0:T(8,128)(2,1)}, bf16[256,128]{1,0:T(8,128)(2,1)S(1)}, u32[]{:S(2)}, u32[]{:S(2)}) collective-permute-start(bf16[256,128]{1,0:T(8,128)(2,1)} %refs_0_.3), channel_id=1, source_target_pairs={{0,1},{1,2},{2,3},{3,0},{4,5},{5,6},{6,7},{7,4},{8,9},{9,10},{10,1... | collective-permute-start | bytes 196616 | tf_op jit(solution)/shard_map/ppermute | solution.py:398
  48.0 10.2 %collective-permute-start.4 = (bf16[128,512]{1,0:T(8,128)(2,1)S(1)}, bf16[128,512]{1,0:T(8,128)(2,1)S(1)}, u32[]{:S(2)}, u32[]{:S(2)}) collective-permute-start(bf16[128,512]{1,0:T(8,128)(2,1)S(1)} %get-tuple-element.55), channel_id=1, source_target_pairs={{0,2},{1,3},{2,0},{3,1},{4,6},{5,7},{6,4},{7,5},{8,10},{9,11},{10,... | collective-permute-start | bytes 393224 | tf_op jit(solution)/shard_map/ppermute | solution.py:398
  48.4 9.9 %collective-permute-start.5 = (bf16[128,512]{1,0:T(8,128)(2,1)S(1)}, bf16[128,512]{1,0:T(8,128)(2,1)S(1)}, u32[]{:S(2)}, u32[]{:S(2)}) collective-permute-start(bf16[128,512]{1,0:T(8,128)(2,1)S(1)} %get-tuple-element.56), channel_id=1, source_target_pairs={{0,3},{1,0},{2,1},{3,2},{4,7},{5,4},{6,5},{7,6},{8,11},{9,8},{10,9... | collective-permute-start | bytes 393224 | tf_op jit(solution)/shard_map/ppermute | solution.py:398
  50.9 7.4 %collective-permute-start.3 = (bf16[128,512]{1,0:T(8,128)(2,1)S(1)}, bf16[128,512]{1,0:T(8,128)(2,1)S(1)}, u32[]{:S(2)}, u32[]{:S(2)}) collective-permute-start(bf16[128,512]{1,0:T(8,128)(2,1)S(1)} %get-tuple-element.54.refs_4_), channel_id=1, source_target_pairs={{0,1},{1,2},{2,3},{3,0},{4,5},{5,6},{6,7},{7,4},{8,9},{9,10},{10,1... | collective-permute-start | bytes 393224 | tf_op jit(solution)/shard_map/ppermute | solution.py:398
  51.6 10.2 %collective-permute-start.6 = (bf16[128,512]{1,0:T(8,128)(2,1)S(1)}, bf16[128,512]{1,0:T(8,128)(2,1)S(1)}, u32[]{:S(2)}, u32[]{:S(2)}) collective-permute-start(bf16[128,512]{1,0:T(8,128)(2,1)S(1)} %get-tuple-element.61), channel_id=1, source_target_pairs={{0,1},{1,2},{2,3},{3,0},{4,5},{5,6},{6,7},{7,4},{8,9},{9,10},{10,1... | collective-permute-start | bytes 393224 | tf_op jit(solution)/shard_map/ppermute | solution.py:398
  51.8 11.5 %collective-permute-start.7 = (bf16[128,512]{1,0:T(8,128)(2,1)S(1)}, bf16[128,512]{1,0:T(8,128)(2,1)S(1)}, u32[]{:S(2)}, u32[]{:S(2)}) collective-permute-start(bf16[128,512]{1,0:T(8,128)(2,1)S(1)} %get-tuple-element.62), channel_id=1, source_target_pairs={{0,2},{1,3},{2,0},{3,1},{4,6},{5,7},{6,4},{7,5},{8,10},{9,11},{10,... | collective-permute-start | bytes 393224 | tf_op jit(solution)/shard_map/ppermute | solution.py:398
  58.2 5.1 %collective-permute-start.8 = (bf16[128,512]{1,0:T(8,128)(2,1)S(1)}, bf16[128,512]{1,0:T(8,128)(2,1)S(1)}, u32[]{:S(2)}, u32[]{:S(2)}) collective-permute-start(bf16[128,512]{1,0:T(8,128)(2,1)S(1)} %get-tuple-element.63), channel_id=1, source_target_pairs={{0,3},{1,0},{2,1},{3,2},{4,7},{5,4},{6,5},{7,6},{8,11},{9,8},{10,9... | collective-permute-start | bytes 393224 | tf_op jit(solution)/shard_map/ppermute | solution.py:398
  58.5 6.9 %collective-permute-start.13 = (bf16[128,512]{1,0:T(8,128)(2,1)S(1)}, bf16[128,512]{1,0:T(8,128)(2,1)S(1)}, u32[]{:S(2)}, u32[]{:S(2)}) collective-permute-start(bf16[128,512]{1,0:T(8,128)(2,1)S(1)} %slope.2.refs_0_), channel_id=1, source_target_pairs={{0,3},{1,0},{2,1},{3,2},{4,7},{5,4},{6,5},{7,6},{8,11},{9,8},{10,9... | collective-permute-start | bytes 393224 | tf_op jit(solution)/shard_map/ppermute | solution.py:398
  59.1 8.3 %collective-permute-start.11 = (bf16[128,512]{1,0:T(8,128)(2,1)S(1)}, bf16[128,512]{1,0:T(8,128)(2,1)S(1)}, u32[]{:S(2)}, u32[]{:S(2)}) collective-permute-start(bf16[128,512]{1,0:T(8,128)(2,1)S(1)} %slope.2.refs_0_), channel_id=1, source_target_pairs={{0,2},{1,3},{2,0},{3,1},{4,6},{5,7},{6,4},{7,5},{8,10},{9,11},{10,... | collective-permute-start | bytes 393224 | tf_op jit(solution)/shard_map/ppermute | solution.py:398
  61.8 6.1 %collective-permute-start.9 = (bf16[128,512]{1,0:T(8,128)(2,1)S(1)}, bf16[128,512]{1,0:T(8,128)(2,1)S(1)}, u32[]{:S(2)}, u32[]{:S(2)}) collective-permute-start(bf16[128,512]{1,0:T(8,128)(2,1)S(1)} %slope.2.refs_0_), channel_id=1, source_target_pairs={{0,1},{1,2},{2,3},{3,0},{4,5},{5,6},{6,7},{7,4},{8,9},{9,10},{10,1... | collective-permute-start | bytes 393224 | tf_op jit(solution)/shard_map/ppermute | solution.py:398
  63.4 7.0 %collective-permute-start.14 = (bf16[128,512]{1,0:T(8,128)(2,1)S(1)}, bf16[128,512]{1,0:T(8,128)(2,1)S(1)}, u32[]{:S(2)}, u32[]{:S(2)}) collective-permute-start(bf16[128,512]{1,0:T(8,128)(2,1)S(1)} %slope.3.refs_1_), channel_id=1, source_target_pairs={{0,3},{1,0},{2,1},{3,2},{4,7},{5,4},{6,5},{7,6},{8,11},{9,8},{10,9... | collective-permute-start | bytes 393224 | tf_op jit(solution)/shard_map/ppermute | solution.py:398
  64.7 5.8 %collective-permute-start.12 = (bf16[128,512]{1,0:T(8,128)(2,1)S(1)}, bf16[128,512]{1,0:T(8,128)(2,1)S(1)}, u32[]{:S(2)}, u32[]{:S(2)}) collective-permute-start(bf16[128,512]{1,0:T(8,128)(2,1)S(1)} %slope.3.refs_1_), channel_id=1, source_target_pairs={{0,2},{1,3},{2,0},{3,1},{4,6},{5,7},{6,4},{7,5},{8,10},{9,11},{10,... | collective-permute-start | bytes 393224 | tf_op jit(solution)/shard_map/ppermute | solution.py:398
  65.4 8.6 %collective-permute-start.10 = (bf16[128,512]{1,0:T(8,128)(2,1)S(1)}, bf16[128,512]{1,0:T(8,128)(2,1)S(1)}, u32[]{:S(2)}, u32[]{:S(2)}) collective-permute-start(bf16[128,512]{1,0:T(8,128)(2,1)S(1)} %slope.3.refs_1_), channel_id=1, source_target_pairs={{0,1},{1,2},{2,3},{3,0},{4,5},{5,6},{6,7},{7,4},{8,9},{9,10},{10,1... | collective-permute-start | bytes 393224 | tf_op jit(solution)/shard_map/ppermute | solution.py:398
  77.1 6.8 %collective-permute-start.15 = (bf16[4,256,512]{2,1,0:T(8,128)(2,1)}, bf16[4,256,512]{2,1,0:T(8,128)(2,1)S(1)}, u32[]{:S(2)}, u32[]{:S(2)}) collective-permute-start(bf16[4,256,512]{2,1,0:T(8,128)(2,1)} %get-tuple-element.66.refs_0_), channel_id=1, source_target_pairs={{0,4},{4,0},{8,12},{12,8},{16,20},{20,16},{24,28},{28,24},{32,36},... | collective-permute-start | bytes 3145736 | tf_op jit(solution)/shard_map/ppermute | solution.py:406
  78.9 5.0 %collective-permute-start.16 = (bf16[256,1024]{1,0:T(8,128)(2,1)S(1)}, bf16[256,1024]{1,0:T(8,128)(2,1)S(1)}, u32[]{:S(2)}, u32[]{:S(2)}) collective-permute-start(bf16[256,1024]{1,0:T(8,128)(2,1)S(1)} %copy-done.8), channel_id=1, source_target_pairs={{0,4},{4,0},{8,12},{12,8},{16,20},{20,16},{24,28},{28,24},{32,36},... | collective-permute-start | bytes 1572872 | tf_op jit(solution)/shard_map/ppermute | solution.py:406
  79.0 16.5 %all-to-all-start.2 = ((bf16[32,16,512]{2,1,0:T(8,128)(2,1)}), bf16[32,16,512]{2,1,0:T(8,128)(2,1)S(1)}, u32[]{:S(2)}, u32[]{:S(2)}) async-start(bf16[32,16,512]{2,1,0:T(8,128)(2,1)} %get-tuple-element.72), calls=%async_computation.2 | async-start | bytes 1048576 | tf_op jit(solution)/shard_map/all_to_all | solution.py:483
  88.8 12.1 %collective-permute-start.17 = (bf16[4,64,1024]{2,1,0:T(8,128)(2,1)}, bf16[4,64,1024]{2,1,0:T(8,128)(2,1)S(1)}, u32[]{:S(2)}, u32[]{:S(2)}) collective-permute-start(bf16[4,64,1024]{2,1,0:T(8,128)(2,1)} %get-tuple-element.69), channel_id=1, source_target_pairs={{0,8},{4,36},{8,16},{12,44},{16,24},{20,52},{24,0},{28,60},{32,40}... | collective-permute-start | bytes 1572872 | tf_op jit(solution)/shard_map/ppermute | solution.py:414
  90.3 15.1 %collective-permute-start.18 = (bf16[4,64,1024]{2,1,0:T(8,128)(2,1)}, bf16[4,64,1024]{2,1,0:T(8,128)(2,1)S(1)}, u32[]{:S(2)}, u32[]{:S(2)}) collective-permute-start(bf16[4,64,1024]{2,1,0:T(8,128)(2,1)} %get-tuple-element.70), channel_id=1, source_target_pairs={{0,16},{4,68},{8,24},{12,76},{16,0},{20,84},{24,8},{28,92},{32,48}... | collective-permute-start | bytes 1572872 | tf_op jit(solution)/shard_map/ppermute | solution.py:414
  92.7 12.7 %collective-permute-start.19 = (bf16[4,64,1024]{2,1,0:T(8,128)(2,1)}, bf16[4,64,1024]{2,1,0:T(8,128)(2,1)S(1)}, u32[]{:S(2)}, u32[]{:S(2)}) collective-permute-start(bf16[4,64,1024]{2,1,0:T(8,128)(2,1)} %get-tuple-element.71), channel_id=1, source_target_pairs={{0,24},{4,100},{8,0},{12,108},{16,8},{20,116},{24,16},{28,124},{32... | collective-permute-start | bytes 1572872 | tf_op jit(solution)/shard_map/ppermute | solution.py:414
  93.8 4.1 %collective-permute-start.27 = (bf16[256,512]{1,0:T(8,128)(2,1)}, bf16[256,512]{1,0:T(8,128)(2,1)S(1)}, u32[]{:S(2)}, u32[]{:S(2)}) collective-permute-start(bf16[256,512]{1,0:T(8,128)(2,1)} %get-tuple-element.84), channel_id=1, source_target_pairs={{0,4},{4,0},{8,12},{12,8},{16,20},{20,16},{24,28},{28,24},{32,36},... | collective-permute-start | bytes 786440 | tf_op jit(solution)/shard_map/ppermute | solution.py:406
  97.8 1.6 %collective-permute-start.26 = (bf16[256,512]{1,0:T(8,128)(2,1)S(1)}, bf16[256,512]{1,0:T(8,128)(2,1)S(1)}, u32[]{:S(2)}, u32[]{:S(2)}) collective-permute-start(bf16[256,512]{1,0:T(8,128)(2,1)S(1)} %get-tuple-element.83.refs_0_), channel_id=1, source_target_pairs={{0,4},{4,0},{8,12},{12,8},{16,20},{20,16},{24,28},{28,24},{32,36},... | collective-permute-start | bytes 786440 | tf_op jit(solution)/shard_map/ppermute | solution.py:406
  97.9 8.4 %collective-permute-start.24 = (bf16[256,256]{1,0:T(8,128)(2,1)S(1)}, bf16[256,256]{1,0:T(8,128)(2,1)S(1)}, u32[]{:S(2)}, u32[]{:S(2)}) collective-permute-start(bf16[256,256]{1,0:T(8,128)(2,1)S(1)} %get-tuple-element.81), channel_id=1, source_target_pairs={{0,2},{1,3},{2,0},{3,1},{4,6},{5,7},{6,4},{7,5},{8,10},{9,11},{10,... | collective-permute-start | bytes 393224 | tf_op jit(solution)/shard_map/ppermute | solution.py:398
  99.4 6.9 %collective-permute-start.25 = (bf16[256,256]{1,0:T(8,128)(2,1)S(1)}, bf16[256,256]{1,0:T(8,128)(2,1)S(1)}, u32[]{:S(2)}, u32[]{:S(2)}) collective-permute-start(bf16[256,256]{1,0:T(8,128)(2,1)S(1)} %get-tuple-element.82), channel_id=1, source_target_pairs={{0,3},{1,0},{2,1},{3,2},{4,7},{5,4},{6,5},{7,6},{8,11},{9,8},{10,9... | collective-permute-start | bytes 393224 | tf_op jit(solution)/shard_map/ppermute | solution.py:398
  100.9 6.8 %collective-permute-start.23 = (bf16[256,256]{1,0:T(8,128)(2,1)S(1)}, bf16[256,256]{1,0:T(8,128)(2,1)S(1)}, u32[]{:S(2)}, u32[]{:S(2)}) collective-permute-start(bf16[256,256]{1,0:T(8,128)(2,1)S(1)} %get-tuple-element.75.refs_4_), channel_id=1, source_target_pairs={{0,1},{1,2},{2,3},{3,0},{4,5},{5,6},{6,7},{7,4},{8,9},{9,10},{10,1... | collective-permute-start | bytes 393224 | tf_op jit(solution)/shard_map/ppermute | solution.py:398
  108.7 15.5 %all-to-all-start.3 = ((bf16[16,160,128]{2,1,0:T(8,128)(2,1)}), bf16[16,160,128]{2,1,0:T(8,128)(2,1)S(1)}, u32[]{:S(2)}, u32[]{:S(2)}) async-start(bf16[16,160,128]{2,1,0:T(8,128)(2,1)} %get-tuple-element.85), calls=%async_computation.3 | async-start | bytes 1310720 | tf_op jit(solution)/shard_map/all_to_all | solution.py:519
  113.5 14.0 %collective-permute-start.20 = (bf16[64,1024]{1,0:T(8,128)(2,1)}, bf16[64,1024]{1,0:T(8,128)(2,1)S(1)}, u32[]{:S(2)}, u32[]{:S(2)}) collective-permute-start(bf16[64,1024]{1,0:T(8,128)(2,1)} %copy-done.6), channel_id=1, source_target_pairs={{0,32},{4,12},{8,40},{12,20},{16,48},{20,28},{24,56},{28,4},{32,64... | collective-permute-start | bytes 393224 | tf_op jit(solution)/shard_map/ppermute | solution.py:414
  114.9 12.8 %collective-permute-start.21 = (bf16[64,1024]{1,0:T(8,128)(2,1)}, bf16[64,1024]{1,0:T(8,128)(2,1)S(1)}, u32[]{:S(2)}, u32[]{:S(2)}) collective-permute-start(bf16[64,1024]{1,0:T(8,128)(2,1)} %copy-done.5), channel_id=1, source_target_pairs={{0,64},{4,20},{8,72},{12,28},{16,80},{20,4},{24,88},{28,12},{32,96... | collective-permute-start | bytes 393224 | tf_op jit(solution)/shard_map/ppermute | solution.py:414
  117.3 10.4 %collective-permute-start.22 = (bf16[64,1024]{1,0:T(8,128)(2,1)S(1)}, bf16[64,1024]{1,0:T(8,128)(2,1)S(1)}, u32[]{:S(2)}, u32[]{:S(2)}) collective-permute-start(bf16[64,1024]{1,0:T(8,128)(2,1)S(1)} %get-tuple-element.79), channel_id=1, source_target_pairs={{0,96},{4,28},{8,104},{12,4},{16,112},{20,12},{24,120},{28,20},{32... | collective-permute-start | bytes 393224 | tf_op jit(solution)/shard_map/ppermute | solution.py:414
  124.2 4.4 %collective-permute-start.28 = (bf16[16,16,128]{2,1,0:T(8,128)(2,1)S(1)}, bf16[16,16,128]{2,1,0:T(8,128)(2,1)S(1)}, u32[]{:S(2)}, u32[]{:S(2)}) collective-permute-start(bf16[16,16,128]{2,1,0:T(8,128)(2,1)S(1)} %get-tuple-element.86.refs_5_), channel_id=1, source_target_pairs={{0,4},{4,0},{8,12},{12,8},{16,20},{20,16},{24,28},{28,24},{32,36},... | collective-permute-start | bytes 196616 | tf_op jit(solution)/shard_map/ppermute | solution.py:406
  (9 other events, 162.9 us)

commit v6 on v5

--- a/solution.py
+++ b/solution.py
@@ -126,7 +126,7 @@
     saved_ref[...] = stacked_ref[...]
     pre = mm(both_ref[...], w1_ref[...])
     sig = 1.0 / (1.0 + jnp.exp(-pre))
-    slope_ref[...] = sig * (1.0 + pre * (1.0 - sig))
+    slope_ref[...] = (sig * (1.0 + pre * (1.0 - sig))).astype(slope_ref.dtype)
 
 
 def second_kernel(
@@ -187,7 +187,7 @@
         return total
 
     mean = (back(UNITS) * wide(inv_ref[...], UNITS)).astype(BF16)
-    own_ref[...] = back(0) + mm(adjt_ref[:ROWS, :], mean)
+    own_ref[...] = (back(0) + mm(adjt_ref[:ROWS, :], mean)).astype(BF16)
     copies.append(pltpu.make_async_copy(own_ref, own_hbm, sems.at[8]))
     copies[-1].start()
     halo_ref[...] = mm(adjt_ref[ROWS:, :], mean).astype(BF16).reshape(PEERS, SLOTS, UNITS)
@@ -252,8 +252,8 @@
     place, back_ref, own_ref, slope_ref, selt_ref, w_ref, grad_ref, mine_ref, s1, s2, s3, full_ref
 ):
     me = place.hid
-    grad = own_ref[...] + mm(selt_ref[...], back_ref[...].reshape(FAR, UNITS))
-    grad = (grad * slope_ref[...]).astype(BF16)
+    grad = own_ref[...].astype(F32) + mm(selt_ref[...], back_ref[...].reshape(FAR, UNITS))
+    grad = (grad * slope_ref[...].astype(F32)).astype(BF16)
     grad_ref[...] = grad
     full_ref[...] = mm_last(grad, w_ref[...])
     for d, out in ((2, s2), (1, s1), (3, s3), (0, mine_ref)):
@@ -434,7 +434,7 @@
     far_feat = lax.all_to_all(
         send_feat.reshape(PEERS * HID, SLOTS, LANES), ("nodes", "hid"), 0, 0, tiled=True
     ).reshape(PEERS, HID, SLOTS, LANES)
-    f2, f1, f3 = around([(2, features), (1, features), (3, features)])
+    f1, f3, f2 = around([(1, features), (3, features), (2, features)])
     adj, adjt, inv = call(
         count_kernel, "count", (jnp.swapaxes(neighbors, 0, 1), degree.reshape(1, ROWS)),
         [((ROWS, ROWS + FAR), BF16), ((ROWS + FAR, ROWS), BF16), ((ROWS, LANES), F32)],
@@ -452,12 +452,12 @@
         [((ROWS, 2 * UNITS), BF16)] + [((ROWS // 2, UNITS), F32)] * 2 + [half_chunk] * 6,
         placed=True, work=10,
     )
-    r2a, r1a, r3a = around([(2, s2a), (1, s1a), (3, s3a)])
-    r2b, r1b, r3b = around([(2, s2b), (1, s1b), (3, s3b)])
+    r1a, r3a, r2a = around([(1, s1a), (3, s3a), (2, s2a)])
+    r1b, r3b, r2b = around([(1, s1b), (3, s3b), (2, s2b)])
     slope, saved, selt = call(
         gate_kernel, "gate", (both, stacked, w1, routes),
-        [wide_chunk, ((ROWS, 2 * UNITS), BF16), ((ROWS, FAR), BF16)],
-        after=(s1a,), late=(2, 3), stored=(0, 1, 2), work=2,
+        [chunk, ((ROWS, 2 * UNITS), BF16), ((ROWS, FAR), BF16)],
+        after=(s1a,), late=(3,), stored=(0, 1, 2), work=2,
     )
     saved_mate = swap(saved)
     def gradient(first_row, own, parts):
@@ -467,9 +467,9 @@
         )
 
     g0a = gradient(0, own_a, (r1a, r2a, r3a))
-    g2a, g1a, g3a = around([(2, g0a), (1, g0a), (3, g0a)])
+    g1a, g3a, g2a = around([(1, g0a), (3, g0a), (2, g0a)])
     g0b = gradient(ROWS // 2, own_b, (r1b, r2b, r3b))
-    g2b, g1b, g3b = around([(2, g0b), (1, g0b), (3, g0b)])
+    g1b, g3b, g2b = around([(1, g0b), (3, g0b), (2, g0b)])
 
     mine_rows, give_rows = call(
         choose_kernel, "choose", (both,), [chunk, chunk], placed=True, stored=(0, 1), work=4, after=(g0b,),
@@ -477,8 +477,8 @@
     mate_rows = swap(give_rows)
     halo_hidden, own_hidden, others = call(
         spread_kernel, "spread", (g0a, g0b, g1a, g1b, g2a, g2b, g3a, g3b, w2, inv, adjt),
-        [halo, wide_chunk, ((HID, ROWS, UNITS), BF16)], placed=True, work=10, loose=(1, 2), after=(in_hbm(mine_rows),),
-        scratch=[pltpu.VMEM((ROWS, UNITS), F32), pltpu.SemaphoreType.DMA((9,))],
+        [halo, chunk, ((HID, ROWS, UNITS), BF16)], placed=True, work=10, loose=(1, 2), after=(in_hbm(mine_rows),),
+        scratch=[pltpu.VMEM((ROWS, UNITS), BF16), pltpu.SemaphoreType.DMA((9,))],
     )
     back_hidden = lax.all_to_all(halo_hidden, "nodes", 0, 0, tiled=True)
     slots = (0, 1, 2, 3)
@@ -498,9 +498,9 @@
         settle_kernel, "settle",
         (back_hidden, own_hidden, slope, selt, w1),
         [chunk, ((ROWS, 2 * LANES), F32)] + [((ROWS, 2 * LANES), BF16)] * 3,
-        scratch=[pltpu.VMEM((ROWS, 2 * UNITS), F32)], placed=True, late=(3, 1, 2, 4), work=6, after=(outer_done,),
-    )
-    r2, r1, r3 = around([(2, s2), (1, s1), (3, s3)])
+        scratch=[pltpu.VMEM((ROWS, 2 * UNITS), F32)], placed=True, late=(3, 1, 2, 4), work=40, after=(outer_done,),
+    )
+    r1, r3, r2 = around([(1, s1), (3, s3), (2, s2)])
     merged = call(
         outer_first_kernel, "outer_first", (grad, swap(grad), mine_rows, mate_rows),
         [((CHIPS, LANES + 2 * SLOTS, LANES), BF16)], after=(s1,), late=(2,), stored=(0,), work=2,

time: 130 us -> 130 us (level)
    ppermute x18, waiting for transfers between devices: 15.1 us -> 13.2 us  [around(): lax.ppermute(v, 'hid', [(i, (i + d) % HID) for i in range(HID)])]
where the time goes in v6:
time: 130 us; the launch traced here: 129 us
  starting transfers between devices  57.8 us (44%)
  Pallas kernels  27 us (21%)
  waiting for transfers between devices  25.8 us (20%)
  blocking collectives  17 us (13%)
  between operations  1.57 us (1%)
    pallas_call x17, Pallas kernels, call(): pl.pallas_call(body, out_shape=shapes, in_specs=in_specs, out_specs=out_s...  27 us
    ppermute x18, starting transfers between devices, around(): lax.ppermute(v, 'hid', [(i, (i + d) % HID) for i in range(HID)])  19.5 us
    all_to_all x1, blocking collectives, on_device(): far_hidden = lax.all_to_all(send_hidden, 'nodes', 0, 0, tiled=True)  17 us
    ppermute x18, waiting for transfers between devices, around(): lax.ppermute(v, 'hid', [(i, (i + d) % HID) for i in range(HID)])  13.2 us
    all_to_all x1, starting transfers between devices, on_device(): lax.all_to_all(send_feat.reshape(PEERS * HID, SLOTS, LANES), ('nodes', 'h...  11.5 us
    ppermute x6, starting transfers between devices, near(): lax.ppermute(v, 'nodes', [(node_at(x, z, c), target(x, z, c, d)) for x in...  10.1 us
    ppermute x5, starting transfers between devices, swap(): return lax.ppermute(value, 'nodes', [(i, i ^ 1) for i in range(PEERS)])  6.41 us
    all_to_all x1, waiting for transfers between devices, on_device(): lax.all_to_all(merged, 'nodes', 0, 0, tiled=True, axis_index_groups=same_...  6.19 us
  transfers between devices with their start and end apart: 32, of which 14 were waited for; matrix products, arithmetic and copies ran while one was open for 0% of the time, Pallas kernels for 14%

profile of v6, /device:TPU:1, one launch (start us, length us, event | category | flops | bytes accessed | tf_op | source)
XLA Modules:
  0.0 129.1 jit_solution(8311429742209641500)
XLA Ops:
  0.7 2.1 %pick.1 = (bf16[512,256]{1,0:T(8,128)(2,1)S(1)}, bf16[32,4,16,128]{3,2,1,0:T(8,128)(2,1)}) custom-call(s32[16,32]{1,0:T(8,128)} %bitcast.15, bf16[256,128]{1,0:T(8,128)(2,1)} %refs_0_.3), custom_call_target="tpu_custom_call" | custom-call | flops 134217728 | bytes 854016 | tf_op jit(solution)/shard_map/pick/pallas_call | solution.py:383
  2.8 11.5 %all-to-all-start = ((bf16[128,16,128]{2,1,0:T(8,128)(2,1)}), bf16[128,16,128]{2,1,0:T(8,128)(2,1)S(1)}, u32[]{:S(2)}, u32[]{:S(2)}) async-start(bf16[128,16,128]{2,1,0:T(8,128)(2,1)} %bitcast.2), calls=%async_computation | async-start | bytes 1048576 | tf_op jit(solution)/shard_map/all_to_all | solution.py:434
  14.3 2.7 %collective-permute-start.2 = (bf16[256,128]{1,0:T(8,128)(2,1)}, bf16[256,128]{1,0:T(8,128)(2,1)S(1)}, u32[]{:S(2)}, u32[]{:S(2)}) collective-permute-start(bf16[256,128]{1,0:T(8,128)(2,1)} %refs_0_.3), channel_id=1, source_target_pairs={{0,3},{1,0},{2,1},{3,2},{4,7},{5,4},{6,5},{7,6},{8,11},{9,8},{10,9... | collective-permute-start | bytes 196616 | tf_op jit(solution)/shard_map/ppermute | solution.py:398
  18.1 3.2 %count.1 = (bf16[256,768]{1,0:T(8,128)(2,1)S(1)}, bf16[768,256]{1,0:T(8,128)(2,1)S(1)}, f32[256,128]{1,0:T(8,128)S(1)}) custom-call(s32[80,256]{1,0:T(8,128)} %bitcast.17, s32[1,256]{1,0:T(1,128)} %bitcast.18, bf16[512,256]{1,0:T(8,128)(2,1)S(1)} %get-tuple-element.48.refs_2_.refs_8_), custom_call_target="tpu_custom_call" | custom-call | flops 1073741824 | bytes 1000448 | tf_op jit(solution)/shard_map/count/pallas_call | solution.py:383
  21.5 4.1 %collective-permute-done.1.refs_2_ = bf16[256,128]{1,0:T(8,128)(2,1)S(1)} collective-permute-done((bf16[256,128]{1,0:T(8,128)(2,1)}, bf16[256,128]{1,0:T(8,128)(2,1)S(1)}, u32[]{:S(2)}, u32[]{:S(2)}) %collective-permute-start.1) | collective-permute-done | bytes 65568 | tf_op jit(solution)/shard_map/ppermute | solution.py:398
  25.5 1.4 %collective-permute-done.refs_1_ = bf16[256,128]{1,0:T(8,128)(2,1)S(1)} collective-permute-done((bf16[256,128]{1,0:T(8,128)(2,1)}, bf16[256,128]{1,0:T(8,128)(2,1)S(1)}, u32[]{:S(2)}, u32[]{:S(2)}) %collective-permute-start) | collective-permute-done | bytes 65568 | tf_op jit(solution)/shard_map/ppermute | solution.py:398
  27.0 1.5 %all-to-all-done = bf16[128,16,128]{2,1,0:T(8,128)(2,1)S(1)} async-done(((bf16[128,16,128]{2,1,0:T(8,128)(2,1)}), bf16[128,16,128]{2,1,0:T(8,128)(2,1)S(1)}, u32[]{:S(2)}, u32[]{:S(2)}) %all-to-all-start) | async-done | bytes 524320 | tf_op jit(solution)/shard_map/all_to_all | solution.py:434
  29.5 17.0 %all_to_all.20.refs_1_ = bf16[32,16,512]{2,1,0:T(8,128)(2,1)S(1)} all-to-all(bf16[32,16,512]{2,1,0:T(8,128)(2,1)S(1)} %get-tuple-element.52), channel_id=1, replica_groups=mesh['nodes'=32,'hid'=4] {'nodes'}, dimensions={0} | all-to-all | bytes 1048576 | tf_op jit(solution)/shard_map/all_to_all | solution.py:448
  46.5 1.5 %second.1 = (bf16[256,1024]{1,0:T(8,128)(2,1)S(1)}, f32[128,512]{1,0:T(8,128)S(1)}, f32[128,512]{1,0:T(8,128)S(1)}, bf16[128,512]{1,0:T(8,128)(2,1)S(1)}, bf16[1...) custom-call(bf16[256,512]{1,0:T(8,128)(2,1)S(1)} %get-tuple-element., ...), custom_call_target="tpu_custom_call" | custom-call | flops 1342177280 | bytes 7340032 | tf_op jit(solution)/shard_map/second/pallas_call | solution.py:383
  48.4 2.5 %collective-permute-start.5 = (bf16[128,512]{1,0:T(8,128)(2,1)S(1)}, bf16[128,512]{1,0:T(8,128)(2,1)S(1)}, u32[]{:S(2)}, u32[]{:S(2)}) collective-permute-start(bf16[128,512]{1,0:T(8,128)(2,1)S(1)} %get-tuple-element.56), channel_id=1, source_target_pairs={{0,3},{1,0},{2,1},{3,2},{4,7},{5,4},{6,5},{7,6},{8,11},{9,8},{10,9... | collective-permute-start | bytes 393224 | tf_op jit(solution)/shard_map/ppermute | solution.py:398
  51.8 3.7 %collective-permute-start.7 = (bf16[128,512]{1,0:T(8,128)(2,1)S(1)}, bf16[128,512]{1,0:T(8,128)(2,1)S(1)}, u32[]{:S(2)}, u32[]{:S(2)}) collective-permute-start(bf16[128,512]{1,0:T(8,128)(2,1)S(1)} %get-tuple-element.62), channel_id=1, source_target_pairs={{0,2},{1,3},{2,0},{3,1},{4,6},{5,7},{6,4},{7,5},{8,10},{9,11},{10,... | collective-permute-start | bytes 393224 | tf_op jit(solution)/shard_map/ppermute | solution.py:398
  55.5 2.2 %gate.1 = (bf16[256,512]{1,0:T(8,128)(2,1)}, bf16[256,1024]{1,0:T(8,128)(2,1)}, bf16[256,512]{1,0:T(8,128)(2,1)}) custom-call(bf16[256,1024]{1,0:T(8,128)(2,1)S(1)} %get-tuple-element.57.refs_0_, bf16[256,1024]{1,0:T(8,128)(2,1)S(1)} %get-tuple-element.58.refs_1_, bf16[1024,512]{1,0:T(8,128)(2,1)S(1)} %bitcast.13, s32[16,32]{1,0:T(8,128)} %bitcast.16, ...), custom_call_target="tpu_custom_call" | custom-call | flops 268435456 | bytes 3147776 | tf_op jit(solution)/shard_map/gate/pallas_call | solution.py:383
  59.1 2.2 %collective-permute-start.11 = (bf16[128,512]{1,0:T(8,128)(2,1)S(1)}, bf16[128,512]{1,0:T(8,128)(2,1)S(1)}, u32[]{:S(2)}, u32[]{:S(2)}) collective-permute-start(bf16[128,512]{1,0:T(8,128)(2,1)S(1)} %slope.2.refs_0_), channel_id=1, source_target_pairs={{0,2},{1,3},{2,0},{3,1},{4,6},{5,7},{6,4},{7,5},{8,10},{9,11},{10,... | collective-permute-start | bytes 393224 | tf_op jit(solution)/shard_map/ppermute | solution.py:398
  61.3 1.9 %collective-permute-done.7.refs_3_ = bf16[128,512]{1,0:T(8,128)(2,1)S(1)} collective-permute-done((bf16[128,512]{1,0:T(8,128)(2,1)S(1)}, bf16[128,512]{1,0:T(8,128)(2,1)S(1)}, u32[]{:S(2)}, u32[]{:S(2)}) %collective-permute-start.7) | collective-permute-done | bytes 131104 | tf_op jit(solution)/shard_map/ppermute | solution.py:398
  64.2 1.6 %collective-permute-start.12 = (bf16[128,512]{1,0:T(8,128)(2,1)S(1)}, bf16[128,512]{1,0:T(8,128)(2,1)S(1)}, u32[]{:S(2)}, u32[]{:S(2)}) collective-permute-start(bf16[128,512]{1,0:T(8,128)(2,1)S(1)} %slope.3.refs_1_), channel_id=1, source_target_pairs={{0,2},{1,3},{2,0},{3,1},{4,6},{5,7},{6,4},{7,5},{8,10},{9,11},{10,... | collective-permute-start | bytes 393224 | tf_op jit(solution)/shard_map/ppermute | solution.py:398
  67.9 1.9 %collective-permute-done.14.refs_7_ = bf16[128,512]{1,0:T(8,128)(2,1)S(1)} collective-permute-done((bf16[128,512]{1,0:T(8,128)(2,1)S(1)}, bf16[128,512]{1,0:T(8,128)(2,1)S(1)}, u32[]{:S(2)}, u32[]{:S(2)}) %collective-permute-start.14) | collective-permute-done | bytes 131104 | tf_op jit(solution)/shard_map/ppermute | solution.py:398
  70.3 2.1 %collective-permute-done.10.refs_3_ = bf16[128,512]{1,0:T(8,128)(2,1)S(1)} collective-permute-done((bf16[128,512]{1,0:T(8,128)(2,1)S(1)}, bf16[128,512]{1,0:T(8,128)(2,1)S(1)}, u32[]{:S(2)}, u32[]{:S(2)}) %collective-permute-start.10) | collective-permute-done | bytes 131104 | tf_op jit(solution)/shard_map/ppermute | solution.py:398
  72.4 2.9 %spread.1 = (bf16[32,16,512]{2,1,0:T(8,128)(2,1)}, bf16[256,512]{1,0:T(8,128)(2,1)}, bf16[4,256,512]{2,1,0:T(8,128)(2,1)}) custom-call(bf16[128,512]{1,0:T(8,128)(2,1)S(1)} %slope.2.refs_0_, bf16[128,512]{1,0:T(8,128)(2,1)S(1)} %slope.3.refs_1_, bf16[128,512]{1,0:T(8,128)(2,1)S(1)} %collective-permute-done.9.refs_2_, ...), custom_call_target="tpu_custom_call" | custom-call | flops 1342177280 | bytes 7602176 | tf_op jit(solution)/shard_map/spread/pallas_call | solution.py:383
  75.3 3.0 %collective-permute-start.15 = (bf16[4,256,512]{2,1,0:T(8,128)(2,1)}, bf16[4,256,512]{2,1,0:T(8,128)(2,1)S(1)}, u32[]{:S(2)}, u32[]{:S(2)}) collective-permute-start(bf16[4,256,512]{2,1,0:T(8,128)(2,1)} %get-tuple-element.66.refs_0_), channel_id=1, source_target_pairs={{0,4},{4,0},{8,12},{12,8},{16,20},{20,16},{24,28},{28,24},{32,36},... | collective-permute-start | bytes 3145736 | tf_op jit(solution)/shard_map/ppermute | solution.py:406
  78.4 5.3 %all-to-all-start.2 = ((bf16[32,16,512]{2,1,0:T(8,128)(2,1)}), bf16[32,16,512]{2,1,0:T(8,128)(2,1)S(1)}, u32[]{:S(2)}, u32[]{:S(2)}) async-start(bf16[32,16,512]{2,1,0:T(8,128)(2,1)} %get-tuple-element.72), calls=%async_computation.2 | async-start | bytes 1048576 | tf_op jit(solution)/shard_map/all_to_all | solution.py:483
  84.0 4.9 %outer_second.1 = (bf16[4,64,1024]{2,1,0:T(8,128)(2,1)}, bf16[4,64,1024]{2,1,0:T(8,128)(2,1)}, bf16[4,64,1024]{2,1,0:T(8,128)(2,1)}, bf16[4,64,1024]{2,1,0:T(8,128)(2,1)}) custom-call(bf16[4,256,512]{2,1,0:T(8,128)(2,1)} %get-tuple-element.66.refs_0_, bf16[4,256,512]{2,1,0:T(8,128)(2,1)S(1)} %collective-permute-done.15.refs_1_, ...), custom_call_target="tpu_custom_call" | custom-call | flops 1610612736 | bytes 5242880 | tf_op jit(solution)/shard_map/outer_second/pallas_call | solution.py:383
  88.9 1.6 %collective-permute-start.17 = (bf16[4,64,1024]{2,1,0:T(8,128)(2,1)}, bf16[4,64,1024]{2,1,0:T(8,128)(2,1)S(1)}, u32[]{:S(2)}, u32[]{:S(2)}) collective-permute-start(bf16[4,64,1024]{2,1,0:T(8,128)(2,1)} %get-tuple-element.69), channel_id=1, source_target_pairs={{0,8},{4,36},{8,16},{12,44},{16,24},{20,52},{24,0},{28,60},{32,40}... | collective-permute-start | bytes 1572872 | tf_op jit(solution)/shard_map/ppermute | solution.py:414
  90.5 2.4 %collective-permute-start.18 = (bf16[4,64,1024]{2,1,0:T(8,128)(2,1)}, bf16[4,64,1024]{2,1,0:T(8,128)(2,1)S(1)}, u32[]{:S(2)}, u32[]{:S(2)}) collective-permute-start(bf16[4,64,1024]{2,1,0:T(8,128)(2,1)} %get-tuple-element.70), channel_id=1, source_target_pairs={{0,16},{4,68},{8,24},{12,76},{16,0},{20,84},{24,8},{28,92},{32,48}... | collective-permute-start | bytes 1572872 | tf_op jit(solution)/shard_map/ppermute | solution.py:414
  94.1 1.3 %all-to-all-done.2.refs_0_ = bf16[32,16,512]{2,1,0:T(8,128)(2,1)S(1)} async-done(((bf16[32,16,512]{2,1,0:T(8,128)(2,1)}), bf16[32,16,512]{2,1,0:T(8,128)(2,1)S(1)}, u32[]{:S(2)}, u32[]{:S(2)}) %all-to-all-start.2) | async-done | bytes 524320 | tf_op jit(solution)/shard_map/all_to_all | solution.py:483
  95.5 2.2 %settle.1 = (bf16[256,512]{1,0:T(8,128)(2,1)S(1)}, f32[256,256]{1,0:T(8,128)S(1)}, bf16[256,256]{1,0:T(8,128)(2,1)S(1)}, bf16[256,256]{1,0:T(8,128)(2,1)S(1)}, bf16[256,256]{1,0:T(8,128)(2,1)S(1)}) custom-call(bf16[32,16,512]{2,1,0:T(8,128)(2,1)S(1)} %all-to-all-done.2.refs_0_, bf16[256,512]{1,0:T(8,128)(2,1)} %get-tuple-element.73.refs_1_, ...), custom_call_target="tpu_custom_call" | custom-call | flops 5368709120 | bytes 3276800 | tf_op jit(solution)/shard_map/settle/pallas_call | solution.py:383
  100.7 2.3 %outer_first.1.refs_6_ = bf16[16,160,128]{2,1,0:T(8,128)(2,1)} custom-call(bf16[256,512]{1,0:T(8,128)(2,1)S(1)} %get-tuple-element.83.refs_0_, bf16[256,512]{1,0:T(8,128)(2,1)S(1)} %collective-permute-done.26.refs_1_, bf16[256,512]{1,0:T(8,128)(2,1)} %get-tuple-element.65.refs_11_.refs_2_, bf16[256,512]{1,0:T(8,128)(2,1)S(1)} %collective-permute-done.27.refs_3_, ...), custom_call_target="tpu_custom_call" | custom-call | flops 268435456 | bytes 1703936 | tf_op jit(solution)/shard_map/outer_first/pallas_call | solution.py:383
  103.0 2.6 %collective-permute-done.18.refs_2_ = bf16[4,64,1024]{2,1,0:T(8,128)(2,1)S(1)} collective-permute-done((bf16[4,64,1024]{2,1,0:T(8,128)(2,1)}, bf16[4,64,1024]{2,1,0:T(8,128)(2,1)S(1)}, u32[]{:S(2)}, u32[]{:S(2)}) %collective-permute-start.18) | collective-permute-done | bytes 524320 | tf_op jit(solution)/shard_map/ppermute | solution.py:414
  108.1 5.0 %all-to-all-start.3 = ((bf16[16,160,128]{2,1,0:T(8,128)(2,1)}), bf16[16,160,128]{2,1,0:T(8,128)(2,1)S(1)}, u32[]{:S(2)}, u32[]{:S(2)}) async-start(bf16[16,160,128]{2,1,0:T(8,128)(2,1)} %get-tuple-element.85), calls=%async_computation.3 | async-start | bytes 1310720 | tf_op jit(solution)/shard_map/all_to_all | solution.py:519
  113.1 1.4 %collective-permute-start.20 = (bf16[64,1024]{1,0:T(8,128)(2,1)S(1)}, bf16[64,1024]{1,0:T(8,128)(2,1)S(1)}, u32[]{:S(2)}, u32[]{:S(2)}) collective-permute-start(bf16[64,1024]{1,0:T(8,128)(2,1)S(1)} %get-tuple-element.77), channel_id=1, source_target_pairs={{0,32},{4,12},{8,40},{12,20},{16,48},{20,28},{24,56},{28,4},{32,64... | collective-permute-start | bytes 393224 | tf_op jit(solution)/shard_map/ppermute | solution.py:414
  114.5 2.4 %collective-permute-start.21 = (bf16[64,1024]{1,0:T(8,128)(2,1)S(1)}, bf16[64,1024]{1,0:T(8,128)(2,1)S(1)}, u32[]{:S(2)}, u32[]{:S(2)}) collective-permute-start(bf16[64,1024]{1,0:T(8,128)(2,1)S(1)} %get-tuple-element.78), channel_id=1, source_target_pairs={{0,64},{4,20},{8,72},{12,28},{16,80},{20,4},{24,88},{28,12},{32,96... | collective-permute-start | bytes 393224 | tf_op jit(solution)/shard_map/ppermute | solution.py:414
  118.1 6.2 %all-to-all-done.3.refs_0_.refs_4_ = bf16[16,160,128]{2,1,0:T(8,128)(2,1)S(1)} async-done(((bf16[16,160,128]{2,1,0:T(8,128)(2,1)}), bf16[16,160,128]{2,1,0:T(8,128)(2,1)S(1)}, u32[]{:S(2)}, u32[]{:S(2)}) %all-to-all-start.3) | async-done | bytes 655392 | tf_op jit(solution)/shard_map/all_to_all | solution.py:519
  124.3 2.9 %collective-permute-start.28 = (bf16[16,16,128]{2,1,0:T(8,128)(2,1)S(1)}, bf16[16,16,128]{2,1,0:T(8,128)(2,1)S(1)}, u32[]{:S(2)}, u32[]{:S(2)}) collective-permute-start(bf16[16,16,128]{2,1,0:T(8,128)(2,1)S(1)} %get-tuple-element.86.refs_5_), channel_id=1, source_target_pairs={{0,4},{4,0},{8,12},{12,8},{16,20},{20,16},{24,28},{28,24},{32,36},... | collective-permute-start | bytes 196616 | tf_op jit(solution)/shard_map/ppermute | solution.py:406
  (64 shorter events, 18.0 us)
Async XLA Ops:
  2.8 25.7 %all-to-all-start = ((bf16[128,16,128]{2,1,0:T(8,128)(2,1)}), bf16[128,16,128]{2,1,0:T(8,128)(2,1)S(1)}, u32[]{:S(2)}, u32[]{:S(2)}) async-start(bf16[128,16,128]{2,1,0:T(8,128)(2,1)} %bitcast.2), calls=%async_computation | async-start | bytes 1048576 | tf_op jit(solution)/shard_map/all_to_all | solution.py:434
  14.3 7.2 %collective-permute-start.2 = (bf16[256,128]{1,0:T(8,128)(2,1)}, bf16[256,128]{1,0:T(8,128)(2,1)S(1)}, u32[]{:S(2)}, u32[]{:S(2)}) collective-permute-start(bf16[256,128]{1,0:T(8,128)(2,1)} %refs_0_.3), channel_id=1, source_target_pairs={{0,3},{1,0},{2,1},{3,2},{4,7},{5,4},{6,5},{7,6},{8,11},{9,8},{10,9... | collective-permute-start | bytes 196616 | tf_op jit(solution)/shard_map/ppermute | solution.py:398
  17.0 8.5 %collective-permute-start.1 = (bf16[256,128]{1,0:T(8,128)(2,1)}, bf16[256,128]{1,0:T(8,128)(2,1)S(1)}, u32[]{:S(2)}, u32[]{:S(2)}) collective-permute-start(bf16[256,128]{1,0:T(8,128)(2,1)} %refs_0_.3), channel_id=1, source_target_pairs={{0,2},{1,3},{2,0},{3,1},{4,6},{5,7},{6,4},{7,5},{8,10},{9,11},{10,... | collective-permute-start | bytes 196616 | tf_op jit(solution)/shard_map/ppermute | solution.py:398
  17.5 9.4 %collective-permute-start = (bf16[256,128]{1,0:T(8,128)(2,1)}, bf16[256,128]{1,0:T(8,128)(2,1)S(1)}, u32[]{:S(2)}, u32[]{:S(2)}) collective-permute-start(bf16[256,128]{1,0:T(8,128)(2,1)} %refs_0_.3), channel_id=1, source_target_pairs={{0,1},{1,2},{2,3},{3,0},{4,5},{5,6},{6,7},{7,4},{8,9},{9,10},{10,1... | collective-permute-start | bytes 196616 | tf_op jit(solution)/shard_map/ppermute | solution.py:398
  48.0 9.7 %collective-permute-start.4 = (bf16[128,512]{1,0:T(8,128)(2,1)S(1)}, bf16[128,512]{1,0:T(8,128)(2,1)S(1)}, u32[]{:S(2)}, u32[]{:S(2)}) collective-permute-start(bf16[128,512]{1,0:T(8,128)(2,1)S(1)} %get-tuple-element.55), channel_id=1, source_target_pairs={{0,2},{1,3},{2,0},{3,1},{4,6},{5,7},{6,4},{7,5},{8,10},{9,11},{10,... | collective-permute-start | bytes 393224 | tf_op jit(solution)/shard_map/ppermute | solution.py:398
  48.4 9.4 %collective-permute-start.5 = (bf16[128,512]{1,0:T(8,128)(2,1)S(1)}, bf16[128,512]{1,0:T(8,128)(2,1)S(1)}, u32[]{:S(2)}, u32[]{:S(2)}) collective-permute-start(bf16[128,512]{1,0:T(8,128)(2,1)S(1)} %get-tuple-element.56), channel_id=1, source_target_pairs={{0,3},{1,0},{2,1},{3,2},{4,7},{5,4},{6,5},{7,6},{8,11},{9,8},{10,9... | collective-permute-start | bytes 393224 | tf_op jit(solution)/shard_map/ppermute | solution.py:398
  50.9 6.9 %collective-permute-start.3 = (bf16[128,512]{1,0:T(8,128)(2,1)S(1)}, bf16[128,512]{1,0:T(8,128)(2,1)S(1)}, u32[]{:S(2)}, u32[]{:S(2)}) collective-permute-start(bf16[128,512]{1,0:T(8,128)(2,1)S(1)} %get-tuple-element.54.refs_4_), channel_id=1, source_target_pairs={{0,1},{1,2},{2,3},{3,0},{4,5},{5,6},{6,7},{7,4},{8,9},{9,10},{10,1... | collective-permute-start | bytes 393224 | tf_op jit(solution)/shard_map/ppermute | solution.py:398
  51.6 9.7 %collective-permute-start.6 = (bf16[128,512]{1,0:T(8,128)(2,1)S(1)}, bf16[128,512]{1,0:T(8,128)(2,1)S(1)}, u32[]{:S(2)}, u32[]{:S(2)}) collective-permute-start(bf16[128,512]{1,0:T(8,128)(2,1)S(1)} %get-tuple-element.61), channel_id=1, source_target_pairs={{0,1},{1,2},{2,3},{3,0},{4,5},{5,6},{6,7},{7,4},{8,9},{9,10},{10,1... | collective-permute-start | bytes 393224 | tf_op jit(solution)/shard_map/ppermute | solution.py:398
  51.8 11.5 %collective-permute-start.7 = (bf16[128,512]{1,0:T(8,128)(2,1)S(1)}, bf16[128,512]{1,0:T(8,128)(2,1)S(1)}, u32[]{:S(2)}, u32[]{:S(2)}) collective-permute-start(bf16[128,512]{1,0:T(8,128)(2,1)S(1)} %get-tuple-element.62), channel_id=1, source_target_pairs={{0,2},{1,3},{2,0},{3,1},{4,6},{5,7},{6,4},{7,5},{8,10},{9,11},{10,... | collective-permute-start | bytes 393224 | tf_op jit(solution)/shard_map/ppermute | solution.py:398
  57.7 5.5 %collective-permute-start.8 = (bf16[128,512]{1,0:T(8,128)(2,1)S(1)}, bf16[128,512]{1,0:T(8,128)(2,1)S(1)}, u32[]{:S(2)}, u32[]{:S(2)}) collective-permute-start(bf16[128,512]{1,0:T(8,128)(2,1)S(1)} %get-tuple-element.63), channel_id=1, source_target_pairs={{0,3},{1,0},{2,1},{3,2},{4,7},{5,4},{6,5},{7,6},{8,11},{9,8},{10,9... | collective-permute-start | bytes 393224 | tf_op jit(solution)/shard_map/ppermute | solution.py:398
  58.0 7.9 %collective-permute-start.13 = (bf16[128,512]{1,0:T(8,128)(2,1)S(1)}, bf16[128,512]{1,0:T(8,128)(2,1)S(1)}, u32[]{:S(2)}, u32[]{:S(2)}) collective-permute-start(bf16[128,512]{1,0:T(8,128)(2,1)S(1)} %slope.2.refs_0_), channel_id=1, source_target_pairs={{0,3},{1,0},{2,1},{3,2},{4,7},{5,4},{6,5},{7,6},{8,11},{9,8},{10,9... | collective-permute-start | bytes 393224 | tf_op jit(solution)/shard_map/ppermute | solution.py:398
  59.1 8.8 %collective-permute-start.11 = (bf16[128,512]{1,0:T(8,128)(2,1)S(1)}, bf16[128,512]{1,0:T(8,128)(2,1)S(1)}, u32[]{:S(2)}, u32[]{:S(2)}) collective-permute-start(bf16[128,512]{1,0:T(8,128)(2,1)S(1)} %slope.2.refs_0_), channel_id=1, source_target_pairs={{0,2},{1,3},{2,0},{3,1},{4,6},{5,7},{6,4},{7,5},{8,10},{9,11},{10,... | collective-permute-start | bytes 393224 | tf_op jit(solution)/shard_map/ppermute | solution.py:398
  61.3 6.6 %collective-permute-start.9 = (bf16[128,512]{1,0:T(8,128)(2,1)S(1)}, bf16[128,512]{1,0:T(8,128)(2,1)S(1)}, u32[]{:S(2)}, u32[]{:S(2)}) collective-permute-start(bf16[128,512]{1,0:T(8,128)(2,1)S(1)} %slope.2.refs_0_), channel_id=1, source_target_pairs={{0,1},{1,2},{2,3},{3,0},{4,5},{5,6},{6,7},{7,4},{8,9},{9,10},{10,1... | collective-permute-start | bytes 393224 | tf_op jit(solution)/shard_map/ppermute | solution.py:398
  63.4 6.3 %collective-permute-start.14 = (bf16[128,512]{1,0:T(8,128)(2,1)S(1)}, bf16[128,512]{1,0:T(8,128)(2,1)S(1)}, u32[]{:S(2)}, u32[]{:S(2)}) collective-permute-start(bf16[128,512]{1,0:T(8,128)(2,1)S(1)} %slope.3.refs_1_), channel_id=1, source_target_pairs={{0,3},{1,0},{2,1},{3,2},{4,7},{5,4},{6,5},{7,6},{8,11},{9,8},{10,9... | collective-permute-start | bytes 393224 | tf_op jit(solution)/shard_map/ppermute | solution.py:398
  64.2 6.1 %collective-permute-start.12 = (bf16[128,512]{1,0:T(8,128)(2,1)S(1)}, bf16[128,512]{1,0:T(8,128)(2,1)S(1)}, u32[]{:S(2)}, u32[]{:S(2)}) collective-permute-start(bf16[128,512]{1,0:T(8,128)(2,1)S(1)} %slope.3.refs_1_), channel_id=1, source_target_pairs={{0,2},{1,3},{2,0},{3,1},{4,6},{5,7},{6,4},{7,5},{8,10},{9,11},{10,... | collective-permute-start | bytes 393224 | tf_op jit(solution)/shard_map/ppermute | solution.py:398
  65.9 6.5 %collective-permute-start.10 = (bf16[128,512]{1,0:T(8,128)(2,1)S(1)}, bf16[128,512]{1,0:T(8,128)(2,1)S(1)}, u32[]{:S(2)}, u32[]{:S(2)}) collective-permute-start(bf16[128,512]{1,0:T(8,128)(2,1)S(1)} %slope.3.refs_1_), channel_id=1, source_target_pairs={{0,1},{1,2},{2,3},{3,0},{4,5},{5,6},{6,7},{7,4},{8,9},{9,10},{10,1... | collective-permute-start | bytes 393224 | tf_op jit(solution)/shard_map/ppermute | solution.py:398
  75.3 8.7 %collective-permute-start.15 = (bf16[4,256,512]{2,1,0:T(8,128)(2,1)}, bf16[4,256,512]{2,1,0:T(8,128)(2,1)S(1)}, u32[]{:S(2)}, u32[]{:S(2)}) collective-permute-start(bf16[4,256,512]{2,1,0:T(8,128)(2,1)} %get-tuple-element.66.refs_0_), channel_id=1, source_target_pairs={{0,4},{4,0},{8,12},{12,8},{16,20},{20,16},{24,28},{28,24},{32,36},... | collective-permute-start | bytes 3145736 | tf_op jit(solution)/shard_map/ppermute | solution.py:406
  78.3 5.7 %collective-permute-start.16 = (bf16[256,1024]{1,0:T(8,128)(2,1)S(1)}, bf16[256,1024]{1,0:T(8,128)(2,1)S(1)}, u32[]{:S(2)}, u32[]{:S(2)}) collective-permute-start(bf16[256,1024]{1,0:T(8,128)(2,1)S(1)} %copy-done.6), channel_id=1, source_target_pairs={{0,4},{4,0},{8,12},{12,8},{16,20},{20,16},{24,28},{28,24},{32,36},... | collective-permute-start | bytes 1572872 | tf_op jit(solution)/shard_map/ppermute | solution.py:406
  78.4 17.0 %all-to-all-start.2 = ((bf16[32,16,512]{2,1,0:T(8,128)(2,1)}), bf16[32,16,512]{2,1,0:T(8,128)(2,1)S(1)}, u32[]{:S(2)}, u32[]{:S(2)}) async-start(bf16[32,16,512]{2,1,0:T(8,128)(2,1)} %get-tuple-element.72), calls=%async_computation.2 | async-start | bytes 1048576 | tf_op jit(solution)/shard_map/all_to_all | solution.py:483
  83.7 14.0 %collective-permute-start.27 = (bf16[256,512]{1,0:T(8,128)(2,1)}, bf16[256,512]{1,0:T(8,128)(2,1)S(1)}, u32[]{:S(2)}, u32[]{:S(2)}) collective-permute-start(bf16[256,512]{1,0:T(8,128)(2,1)} %get-tuple-element.84), channel_id=1, source_target_pairs={{0,4},{4,0},{8,12},{12,8},{16,20},{20,16},{24,28},{28,24},{32,36},... | collective-permute-start | bytes 786440 | tf_op jit(solution)/shard_map/ppermute | solution.py:406
  88.9 11.3 %collective-permute-start.17 = (bf16[4,64,1024]{2,1,0:T(8,128)(2,1)}, bf16[4,64,1024]{2,1,0:T(8,128)(2,1)S(1)}, u32[]{:S(2)}, u32[]{:S(2)}) collective-permute-start(bf16[4,64,1024]{2,1,0:T(8,128)(2,1)} %get-tuple-element.69), channel_id=1, source_target_pairs={{0,8},{4,36},{8,16},{12,44},{16,24},{20,52},{24,0},{28,60},{32,40}... | collective-permute-start | bytes 1572872 | tf_op jit(solution)/shard_map/ppermute | solution.py:414
  90.5 15.1 %collective-permute-start.18 = (bf16[4,64,1024]{2,1,0:T(8,128)(2,1)}, bf16[4,64,1024]{2,1,0:T(8,128)(2,1)S(1)}, u32[]{:S(2)}, u32[]{:S(2)}) collective-permute-start(bf16[4,64,1024]{2,1,0:T(8,128)(2,1)} %get-tuple-element.70), channel_id=1, source_target_pairs={{0,16},{4,68},{8,24},{12,76},{16,0},{20,84},{24,8},{28,92},{32,48}... | collective-permute-start | bytes 1572872 | tf_op jit(solution)/shard_map/ppermute | solution.py:414
  93.0 12.7 %collective-permute-start.19 = (bf16[4,64,1024]{2,1,0:T(8,128)(2,1)}, bf16[4,64,1024]{2,1,0:T(8,128)(2,1)S(1)}, u32[]{:S(2)}, u32[]{:S(2)}) collective-permute-start(bf16[4,64,1024]{2,1,0:T(8,128)(2,1)} %get-tuple-element.71), channel_id=1, source_target_pairs={{0,24},{4,100},{8,0},{12,108},{16,8},{20,116},{24,16},{28,124},{32... | collective-permute-start | bytes 1572872 | tf_op jit(solution)/shard_map/ppermute | solution.py:414
  97.7 1.6 %collective-permute-start.26 = (bf16[256,512]{1,0:T(8,128)(2,1)S(1)}, bf16[256,512]{1,0:T(8,128)(2,1)S(1)}, u32[]{:S(2)}, u32[]{:S(2)}) collective-permute-start(bf16[256,512]{1,0:T(8,128)(2,1)S(1)} %get-tuple-element.83.refs_0_), channel_id=1, source_target_pairs={{0,4},{4,0},{8,12},{12,8},{16,20},{20,16},{24,28},{28,24},{32,36},... | collective-permute-start | bytes 786440 | tf_op jit(solution)/shard_map/ppermute | solution.py:406
  97.8 8.2 %collective-permute-start.24 = (bf16[256,256]{1,0:T(8,128)(2,1)S(1)}, bf16[256,256]{1,0:T(8,128)(2,1)S(1)}, u32[]{:S(2)}, u32[]{:S(2)}) collective-permute-start(bf16[256,256]{1,0:T(8,128)(2,1)S(1)} %get-tuple-element.81), channel_id=1, source_target_pairs={{0,2},{1,3},{2,0},{3,1},{4,6},{5,7},{6,4},{7,5},{8,10},{9,11},{10,... | collective-permute-start | bytes 393224 | tf_op jit(solution)/shard_map/ppermute | solution.py:398
  99.3 6.7 %collective-permute-start.25 = (bf16[256,256]{1,0:T(8,128)(2,1)S(1)}, bf16[256,256]{1,0:T(8,128)(2,1)S(1)}, u32[]{:S(2)}, u32[]{:S(2)}) collective-permute-start(bf16[256,256]{1,0:T(8,128)(2,1)S(1)} %get-tuple-element.82), channel_id=1, source_target_pairs={{0,3},{1,0},{2,1},{3,2},{4,7},{5,4},{6,5},{7,6},{8,11},{9,8},{10,9... | collective-permute-start | bytes 393224 | tf_op jit(solution)/shard_map/ppermute | solution.py:398
  100.2 6.9 %collective-permute-start.23 = (bf16[256,256]{1,0:T(8,128)(2,1)S(1)}, bf16[256,256]{1,0:T(8,128)(2,1)S(1)}, u32[]{:S(2)}, u32[]{:S(2)}) collective-permute-start(bf16[256,256]{1,0:T(8,128)(2,1)S(1)} %get-tuple-element.75.refs_4_), channel_id=1, source_target_pairs={{0,1},{1,2},{2,3},{3,0},{4,5},{5,6},{6,7},{7,4},{8,9},{9,10},{10,1... | collective-permute-start | bytes 393224 | tf_op jit(solution)/shard_map/ppermute | solution.py:398
  108.1 16.1 %all-to-all-start.3 = ((bf16[16,160,128]{2,1,0:T(8,128)(2,1)}), bf16[16,160,128]{2,1,0:T(8,128)(2,1)S(1)}, u32[]{:S(2)}, u32[]{:S(2)}) async-start(bf16[16,160,128]{2,1,0:T(8,128)(2,1)} %get-tuple-element.85), calls=%async_computation.3 | async-start | bytes 1310720 | tf_op jit(solution)/shard_map/all_to_all | solution.py:519
  113.1 14.0 %collective-permute-start.20 = (bf16[64,1024]{1,0:T(8,128)(2,1)S(1)}, bf16[64,1024]{1,0:T(8,128)(2,1)S(1)}, u32[]{:S(2)}, u32[]{:S(2)}) collective-permute-start(bf16[64,1024]{1,0:T(8,128)(2,1)S(1)} %get-tuple-element.77), channel_id=1, source_target_pairs={{0,32},{4,12},{8,40},{12,20},{16,48},{20,28},{24,56},{28,4},{32,64... | collective-permute-start | bytes 393224 | tf_op jit(solution)/shard_map/ppermute | solution.py:414
  114.5 12.8 %collective-permute-start.21 = (bf16[64,1024]{1,0:T(8,128)(2,1)S(1)}, bf16[64,1024]{1,0:T(8,128)(2,1)S(1)}, u32[]{:S(2)}, u32[]{:S(2)}) collective-permute-start(bf16[64,1024]{1,0:T(8,128)(2,1)S(1)} %get-tuple-element.78), channel_id=1, source_target_pairs={{0,64},{4,20},{8,72},{12,28},{16,80},{20,4},{24,88},{28,12},{32,96... | collective-permute-start | bytes 393224 | tf_op jit(solution)/shard_map/ppermute | solution.py:414
  116.9 10.4 %collective-permute-start.22 = (bf16[64,1024]{1,0:T(8,128)(2,1)S(1)}, bf16[64,1024]{1,0:T(8,128)(2,1)S(1)}, u32[]{:S(2)}, u32[]{:S(2)}) collective-permute-start(bf16[64,1024]{1,0:T(8,128)(2,1)S(1)} %get-tuple-element.79), channel_id=1, source_target_pairs={{0,96},{4,28},{8,104},{12,4},{16,112},{20,12},{24,120},{28,20},{32... | collective-permute-start | bytes 393224 | tf_op jit(solution)/shard_map/ppermute | solution.py:414
  124.3 3.9 %collective-permute-start.28 = (bf16[16,16,128]{2,1,0:T(8,128)(2,1)S(1)}, bf16[16,16,128]{2,1,0:T(8,128)(2,1)S(1)}, u32[]{:S(2)}, u32[]{:S(2)}) collective-permute-start(bf16[16,16,128]{2,1,0:T(8,128)(2,1)S(1)} %get-tuple-element.86.refs_5_), channel_id=1, source_target_pairs={{0,4},{4,0},{8,12},{12,8},{16,20},{20,16},{24,28},{28,24},{32,36},... | collective-permute-start | bytes 196616 | tf_op jit(solution)/shard_map/ppermute | solution.py:406
  (7 other events, 152.2 us)
